TPU v7x, 256 devices: a whole 4x4x8 slice. The times are simulated.
256 devices in a mesh: band: 4 (over x), dom: 64 (over z, y, core).
Axes of the slice: x: 4, y: 4, z: 8, core: 2. Of those that a mesh axis runs over, the one named last changes fastest.
Arguments:
- orbitals: bfloat16 [343, 1536, 512], P(None, 'dom', 'band'), may hold values from -6 to 6
- occupancy: float32 [512], P('band'), may hold values from 0 to 0.00390625
- shape_values: bfloat16 [512, 343], replicated, may hold values from -0.3125 to 0.3125
- shape_grads: bfloat16 [3, 512, 343], replicated, may hold values from -6 to 6
- cell_slot: int32 [1536], P('dom'), may hold values from 0 to 3071, as said below
- slot_cell: int32 [3072], P('dom'), may hold values from -1 to 1535, as said below
- potential_nodes: float32 [729, 3072], P(None, 'dom'), may hold values from -6 to 6
- stiffness: float32 [729, 729], replicated, may hold values from -0.21875 to 0.21875
- stiff_scale: float32 [3072], P('dom'), may hold values from 0.5 to 2
- electro_shape: float32 [512, 729], replicated, may hold values from -0.21875 to 0.21875
- core_density: float32 [3072, 512], P('dom'), may hold values from 0.1 to 1
- quad_weight: float32 [3072, 512], P('dom'), may hold values from 0.25 to 4
Outputs:
- hamiltonian_action: bfloat16 [343, 1536, 512], P(None, 'dom', 'band')
- poisson_residual: float32 [729, 3072], P(None, 'dom')
Inputs may be any that keep to these rules, and one draw needn't show every extreme that they name: cell_slot is the owner domain times 48 plus the position in it, distinct over cells. The cells of one wavefunction domain go to exactly 12 electrostatics domains, 2 cells to each; an electrostatics domain holds 48 cells or none. slot_cell is the inverse of cell_slot: slot_cell[cell_slot[c]] = c, and -1 in every other slot.
All inputs are finite; a program needn't handle non-finite values.
Results may differ from a plain program's by a relative error of at most 0.0045.
Values sent between devices are 32-bit elements; how exact they have to be, the bound alone decides.
No kernel may reach another device: no remote copies, remote signals or barrier semaphores. Data moves between devices by JAX's collectives and lax.ppermute only.
A program may use at most 64 MiB of HBM per device.

v0:
```python
import jax
import jax.numpy as jnp
from jax import lax
from jax.sharding import PartitionSpec as P

slater_coef = 0.7385587663820224
bound_kappa = 0.804
slope_coef = 0.2195149727645171
reduced_coef = 0.026121172985233605


def exchange_energy(density, square):
    power_four = density * jnp.cbrt(density)
    reduced = reduced_coef * square / (power_four * power_four)
    enhance = 1.0 + bound_kappa - bound_kappa / (1.0 + slope_coef * reduced / bound_kappa)
    return -slater_coef * power_four * enhance


def exchange_parts(density, square):
    return jax.grad(
        lambda dens_in, square_in: jnp.sum(exchange_energy(dens_in, square_in)), argnums=(0, 1)
    )(density, square)


def weighted_potential(density, gradient, weight, hartree):
    square = jnp.sum(gradient * gradient, axis=0)
    d_density, d_square = exchange_parts(density, square)
    first_term = weight * (d_density + hartree)
    other_terms = 2.0 * weight * d_square * gradient
    return jnp.concatenate([first_term[None], other_terms], axis=0)


def poisson_apply(density, weight, node_field, cell_scale, stiffness, interp):
    stiff_part = jnp.dot(stiffness, node_field, precision=lax.Precision.HIGHEST)
    load_term = jnp.dot(interp.T, weight * density, precision=lax.Precision.HIGHEST)
    return cell_scale * stiff_part - load_term


def quad_terms(shape_table, orbit_block):
    node_count, cell_count, band_count = orbit_block.shape
    flattened = jnp.dot(
        shape_table,
        orbit_block.reshape(node_count, cell_count * band_count),
        preferred_element_type=jnp.float32,
    )
    return flattened.reshape(4, -1, cell_count, band_count)


def density_terms(quad_vals, occupancy):
    weighted_lead = quad_vals[0] * occupancy
    first_term = jnp.sum(weighted_lead * quad_vals[0], axis=-1)
    other_terms = 2.0 * jnp.sum(weighted_lead[None] * quad_vals[1:], axis=-1)
    return jnp.concatenate([first_term[None], other_terms], axis=0)


def apply_potential(shape_table, quad_vals, weighted):
    expanded = weighted[..., None]
    value_term = expanded[0] * quad_vals[0] + (
        expanded[1] * quad_vals[1] + expanded[2] * quad_vals[2] + expanded[3] * quad_vals[3]
    )
    grad_terms = expanded[1:] * quad_vals[0][None]
    products = jnp.concatenate([value_term[None], grad_terms], axis=0).astype(jnp.bfloat16)
    node_count = shape_table.shape[1]
    cell_count, band_count = (quad_vals.shape[2], quad_vals.shape[3])
    result = jnp.dot(
        shape_table.T,
        products.reshape(-1, cell_count * band_count),
        preferred_element_type=jnp.float32,
    )
    return result.astype(jnp.bfloat16).reshape(node_count, cell_count, band_count)


def wave_rows(cell_slot, slot_count, capacity):
    owner_index = cell_slot // slot_count
    cell_count = cell_slot.shape[0]
    matching = owner_index[:, None] == owner_index[None, :]
    earlier = jnp.arange(cell_count)[None, :] < jnp.arange(cell_count)[:, None]
    position = jnp.sum((matching & earlier).astype(jnp.int32), axis=1)
    return owner_index * capacity + position


def owner_rows(slot_cell, cell_count, capacity, domains):
    filled = slot_cell >= 0
    source = jnp.where(filled, slot_cell // cell_count, 0)
    matching = (
        (source[:, None] == source[None, :])
        & filled[None, :]
        & (slot_cell[None, :] < slot_cell[:, None])
    )
    position = jnp.sum(matching.astype(jnp.int32), axis=1)
    row_index = jnp.where(filled, source * capacity + position, domains * capacity)
    return row_index


def body(
    orbitals,
    occupancy,
    shape_values,
    shape_grads,
    cell_slot,
    slot_cell,
    potential_nodes,
    stiffness,
    stiff_scale,
    electro_shape,
    core_density,
    quad_weight,
):
    node_count, cell_count, band_count = orbitals.shape
    points = shape_values.shape[0]
    core_field = core_density.T
    weight_field = quad_weight.T
    shape_table = jnp.concatenate([shape_values[None], shape_grads], axis=0).reshape(
        4 * points, node_count
    )
    block_total = cell_count // 4

    def first_pass(block_index):
        orbit_block = lax.dynamic_slice_in_dim(orbitals, block_index * 4, 4, 1)
        return density_terms(quad_terms(shape_table, orbit_block), occupancy)

    local_terms = lax.map(first_pass, jnp.arange(block_total, dtype=jnp.int32))
    local_terms = local_terms.transpose(1, 2, 0, 3).reshape(4, points, cell_count)
    partial_value = lax.psum(local_terms, "band")
    domains = lax.axis_size("dom")
    slot_count = slot_cell.shape[0]
    groups = min(domains // 2, cell_count // 2)
    capacity = cell_count // groups
    send_rows = wave_rows(cell_slot, slot_count, capacity)
    recv_rows = owner_rows(slot_cell, cell_count, capacity, domains)
    hartree = jnp.dot(electro_shape, potential_nodes, precision=lax.Precision.HIGHEST)
    outgoing = (
        jnp.zeros((domains * capacity, 4, points), jnp.float32)
        .at[send_rows]
        .set(partial_value.transpose(2, 0, 1))
    )
    incoming = lax.all_to_all(
        outgoing.reshape(domains, capacity, 4, points),
        "dom",
        split_axis=0,
        concat_axis=0,
        tiled=True,
    )
    arrived = jnp.take(
        incoming.reshape(-1, 4, points), recv_rows, axis=0, mode="fill", fill_value=0.0
    ).transpose(1, 2, 0)
    density = core_field + arrived[0]
    weighted = weighted_potential(density, arrived[1:], weight_field, hartree)
    residual = poisson_apply(
        density, weight_field, potential_nodes, stiff_scale, stiffness, electro_shape
    )
    backward = (
        jnp.zeros((domains * capacity, 4, points), jnp.float32)
        .at[recv_rows]
        .set(weighted.transpose(2, 0, 1), mode="drop")
    )
    coming = lax.all_to_all(
        backward.reshape(domains, capacity, 4, points),
        "dom",
        split_axis=0,
        concat_axis=0,
        tiled=True,
    )
    returned = coming.reshape(-1, 4, points)[send_rows].transpose(1, 2, 0)

    def second_pass(block_index):
        orbit_block = lax.dynamic_slice_in_dim(orbitals, block_index * 4, 4, 1)
        quad_vals = quad_terms(shape_table, orbit_block)
        block_pot = lax.dynamic_slice_in_dim(returned, block_index * 4, 4, 2)
        return apply_potential(shape_table, quad_vals, block_pot)

    action = lax.map(second_pass, jnp.arange(block_total, dtype=jnp.int32))
    action = action.transpose(1, 0, 2, 3).reshape(node_count, cell_count, band_count)
    return (action, residual)


def solution(mesh):
    return jax.shard_map(
        body,
        mesh=mesh,
        in_specs=(
            P(None, "dom", "band"),
            P("band"),
            P(),
            P(),
            P("dom"),
            P("dom"),
            P(None, "dom"),
            P(),
            P("dom"),
            P(),
            P("dom", None),
            P("dom", None),
        ),
        out_specs=(P(None, "dom", "band"), P(None, "dom")),
        check_vma=False,
    )
```

profile of v0, /device:TPU:8, one launch (start us, length us, event | category | flops | bytes accessed | tf_op | source)
XLA Modules:
  0.0 429.7 jit_solution(4128693617992666624)
XLA Ops:
  12.5 161.9 %while.20 = (s32[]{:T(128)}, f32[6,4,512,4]{2,3,1,0:T(4,128)S(1)}, s32[6]{0:T(128)S(1)}, bf16[343,24,128]{2,1,0:T(8,128)(2,1)}, bf16[2048,343]{1,0:T(8,128)(2,1)...) while((s32[]{:T(128)}, f32[6,4,512,4]{2,3,1,0:T(4,128)S(1)}, ...), condition=%wide.region_5.6_spmd, body=%wide.region_2.5_spmd.sunk | while | flops 721688576 | bytes 57918184 | solution.py:122
  21.3 3.8 slice.94
  28.6 4.9 %slice.95 = f32[3,512,4,128]{3,2,1,0:T(4,128)} reshape(f32[1536,512]{1,0:T(8,128)} %copy.115) | data formatting | bytes 6291456 | tf_op jit(solution)/shard_map/while/body/eval_jaxpr/slice | solution.py:52
  33.5 4.5 %multiply_reduce_fusion.6 = f32[3,512,4]{2,1,0:T(8,128)} fusion(f32[3,512,4,128]{3,2,1,0:T(4,128)} %slice.95, f32[512,4,128]{2,1,0:T(4,128)S(1)} %copy.116), kind=kLoop, calls=%fused_computation.5.clone.1 | loop fusion | flops 1566720 | bytes 4218880 | tf_op jit(solution)/shard_map/while/body/eval_jaxpr/reduce_sum | solution.py:52
  55.6 4.9 %slice.95 = f32[3,512,4,128]{3,2,1,0:T(4,128)} reshape(f32[1536,512]{1,0:T(8,128)} %copy.115) | data formatting | bytes 6291456 | tf_op jit(solution)/shard_map/while/body/eval_jaxpr/slice | solution.py:52
  60.5 4.5 %multiply_reduce_fusion.6 = f32[3,512,4]{2,1,0:T(8,128)} fusion(f32[3,512,4,128]{3,2,1,0:T(4,128)} %slice.95, f32[512,4,128]{2,1,0:T(4,128)S(1)} %copy.116), kind=kLoop, calls=%fused_computation.5.clone.1 | loop fusion | flops 1566720 | bytes 4218880 | tf_op jit(solution)/shard_map/while/body/eval_jaxpr/reduce_sum | solution.py:52
  82.6 4.9 %slice.95 = f32[3,512,4,128]{3,2,1,0:T(4,128)} reshape(f32[1536,512]{1,0:T(8,128)} %copy.115) | data formatting | bytes 6291456 | tf_op jit(solution)/shard_map/while/body/eval_jaxpr/slice | solution.py:52
  87.5 4.5 %multiply_reduce_fusion.6 = f32[3,512,4]{2,1,0:T(8,128)} fusion(f32[3,512,4,128]{3,2,1,0:T(4,128)} %slice.95, f32[512,4,128]{2,1,0:T(4,128)S(1)} %copy.116), kind=kLoop, calls=%fused_computation.5.clone.1 | loop fusion | flops 1566720 | bytes 4218880 | tf_op jit(solution)/shard_map/while/body/eval_jaxpr/reduce_sum | solution.py:52
  102.3 3.8 slice.94
  109.6 4.9 %slice.95 = f32[3,512,4,128]{3,2,1,0:T(4,128)} reshape(f32[1536,512]{1,0:T(8,128)} %copy.115) | data formatting | bytes 6291456 | tf_op jit(solution)/shard_map/while/body/eval_jaxpr/slice | solution.py:52
  114.5 4.5 %multiply_reduce_fusion.6 = f32[3,512,4]{2,1,0:T(8,128)} fusion(f32[3,512,4,128]{3,2,1,0:T(4,128)} %slice.95, f32[512,4,128]{2,1,0:T(4,128)S(1)} %copy.116), kind=kLoop, calls=%fused_computation.5.clone.1 | loop fusion | flops 1566720 | bytes 4218880 | tf_op jit(solution)/shard_map/while/body/eval_jaxpr/reduce_sum | solution.py:52
  129.3 3.8 slice.94
  136.6 4.9 %slice.95 = f32[3,512,4,128]{3,2,1,0:T(4,128)} reshape(f32[1536,512]{1,0:T(8,128)} %copy.115) | data formatting | bytes 6291456 | tf_op jit(solution)/shard_map/while/body/eval_jaxpr/slice | solution.py:52
  141.5 4.5 %multiply_reduce_fusion.6 = f32[3,512,4]{2,1,0:T(8,128)} fusion(f32[3,512,4,128]{3,2,1,0:T(4,128)} %slice.95, f32[512,4,128]{2,1,0:T(4,128)S(1)} %copy.116), kind=kLoop, calls=%fused_computation.5.clone.1 | loop fusion | flops 1566720 | bytes 4218880 | tf_op jit(solution)/shard_map/while/body/eval_jaxpr/reduce_sum | solution.py:52
  163.6 4.9 %slice.95 = f32[3,512,4,128]{3,2,1,0:T(4,128)} reshape(f32[1536,512]{1,0:T(8,128)} %copy.115) | data formatting | bytes 6291456 | tf_op jit(solution)/shard_map/while/body/eval_jaxpr/slice | solution.py:52
  168.5 4.5 %multiply_reduce_fusion.6 = f32[3,512,4]{2,1,0:T(8,128)} fusion(f32[3,512,4,128]{3,2,1,0:T(4,128)} %slice.95, f32[512,4,128]{2,1,0:T(4,128)S(1)} %copy.116), kind=kLoop, calls=%fused_computation.5.clone.1 | loop fusion | flops 1566720 | bytes 4218880 | tf_op jit(solution)/shard_map/while/body/eval_jaxpr/reduce_sum | solution.py:52
  175.4 49.3 %all-reduce.2.cloned.1.call-done = f32[24,4,512]{2,1,0:T(4,128)} async-done(((f32[24,4,512]{2,1,0:T(4,128)}), f32[24,4,512]{2,1,0:T(4,128)}) %all-reduce.2.cloned.1.call-update) | async-done | bytes 196624 | tf_op jit(solution)/shard_map/psum | solution.py:124
  225.9 4.1 scatter_fusion
  230.0 10.7 %all-to-all-start = ((f32[64,2,4,512]{3,2,1,0:T(4,128)}), f32[64,2,4,512]{3,2,1,0:T(4,128)S(1)}, u32[]{:S(2)}, u32[]{:S(2)}) async-start(f32[64,2,4,512]{3,2,1,0:T(4,128)} %bitcast.23), calls=%async_computation | async-start | bytes 2097152 | tf_op jit(solution)/shard_map/all_to_all | solution.py:137
  241.0 28.5 %all-to-all-done = f32[64,2,4,512]{3,2,1,0:T(4,128)S(1)} async-done(((f32[64,2,4,512]{3,2,1,0:T(4,128)}), f32[64,2,4,512]{3,2,1,0:T(4,128)S(1)}, u32[]{:S(2)}, u32[]{:S(2)}) %all-to-all-start) | async-done | bytes 1048608 | tf_op jit(solution)/shard_map/all_to_all | solution.py:137
  275.2 4.9 %scatter_fusion.1 = f32[128,4,512]{2,1,0:T(4,128)} fusion(f32[128,4,512]{2,1,0:T(4,128)} %broadcast.90, s32[48]{0:T(128)S(1)} %get-tuple-element.123, f32[48,4,512]{2,1,0:T(4,128)S(1)} %copy.75), kind=kCustom, calls=%fused_computation.3 | custom fusion | bytes 1179840 | tf_op jit(solution)/shard_map/scatter | solution.py:155
  280.2 6.5 %all-to-all-start.1 = ((f32[64,2,4,512]{3,2,1,0:T(4,128)}), f32[64,2,4,512]{3,2,1,0:T(4,128)}, u32[]{:S(2)}, u32[]{:S(2)}) async-start(f32[64,2,4,512]{3,2,1,0:T(4,128)} %bitcast.30), calls=%async_computation.1 | async-start | bytes 2097152 | tf_op jit(solution)/shard_map/all_to_all | solution.py:157
  292.3 23.1 %all-to-all-done.1 = f32[64,2,4,512]{3,2,1,0:T(4,128)} async-done(((f32[64,2,4,512]{3,2,1,0:T(4,128)}), f32[64,2,4,512]{3,2,1,0:T(4,128)}, u32[]{:S(2)}, u32[]{:S(2)}) %all-to-all-start.1) | async-done | bytes 1048608 | tf_op jit(solution)/shard_map/all_to_all | solution.py:157
  317.3 101.9 %while.21 = (s32[]{:T(128)}, bf16[6,343,4,128]{3,2,1,0:T(4,128)(2,1)}, s32[6]{0:T(128)S(1)}, f32[4,512,24]{1,0,2:T(4,128)S(1)}, bf16[343,24,128]{2,1,0:T(8,128)(...) while((s32[]{:T(128)}, ...), condition=%wide.region_11.12_spmd, body=%wide.region_10.11_spmd.sunk | while | flops 1443540480 | bytes 50011988 | solution.py:172
  (293 shorter events, 211.8 us)
Async XLA Ops:
  7.2 282.3 %copy-start = (f32[729,729]{1,0:T(8,128)S(1)}, f32[729,729]{1,0:T(8,128)}, u32[]{:S(2)}) copy-start(f32[729,729]{1,0:T(8,128)} %param.23) | copy-start | bytes 6377296
  7.2 217.6 %all-reduce.2.cloned.1.call-start = ((), (), s32[]{:S(2)}) async-start(), calls=%async_computation.2 | async-start | bytes 393216 | tf_op jit(solution)/shard_map/psum | solution.py:124
  9.9 2.6 copy-start.10
  12.5 162.7 %copy-start.13 = (s32[24]{0:T(128)S(1)}, s32[24]{0:T(128)}, u32[]{:S(2)}) copy-start(s32[24]{0:T(128)} %param.20) | copy-start | bytes 292
  16.6 1.9 copy-start.1
  43.6 1.9 copy-start.1
  70.6 1.9 copy-start.1
  97.6 1.9 copy-start.1
  124.6 1.9 copy-start.1
  151.6 1.9 copy-start.1
  225.9 14.8 %copy-start.11 = (s32[48]{0:T(128)S(1)}, s32[48]{0:T(128)}, u32[]{:S(2)}) copy-start(s32[48]{0:T(128)} %param.21) | copy-start | bytes 580
  230.0 42.3 %copy-start.7 = (f32[48,512]{1,0:T(8,128)S(1)}, f32[48,512]{1,0:T(8,128)}, u32[]{:S(2)}) copy-start(f32[48,512]{1,0:T(8,128)} %param.27) | copy-start | bytes 294916
  230.0 42.3 %copy-start.8 = (f32[48,512]{1,0:T(8,128)S(1)}, f32[48,512]{1,0:T(8,128)}, u32[]{:S(2)}) copy-start(f32[48,512]{1,0:T(8,128)} %param.26) | copy-start | bytes 294916
  230.0 39.5 %all-to-all-start = ((f32[64,2,4,512]{3,2,1,0:T(4,128)}), f32[64,2,4,512]{3,2,1,0:T(4,128)S(1)}, u32[]{:S(2)}, u32[]{:S(2)}) async-start(f32[64,2,4,512]{3,2,1,0:T(4,128)} %bitcast.23), calls=%async_computation | async-start | bytes 2097152 | tf_op jit(solution)/shard_map/all_to_all | solution.py:137
  280.2 9.4 %copy-start.12 = (f32[48]{0:T(128)S(1)}, f32[48]{0:T(128)}, u32[]{:S(2)}) copy-start(f32[48]{0:T(128)} %param.24) | copy-start | bytes 580
  280.2 35.2 %all-to-all-start.1 = ((f32[64,2,4,512]{3,2,1,0:T(4,128)}), f32[64,2,4,512]{3,2,1,0:T(4,128)}, u32[]{:S(2)}, u32[]{:S(2)}) async-start(f32[64,2,4,512]{3,2,1,0:T(4,128)} %bitcast.30), calls=%async_computation.1 | async-start | bytes 2097152 | tf_op jit(solution)/shard_map/all_to_all | solution.py:157
  318.6 1.7 copy-start.3
  327.3 3.5 copy-start.5
  335.6 1.7 copy-start.3
  344.3 3.5 copy-start.5
  361.3 3.5 copy-start.5
  378.3 3.5 copy-start.5
  395.3 3.5 copy-start.5
  412.3 3.5 copy-start.5
  (18 other events, 28.2 us)
Sparse Core Ops, SparseCore 0:
  175.3 49.4 all-reduce.1
where the time goes:
time: 433 us; the launch traced here: 430 us
  local copies, waits for them, and re-layouts  184 us (42%)
  waiting for transfers between devices  101 us (23%)
  other arithmetic  75.9 us (18%)
  matrix products  28.2 us (7%)
  starting transfers between devices  17.2 us (4%)
  between operations  14.3 us (3%)
  loops' own time  8.65 us (2%)
    slice x18, local copies, waits for them, and re-layouts, density_terms(): other_terms = 2.0 * jnp.sum(weighted_lead[None] * quad_vals[1:], axis=-1)  73.1 us
    psum x1, waiting for transfers between devices, body(): partial_value = lax.psum(local_terms, 'band')  49.3 us
    another operation x12, other arithmetic  28.9 us
    all_to_all x1, waiting for transfers between devices, body(): lax.all_to_all(outgoing.reshape(domains, capacity, 4, points), 'dom', spl...  28.5 us
    reduce_sum x6, other arithmetic, density_terms(): other_terms = 2.0 * jnp.sum(weighted_lead[None] * quad_vals[1:], axis=-1)  27.1 us
    all_to_all x1, waiting for transfers between devices, body(): lax.all_to_all(backward.reshape(domains, capacity, 4, points), 'dom', spl...  23.1 us
    dot_general x12, matrix products, quad_terms(): jnp.dot(shape_table, orbit_block.reshape(node_count, cell_count * band_co...  15.8 us
    another operation x8, local copies, waits for them, and re-layouts  14.9 us
  transfers between devices with their start and end apart: 3, of which 3 were waited for; matrix products, arithmetic and copies ran while one was open for 1% of the time, Pallas kernels for 0%

commit v1 on v0

v1 whole, which is shorter than its diff:
```python
import functools

import jax
import jax.numpy as jnp
from jax import lax
from jax.experimental import pallas as pl
from jax.experimental.pallas import tpu as pltpu
from jax.sharding import PartitionSpec as P

F32, BF16, I32 = jnp.float32, jnp.bfloat16, jnp.int32
NODES, CELLS, BANDS, POINTS = 343, 24, 128, 512
KPAD = 384
SLOTS, ENODES, DOMAINS, CAP = 48, 729, 64, 2
ROWS = DOMAINS * CAP
RANKS, PART = 4, 128
GROUP = 4
STEP = 49
HIGHEST = lax.Precision.HIGHEST
NT = (((1,), (1,)), ((), ()))
MIB = 1 << 20

slater_coef = 0.7385587663820224
bound_kappa = 0.804
slope_coef = 0.2195149727645171
reduced_coef = 0.026121172985233605

VM = pl.BlockSpec(memory_space=pltpu.VMEM)
SM = pl.BlockSpec(memory_space=pltpu.SMEM)
HB = pl.BlockSpec(memory_space=pl.ANY)


def params(mib):
    return pltpu.CompilerParams(vmem_limit_bytes=mib * MIB)


def cost(flops, nbytes):
    return pl.CostEstimate(flops=int(flops), bytes_accessed=int(nbytes), transcendentals=0)


def lanes(index):
    return slice(index * 128, index * 128 + 128)


def fields_kernel(
    band_ref, slot_cell_ref, cell_slot_ref, nodes_ref, shape_ref, core_ref, weight_ref,
    send_ref, wave_row_ref, slot_row_ref, field_ref, count_ref,
):
    del band_ref

    def clear(d, carry):
        count_ref[d] = 0
        return carry

    lax.fori_loop(0, DOMAINS, clear, 0)
    field_ref[:, lanes(0)] = core_ref[...]
    field_ref[:, lanes(1)] = weight_ref[...]
    field_ref[:, lanes(2)] = jnp.dot(
        nodes_ref[...], shape_ref[...], precision=HIGHEST, preferred_element_type=F32
    )
    for s in range(SLOTS):
        cell = slot_cell_ref[s]
        slot_row_ref[s] = -1

        @pl.when(cell >= 0)
        def _():
            source = lax.shift_right_logical(cell * 10923, 18)
            place = count_ref[source]
            count_ref[source] = place + 1
            row = source * CAP + jnp.minimum(place, CAP - 1)
            slot_row_ref[s] = row
            send_ref[row] = field_ref[s : s + 1, :]

    def forget(d, carry):
        count_ref[d] = -1
        return carry

    lax.fori_loop(0, DOMAINS, forget, 0)

    def place_cell(c, carry):
        slot = cell_slot_ref[c]
        owner = lax.shift_right_logical(slot * 21846, 20)
        other = count_ref[owner]
        known = other >= 0
        first = jnp.maximum(other, 0)
        later = cell_slot_ref[first] > slot
        wave_row_ref[c] = owner * CAP + jnp.where(known & jnp.logical_not(later), 1, 0)

        @pl.when(known & later)
        def _():
            wave_row_ref[first] = owner * CAP + 1

        count_ref[owner] = c
        return carry

    lax.fori_loop(0, CELLS, place_cell, 0)


def pack_fields(band, slot_cell, cell_slot, nodes, shape, core, weight):
    quarter = lambda i, b: (0, b[0])
    return pl.pallas_call(
        fields_kernel,
        out_shape=(
            jax.ShapeDtypeStruct((ROWS, 1, 3 * PART), F32),
            jax.ShapeDtypeStruct((CELLS,), I32),
            jax.ShapeDtypeStruct((SLOTS,), I32),
        ),
        grid_spec=pltpu.PrefetchScalarGridSpec(
            num_scalar_prefetch=1,
            grid=(1,),
            in_specs=[
                SM,
                SM,
                pl.BlockSpec((SLOTS, ENODES), lambda i, b: (0, 0)),
                pl.BlockSpec((ENODES, PART), quarter),
                pl.BlockSpec((SLOTS, PART), quarter),
                pl.BlockSpec((SLOTS, PART), quarter),
            ],
            out_specs=(pl.BlockSpec((ROWS, 1, 3 * PART), lambda i, b: (0, 0, 0)), SM, SM),
            scratch_shapes=[pltpu.VMEM((SLOTS, 3 * PART), F32), pltpu.SMEM((DOMAINS,), I32)],
        ),
        compiler_params=params(8),
        cost_estimate=cost(12 * SLOTS * ENODES * PART, 2 * MIB),
        name="pack_fields",
    )(band, slot_cell, cell_slot, nodes, shape, core, weight)


def first_kernel(
    orb_ref, occ_ref, val_ref, grad_ref, part_ref, quad_ref,
    wide_ref, node_ref, table_ref, spread_ref, slab_ref, sem_ref,
):
    table_ref[:, NODES - 7 :, :] = jnp.zeros((4, KPAD - NODES + 7, POINTS), BF16)
    table_ref[0, :NODES, :] = val_ref[...]
    for k in range(3):
        table_ref[k + 1, :NODES, :] = grad_ref[k]
    spread_ref[...] = jnp.broadcast_to(occ_ref[...], (BANDS, BANDS)).T

    def widen(i, carry):
        part = orb_ref[pl.ds(i * STEP, STEP)].astype(F32)
        wide_ref[pl.ds(i * STEP * CELLS, STEP * CELLS), :] = part.reshape(STEP * CELLS, BANDS)
        return carry

    lax.fori_loop(0, NODES // STEP, widen, 0)
    wide_ref[NODES * CELLS :, :] = jnp.zeros(((KPAD - NODES) * CELLS, BANDS), F32)

    def send(g):
        return pltpu.make_async_copy(
            slab_ref.at[g % 2], quad_ref.at[pl.ds(g * GROUP, GROUP)], sem_ref.at[g % 2]
        )

    for g in range(CELLS // GROUP):
        slab = slab_ref.at[g % 2]
        if g >= 2:
            send(g - 2).wait()
        for i in range(GROUP):
            block = wide_ref[pl.ds(g * GROUP + i, KPAD, stride=CELLS), :]
            node_ref[i * BANDS : (i + 1) * BANDS, :] = block.T.astype(BF16)
        for k in range(4):
            values = jnp.dot(node_ref[...], table_ref[k], preferred_element_type=F32)
            for i in range(GROUP):
                slab[i, k] = values[i * BANDS : (i + 1) * BANDS]
        for i in range(GROUP):
            c = g * GROUP + i
            for lane in range(POINTS // 128):
                cols = lanes(lane)
                lead = slab[i, 0, :, cols]
                scaled = spread_ref[...] * lead
                part_ref[0, c : c + 1, cols] = jnp.sum(scaled * lead, axis=0, keepdims=True)
                for k in range(1, 4):
                    term = slab[i, k, :, cols]
                    part_ref[k, c : c + 1, cols] = 2.0 * jnp.sum(scaled * term, axis=0, keepdims=True)
        send(g).start()
    send(CELLS // GROUP - 2).wait()
    send(CELLS // GROUP - 1).wait()


def first_pass(orbitals, occupancy, values, grads):
    return pl.pallas_call(
        first_kernel,
        out_shape=(
            jax.ShapeDtypeStruct((4, CELLS, POINTS), F32),
            jax.ShapeDtypeStruct((CELLS, 4, BANDS, POINTS), F32),
        ),
        in_specs=[VM] * 4,
        out_specs=(VM, HB),
        scratch_shapes=[
            pltpu.VMEM((KPAD * CELLS, BANDS), F32),
            pltpu.VMEM((GROUP * BANDS, KPAD), BF16),
            pltpu.VMEM((4, KPAD, POINTS), BF16),
            pltpu.VMEM((BANDS, BANDS), F32),
            pltpu.VMEM((2, GROUP, 4, BANDS, POINTS), F32),
            pltpu.SemaphoreType.DMA((2,)),
        ],
        compiler_params=params(32),
        cost_estimate=cost(2 * 2048 * 512 * 3072, 28 * MIB),
        name="first_pass",
    )(orbitals, occupancy, values, grads)


def density_kernel(row_ref, a_ref, b_ref, c_ref, d_ref, send_ref, sum_ref):
    sum_ref[...] = (a_ref[0] + b_ref[0]) + (c_ref[0] + d_ref[0])
    for c in range(CELLS):
        send_ref[row_ref[c]] = sum_ref[c : c + 1, :]


def pack_density(rows, parts):
    lead = pl.BlockSpec((1, CELLS, POINTS), lambda i: (0, 0, 0))
    return pl.pallas_call(
        density_kernel,
        out_shape=jax.ShapeDtypeStruct((ROWS, 1, POINTS), F32),
        grid=(1,),
        in_specs=[SM] + [lead] * 4,
        out_specs=pl.BlockSpec((ROWS, 1, POINTS), lambda i: (0, 0, 0)),
        scratch_shapes=[pltpu.VMEM((CELLS, POINTS), F32)],
        compiler_params=params(8),
        cost_estimate=cost(1e5, MIB // 2),
        name="pack_density",
    )(rows, *parts)


def exchange_terms(density, square):
    third = jnp.exp(jnp.log(density) * (1.0 / 3.0))
    power_four = density * third
    reduced = reduced_coef * square / (power_four * power_four)
    inner = 1.0 + slope_coef * reduced / bound_kappa
    slope = slope_coef / (inner * inner)
    enhance = 1.0 + bound_kappa - bound_kappa / inner
    d_density = -slater_coef * third * ((4.0 / 3.0) * enhance - (8.0 / 3.0) * reduced * slope)
    d_square = -slater_coef * reduced_coef * slope / power_four
    return d_density, d_square


def second_kernel(
    band_ref, row_ref, e0_ref, e1_ref, e2_ref, e3_ref, a_ref, b_ref, c_ref, d_ref,
    val_ref, grad_ref, quad_ref, out_ref,
    field_ref, wt_ref, wide_ref, table_ref, prod_ref, slab_ref, sem_ref,
):
    pairs = CELLS // 2

    def fetch(p):
        return pltpu.make_async_copy(
            quad_ref.at[pl.ds(2 * p, 2)], slab_ref.at[p % 3], sem_ref.at[p % 3]
        )

    fetch(0).start()
    fetch(1).start()
    table_ref[:, :POINTS] = val_ref[...]
    for k in range(3):
        table_ref[:, (k + 1) * POINTS : (k + 2) * POINTS] = grad_ref[k]
    for d, source in enumerate((e0_ref, e1_ref, e2_ref, e3_ref)):
        rank = (band_ref[0] + RANKS - d) & (RANKS - 1)
        for c in range(CELLS):
            row = row_ref[c]
            for f in range(3):
                field_ref[rank, f, c : c + 1, :] = source[row, :, lanes(f)]
    for q in range(RANKS):
        cols = lanes(q)
        total = [(a_ref[k, :, cols] + b_ref[k, :, cols]) + (c_ref[k, :, cols] + d_ref[k, :, cols]) for k in range(4)]
        core, weight, hartree = field_ref[q, 0], field_ref[q, 1], field_ref[q, 2]
        square = total[1] * total[1] + total[2] * total[2] + total[3] * total[3]
        d_density, d_square = exchange_terms(core + total[0], square)
        wt_ref[0, :, cols] = weight * (d_density + hartree)
        for k in range(1, 4):
            wt_ref[k, :, cols] = 2.0 * weight * d_square * total[k]

    def products(p):
        slab, prod = slab_ref.at[p % 3], prod_ref.at[p % 2]
        for half in range(2):
            c = 2 * p + half
            rows = slice(half * BANDS, half * BANDS + BANDS)
            for lane in range(POINTS // 128):
                cols = lanes(lane)
                r = [wt_ref[k, c : c + 1, cols] for k in range(4)]
                q = [slab[half, k, :, cols] for k in range(4)]
                value = r[0] * q[0] + (r[1] * q[1] + r[2] * q[2] + r[3] * q[3])
                prod[rows, cols] = value.astype(BF16)
                for k in range(1, 4):
                    prod[rows, lanes(4 * k + lane)] = (r[k] * q[0]).astype(BF16)

    def multiply(p):
        result = lax.dot_general(table_ref[...], prod_ref[p % 2], NT, preferred_element_type=F32)
        for half in range(2):
            wide_ref[pl.ds(2 * p + half, NODES, stride=CELLS), :] = result[:, half * BANDS : half * BANDS + BANDS]

    fetch(0).wait()
    products(0)
    for p in range(pairs):
        if p + 2 < pairs:
            fetch(p + 2).start()
        if p + 1 < pairs:
            fetch(p + 1).wait()
            products(p + 1)
        multiply(p)

    def narrow(i, carry):
        part = wide_ref[pl.ds(i * STEP * CELLS, STEP * CELLS), :].reshape(STEP, CELLS, BANDS)
        out_ref[pl.ds(i * STEP, STEP)] = part.astype(BF16)
        return carry

    lax.fori_loop(0, NODES // STEP, narrow, 0)


def second_pass(band, rows, fields, parts, values, grads, quads):
    return pl.pallas_call(
        second_kernel,
        out_shape=jax.ShapeDtypeStruct((NODES, CELLS, BANDS), BF16),
        in_specs=[SM, SM] + [VM] * 10 + [HB],
        out_specs=VM,
        scratch_shapes=[
            pltpu.VMEM((RANKS, 3, CELLS, PART), F32),
            pltpu.VMEM((4, CELLS, POINTS), F32),
            pltpu.VMEM((NODES * CELLS, BANDS), F32),
            pltpu.VMEM((NODES, 4 * POINTS), BF16),
            pltpu.VMEM((2, 2 * BANDS, 4 * POINTS), BF16),
            pltpu.VMEM((3, 2, 4, BANDS, POINTS), F32),
            pltpu.SemaphoreType.DMA((3,)),
        ],
        compiler_params=params(32),
        cost_estimate=cost(2 * 2048 * 343 * 3072, 30 * MIB),
        name="second_pass",
    )(band, rows, *fields, *parts, values, grads, quads)


def stiff_kernel(nodes_ref, stiff_ref, scale_ref, out_ref):
    product = lax.dot_general(nodes_ref[...], stiff_ref[...], NT, precision=HIGHEST, preferred_element_type=F32)
    spread = jnp.broadcast_to(scale_ref[...], (128, SLOTS)).T
    for j in range(0, ENODES, 128):
        width = min(128, ENODES - j)
        out_ref[:, j : j + width] = product[:, j : j + width] * spread[:, :width]


def stiff_part(nodes, stiffness, scale):
    return pl.pallas_call(
        stiff_kernel,
        out_shape=jax.ShapeDtypeStruct((SLOTS, ENODES), F32),
        in_specs=[VM] * 3,
        out_specs=VM,
        compiler_params=params(12),
        cost_estimate=cost(12 * SLOTS * ENODES * ENODES, 3 * MIB),
        name="stiff_part",
    )(nodes, stiffness, scale)


def residual_kernel(row_ref, arrived_ref, core_ref, weight_ref, shape_ref, stiff_ref, out_ref, dens_ref):
    for s in range(SLOTS):
        row = row_ref[s]
        value = arrived_ref[jnp.maximum(row, 0)]
        dens_ref[s : s + 1, :] = jnp.where(row >= 0, value, 0.0)
    source = weight_ref[...] * (core_ref[...] + dens_ref[...])
    load = lax.dot_general(source, shape_ref[...], NT, precision=HIGHEST, preferred_element_type=F32)
    out_ref[...] = stiff_ref[...] - load


def residual(rows, arrived, core, weight, shape, stiff):
    return pl.pallas_call(
        residual_kernel,
        out_shape=jax.ShapeDtypeStruct((SLOTS, ENODES), F32),
        in_specs=[SM] + [VM] * 5,
        out_specs=VM,
        scratch_shapes=[pltpu.VMEM((SLOTS, POINTS), F32)],
        compiler_params=params(12),
        cost_estimate=cost(12 * SLOTS * ENODES * POINTS, 3 * MIB),
        name="residual",
    )(rows, arrived, core, weight, shape, stiff)


def around_band(array, distance):
    return lax.ppermute(array, "band", [(i, (i + distance) % RANKS) for i in range(RANKS)])


def body(
    orbitals, occupancy, shape_values, shape_grads, cell_slot, slot_cell, potential_nodes,
    stiffness, stiff_scale, electro_shape, core_density, quad_weight,
):
    values, grads = shape_values.T, shape_grads.transpose(0, 2, 1)
    nodes, shape = potential_nodes.T, electro_shape.T
    band = lax.axis_index("band").astype(I32).reshape(1)

    send, wave_rows, slot_rows = pack_fields(band, slot_cell, cell_slot, nodes, shape, core_density, quad_weight)
    came = lax.all_to_all(send, "dom", split_axis=0, concat_axis=0, tiled=True)

    part, quads = first_pass(orbitals, occupancy.reshape(1, BANDS), values, grads)
    parts = [part] + [around_band(part, d) for d in (1, 2, 3)]

    stiff = stiff_part(nodes, stiffness, stiff_scale.reshape(1, SLOTS))

    fields = [came] + [around_band(came, d) for d in (1, 2, 3)]
    arrived = lax.all_to_all(pack_density(wave_rows, parts), "dom", split_axis=0, concat_axis=0, tiled=True)

    action = second_pass(band, wave_rows, fields, parts, values, grads, quads)
    rest = residual(slot_rows, arrived, core_density, quad_weight, shape, stiff)
    return action, rest.T


def solution(mesh):
    return jax.shard_map(
        body,
        mesh=mesh,
        in_specs=(
            P(None, "dom", "band"), P("band"), P(), P(), P("dom"), P("dom"),
            P(None, "dom"), P(), P("dom"), P(), P("dom", None), P("dom", None),
        ),
        out_specs=(P(None, "dom", "band"), P(None, "dom")),
        check_vma=False,
    )
```

time: 433 us -> 93.8 us (0.22)
  the two profiles are of different devices: /device:TPU:8 before, /device:TPU:11 now
where the time goes in v1:
time: 93.8 us; the launch traced here: 93.9 us
  Pallas kernels  42.7 us (46%)
  starting transfers between devices  35.3 us (38%)
  local copies, waits for them, and re-layouts  10.3 us (11%)
  waiting for transfers between devices  4.77 us (5%)
    pallas_call x1, Pallas kernels, second_pass(): pl.pallas_call(second_kernel, out_shape=jax.ShapeDtypeStruct((NODES, CELL...  20.7 us
    all_to_all x1, starting transfers between devices, body(): lax.all_to_all(pack_density(wave_rows, parts), 'dom', split_axis=0, conca...  15 us
    pallas_call x1, Pallas kernels, first_pass(): pl.pallas_call(first_kernel, out_shape=(jax.ShapeDtypeStruct((4, CELLS, P...  12.5 us
    all_to_all x1, starting transfers between devices, body(): came = lax.all_to_all(send, 'dom', split_axis=0, concat_axis=0, tiled=True)  12.2 us
    unnamed x40, local copies, waits for them, and re-layouts  10.3 us
    ppermute x6, starting transfers between devices, around_band(): lax.ppermute(array, 'band', [(i, (i + distance) % RANKS) for i in range(R...  8.01 us
    ppermute x6, waiting for transfers between devices, around_band(): lax.ppermute(array, 'band', [(i, (i + distance) % RANKS) for i in range(R...  4.76 us
    pallas_call x1, Pallas kernels, pack_fields(): pl.pallas_call(fields_kernel, out_shape=(jax.ShapeDtypeStruct((ROWS, 1, 3...  3.44 us
  transfers between devices with their start and end apart: 8, of which 2 were waited for; matrix products, arithmetic and copies ran while one was open for 0% of the time, Pallas kernels for 39%

profile of v1, /device:TPU:11, one launch (start us, length us, event | category | flops | bytes accessed | tf_op | source)
XLA Modules:
  0.0 93.9 jit_solution(14138058867154000448)
XLA Ops:
  0.7 1.4 %copy-done = f32[512,729]{0,1:T(8,128)S(1)} copy-done((f32[512,729]{0,1:T(8,128)S(1)}, f32[512,729]{0,1:T(8,128)}, u32[]{:S(2)}) %copy-start) | copy-done | bytes 1493016
  2.0 0.9 copy-done.7
  2.9 0.9 copy-done.9
  3.8 0.9 copy-done.11
  4.7 0.7 copy-done.15
  6.0 3.4 %pack_fields.1 = (f32[128,1,384]{2,1,0:T(1,128)}, s32[24]{0:T(128)S(1)}, s32[48]{0:T(128)S(1)}) custom-call(s32[1]{0:T(128)} %bitcast.band_ref, s32[48]{0:T(128)S(1)} %copy-done.15, s32[24]{0:T(128)S(1)} %copy-done.16, f32[48,729]{1,0:T(8,128)S(1)} %bitcast.12, f32[729,512]{1,0:T(8,128)S(1)} %bitcast.8, f32[48,512]{1,0:T(8,128)S(1)} %copy-done.9, ...), custom_call_target="tpu_custom_call" | custom-call | flops 53747712 | bytes 2097152 | tf_op jit(solution)/shard_map/pack_fields/pallas_call | solution.py:100
  9.5 12.2 %all-to-all-start = ((f32[128,1,384]{2,1,0:T(1,128)}), f32[128,1,384]{2,1,0:T(1,128)S(1)}, u32[]{:S(2)}, u32[]{:S(2)}) async-start(f32[128,1,384]{2,1,0:T(1,128)} %get-tuple-element.8), calls=%async_computation | async-start | bytes 393216 | tf_op jit(solution)/shard_map/all_to_all | solution.py:379
  21.8 1.0 %copy-done.13 = bf16[512,343]{0,1:T(8,128)(2,1)S(1)} copy-done((bf16[512,343]{0,1:T(8,128)(2,1)S(1)}, bf16[512,343]{0,1:T(8,128)(2,1)}, u32[]{:S(2)}) %copy-start.13) | copy-done | bytes 351256
  22.8 1.6 %copy-done.18 = bf16[343,24,128]{2,1,0:T(8,128)(2,1)S(1)} copy-done((bf16[343,24,128]{2,1,0:T(8,128)(2,1)S(1)}, bf16[343,24,128]{2,1,0:T(8,128)(2,1)}, u32[]{:S(2)}) %copy-start.18) | copy-done | bytes 2107416
  24.4 12.5 %first_pass.1 = (f32[4,24,512]{2,1,0:T(8,128)}, f32[24,4,128,512]{3,2,1,0:T(8,128)}) custom-call(bf16[343,24,128]{2,1,0:T(8,128)(2,1)S(1)} %copy-done.18, f32[1,128]{1,0:T(1,128)S(1)} %bitcast.17, bf16[343,512]{1,0:T(8,128)(2,1)S(1)} %bitcast.14, bf16[3,343,512]{2,1,0:T(8,128)(2,1)S(1)} %bitcast.10), custom_call_target="tpu_custom_call" | custom-call | flops 6442450944 | bytes 29360128 | tf_op jit(solution)/shard_map/first_pass/pallas_call | solution.py:177
  36.9 1.3 %collective-permute-start.3 = (f32[4,24,512]{2,1,0:T(8,128)}, f32[4,24,512]{2,1,0:T(8,128)}, u32[]{:S(2)}, u32[]{:S(2)}) collective-permute-start(f32[4,24,512]{2,1,0:T(8,128)} %get-tuple-element.9.a_ref), channel_id=1, source_target_pairs={{0,64},{64,128},{128,192},{192,0},{1,65},{65,129},{129,193},{193,1... | collective-permute-start | bytes 589832 | tf_op jit(solution)/shard_map/ppermute | solution.py:367
  38.2 0.8 collective-permute-start.4
  39.0 1.9 %collective-permute-start.5 = (f32[4,24,512]{2,1,0:T(8,128)}, f32[4,24,512]{2,1,0:T(8,128)}, u32[]{:S(2)}, u32[]{:S(2)}) collective-permute-start(f32[4,24,512]{2,1,0:T(8,128)} %get-tuple-element.9.a_ref), channel_id=1, source_target_pairs={{0,192},{64,0},{128,64},{192,128},{1,193},{65,1},{129,65},{193,129... | collective-permute-start | bytes 589832 | tf_op jit(solution)/shard_map/ppermute | solution.py:367
  40.9 2.9 %collective-permute-start.1 = (f32[128,1,384]{2,1,0:T(1,128)S(1)}, f32[128,1,384]{2,1,0:T(1,128)}, u32[]{:S(2)}, u32[]{:S(2)}) collective-permute-start(f32[128,1,384]{2,1,0:T(1,128)S(1)} %all-to-all-done.e0_ref), channel_id=1, source_target_pairs={{0,128},{64,192},{128,0},{192,64},{1,129},{65,193},{129,1},{193,65... | collective-permute-start | bytes 589832 | tf_op jit(solution)/shard_map/ppermute | solution.py:367
  43.8 1.1 %collective-permute-start.2 = (f32[128,1,384]{2,1,0:T(1,128)S(1)}, f32[128,1,384]{2,1,0:T(1,128)}, u32[]{:S(2)}, u32[]{:S(2)}) collective-permute-start(f32[128,1,384]{2,1,0:T(1,128)S(1)} %all-to-all-done.e0_ref), channel_id=1, source_target_pairs={{0,192},{64,0},{128,64},{192,128},{1,193},{65,1},{129,65},{193,129... | collective-permute-start | bytes 589832 | tf_op jit(solution)/shard_map/ppermute | solution.py:367
  44.9 1.0 %collective-permute-done.4.c_ref = f32[4,24,512]{2,1,0:T(8,128)} collective-permute-done((f32[4,24,512]{2,1,0:T(8,128)}, f32[4,24,512]{2,1,0:T(8,128)}, u32[]{:S(2)}, u32[]{:S(2)}) %collective-permute-start.4) | collective-permute-done | bytes 196640 | tf_op jit(solution)/shard_map/ppermute | solution.py:367
  45.9 3.7 %collective-permute-done.5.d_ref = f32[4,24,512]{2,1,0:T(8,128)} collective-permute-done((f32[4,24,512]{2,1,0:T(8,128)}, f32[4,24,512]{2,1,0:T(8,128)}, u32[]{:S(2)}, u32[]{:S(2)}) %collective-permute-start.5) | collective-permute-done | bytes 196640 | tf_op jit(solution)/shard_map/ppermute | solution.py:367
  49.6 0.9 pack_density.1
  50.6 0.7 copy-done.4
  51.3 15.0 %all-to-all-start.1 = ((f32[128,1,512]{2,1,0:T(1,128)}), f32[128,1,512]{2,1,0:T(1,128)}, u32[]{:S(2)}, u32[]{:S(2)}) async-start(f32[128,1,512]{2,1,0:T(1,128)} %copy-done.4), calls=%async_computation.1 | async-start | bytes 524288 | tf_op jit(solution)/shard_map/all_to_all | solution.py:387
  66.3 0.9 copy-done.8
  67.2 2.0 %stiff_part.1.stiff_ref = f32[48,729]{1,0:T(8,128)S(1)} custom-call(f32[48,729]{1,0:T(8,128)S(1)} %bitcast.13, f32[729,729]{1,0:T(8,128)S(1)} %copy-done.2, f32[1,48]{1,0:T(1,128)S(1)} %bitcast.16), custom_call_target="tpu_custom_call" | custom-call | flops 306110016 | bytes 3145728 | tf_op jit(solution)/shard_map/stiff_part/pallas_call | solution.py:332
  70.0 20.7 %second_pass.1 = bf16[343,24,128]{2,1,0:T(8,128)(2,1)} custom-call(s32[1]{0:T(128)} %bitcast.band_ref, s32[24]{0:T(128)S(1)} %get-tuple-element.7.row_ref, f32[128,1,384]{2,1,0:T(1,128)S(1)} %all-to-all-done.e0_ref, f32[128,1,384]{2,1,0:T(1,128)} %collective-permute-done.e1_ref, f32[128,1,384]{2,1,0:T(1,128)} %collective-permute-done.1.e2_ref, ...), custom_call_target="tpu_custom_call" | custom-call | flops 4315938816 | bytes 31457280 | tf_op jit(solution)/shard_map/second_pass/pallas_call | solution.py:303
  90.8 3.1 %residual.1 = f32[48,729]{1,0:T(8,128)} custom-call(s32[48]{0:T(128)S(1)} %get-tuple-element.11.row_ref, f32[128,1,512]{2,1,0:T(1,128)} %all-to-all-done.1.arrived_ref, f32[48,512]{1,0:T(8,128)S(1)} %copy-done.10, f32[48,512]{1,0:T(8,128)S(1)} %copy-done.12, f32[729,512]{1,0:T(8,128)S(1)} %bitcast.9, f32[48,729]{1,0:T(8,128)S(1)} %copy-done.6), custom_call_target="tpu_custom_call" | custom-call | flops 214990848 | bytes 3145728 | tf_op jit(solution)/shard_map/residual/pallas_call | solution.py:354
  (38 shorter events, 1.4 us)
Async XLA Ops:
  0.6 21.1 %copy-start.19 = (f32[128]{0:T(128)S(1)}, f32[128]{0:T(128)}, u32[]{:S(2)}) copy-start(f32[128]{0:T(128)} %param.13) | copy-start | bytes 1540
  0.6 1.4 %copy-start = (f32[512,729]{0,1:T(8,128)S(1)}, f32[512,729]{0,1:T(8,128)}, u32[]{:S(2)}) copy-start(f32[512,729]{0,1:T(8,128)} %param.21) | copy-start | bytes 4478980
  2.0 0.9 copy-start.7
  2.9 0.9 copy-start.9
  3.8 0.9 copy-start.11
  6.0 15.7 %copy-start.3 = (bf16[3,512,343]{1,2,0:T(8,128)(2,1)S(1)}, bf16[3,512,343]{1,2,0:T(8,128)(2,1)}, u32[]{:S(2)}) copy-start(bf16[3,512,343]{1,2,0:T(8,128)(2,1)} %param.15) | copy-start | bytes 3161092
  9.5 31.4 %all-to-all-start = ((f32[128,1,384]{2,1,0:T(1,128)}), f32[128,1,384]{2,1,0:T(1,128)S(1)}, u32[]{:S(2)}, u32[]{:S(2)}) async-start(f32[128,1,384]{2,1,0:T(1,128)} %get-tuple-element.8), calls=%async_computation | async-start | bytes 393216 | tf_op jit(solution)/shard_map/all_to_all | solution.py:379
  21.8 1.0 %copy-start.13 = (bf16[512,343]{0,1:T(8,128)(2,1)S(1)}, bf16[512,343]{0,1:T(8,128)(2,1)}, u32[]{:S(2)}) copy-start(bf16[512,343]{0,1:T(8,128)(2,1)} %param.14) | copy-start | bytes 1053700
  22.8 1.6 %copy-start.18 = (bf16[343,24,128]{2,1,0:T(8,128)(2,1)S(1)}, bf16[343,24,128]{2,1,0:T(8,128)(2,1)}, u32[]{:S(2)}) copy-start(bf16[343,24,128]{2,1,0:T(8,128)(2,1)} %orb_ref.1) | copy-start | bytes 6322180
  24.3 42.0 %copy-start.2 = (f32[729,729]{1,0:T(8,128)S(1)}, f32[729,729]{1,0:T(8,128)}, u32[]{:S(2)}) copy-start(f32[729,729]{1,0:T(8,128)} %stiff_ref.1) | copy-start | bytes 6377296
  24.3 42.0 %copy-start.17 = (f32[48]{0:T(128)S(1)}, f32[48]{0:T(128)}, u32[]{:S(2)}) copy-start(f32[48]{0:T(128)} %param.20) | copy-start | bytes 580
  36.9 7.0 %collective-permute-start.3 = (f32[4,24,512]{2,1,0:T(8,128)}, f32[4,24,512]{2,1,0:T(8,128)}, u32[]{:S(2)}, u32[]{:S(2)}) collective-permute-start(f32[4,24,512]{2,1,0:T(8,128)} %get-tuple-element.9.a_ref), channel_id=1, source_target_pairs={{0,64},{64,128},{128,192},{192,0},{1,65},{65,129},{129,193},{193,1... | collective-permute-start | bytes 589832 | tf_op jit(solution)/shard_map/ppermute | solution.py:367
  38.2 7.7 %collective-permute-start.4 = (f32[4,24,512]{2,1,0:T(8,128)}, f32[4,24,512]{2,1,0:T(8,128)}, u32[]{:S(2)}, u32[]{:S(2)}) collective-permute-start(f32[4,24,512]{2,1,0:T(8,128)} %get-tuple-element.9.a_ref), channel_id=1, source_target_pairs={{0,128},{64,192},{128,0},{192,64},{1,129},{65,193},{129,1},{193,65... | collective-permute-start | bytes 589832 | tf_op jit(solution)/shard_map/ppermute | solution.py:367
  39.0 10.6 %collective-permute-start.5 = (f32[4,24,512]{2,1,0:T(8,128)}, f32[4,24,512]{2,1,0:T(8,128)}, u32[]{:S(2)}, u32[]{:S(2)}) collective-permute-start(f32[4,24,512]{2,1,0:T(8,128)} %get-tuple-element.9.a_ref), channel_id=1, source_target_pairs={{0,192},{64,0},{128,64},{192,128},{1,193},{65,1},{129,65},{193,129... | collective-permute-start | bytes 589832 | tf_op jit(solution)/shard_map/ppermute | solution.py:367
  40.9 29.0 %collective-permute-start = (f32[128,1,384]{2,1,0:T(1,128)S(1)}, f32[128,1,384]{2,1,0:T(1,128)}, u32[]{:S(2)}, u32[]{:S(2)}) collective-permute-start(f32[128,1,384]{2,1,0:T(1,128)S(1)} %all-to-all-done.e0_ref), channel_id=1, source_target_pairs={{0,64},{64,128},{128,192},{192,0},{1,65},{65,129},{129,193},{193,1... | collective-permute-start | bytes 589832 | tf_op jit(solution)/shard_map/ppermute | solution.py:367
  40.9 29.0 %collective-permute-start.1 = (f32[128,1,384]{2,1,0:T(1,128)S(1)}, f32[128,1,384]{2,1,0:T(1,128)}, u32[]{:S(2)}, u32[]{:S(2)}) collective-permute-start(f32[128,1,384]{2,1,0:T(1,128)S(1)} %all-to-all-done.e0_ref), channel_id=1, source_target_pairs={{0,128},{64,192},{128,0},{192,64},{1,129},{65,193},{129,1},{193,65... | collective-permute-start | bytes 589832 | tf_op jit(solution)/shard_map/ppermute | solution.py:367
  43.8 26.1 %collective-permute-start.2 = (f32[128,1,384]{2,1,0:T(1,128)S(1)}, f32[128,1,384]{2,1,0:T(1,128)}, u32[]{:S(2)}, u32[]{:S(2)}) collective-permute-start(f32[128,1,384]{2,1,0:T(1,128)S(1)} %all-to-all-done.e0_ref), channel_id=1, source_target_pairs={{0,192},{64,0},{128,64},{192,128},{1,193},{65,1},{129,65},{193,129... | collective-permute-start | bytes 589832 | tf_op jit(solution)/shard_map/ppermute | solution.py:367
  51.3 39.4 %all-to-all-start.1 = ((f32[128,1,512]{2,1,0:T(1,128)}), f32[128,1,512]{2,1,0:T(1,128)}, u32[]{:S(2)}, u32[]{:S(2)}) async-start(f32[128,1,512]{2,1,0:T(1,128)} %copy-done.4), calls=%async_computation.1 | async-start | bytes 524288 | tf_op jit(solution)/shard_map/all_to_all | solution.py:387
  66.3 0.9 copy-start.8
  67.2 2.7 %copy-start.14 = (bf16[512,343]{0,1:T(8,128)(2,1)S(1)}, bf16[512,343]{0,1:T(8,128)(2,1)}, u32[]{:S(2)}) copy-start(bf16[512,343]{0,1:T(8,128)(2,1)} %param.14) | copy-start | bytes 1053700
  70.0 20.8 %copy-start.1 = (f32[512,729]{0,1:T(8,128)S(1)}, f32[512,729]{0,1:T(8,128)}, u32[]{:S(2)}) copy-start(f32[512,729]{0,1:T(8,128)} %param.21) | copy-start | bytes 4478980
  70.0 20.8 %copy-start.6 = (f32[48,729]{1,0:T(8,128)S(1)}, f32[48,729]{1,0:T(8,128)}, u32[]{:S(2)}) copy-start(f32[48,729]{1,0:T(8,128)} %copy-done.5) | copy-start | bytes 419908
  70.0 20.8 %copy-start.10 = (f32[48,512]{1,0:T(8,128)S(1)}, f32[48,512]{1,0:T(8,128)}, u32[]{:S(2)}) copy-start(f32[48,512]{1,0:T(8,128)} %core_ref.3) | copy-start | bytes 294916
  70.0 20.8 %copy-start.12 = (f32[48,512]{1,0:T(8,128)S(1)}, f32[48,512]{1,0:T(8,128)}, u32[]{:S(2)}) copy-start(f32[48,512]{1,0:T(8,128)} %weight_ref.3) | copy-start | bytes 294916
  (4 other events, 2.7 us)

commit v2 on v1

v2 whole, which is shorter than its diff:
```python
import functools

import jax
import jax.numpy as jnp
from jax import lax
from jax.experimental import pallas as pl
from jax.experimental.pallas import tpu as pltpu
from jax.sharding import PartitionSpec as P

F32, BF16, I32 = jnp.float32, jnp.bfloat16, jnp.int32
NODES, CELLS, BANDS, POINTS = 343, 24, 128, 512
KPAD = 384
SLOTS, ENODES, DOMAINS, CAP = 48, 729, 64, 2
ROWS = DOMAINS * CAP
RANKS, PART = 4, 128
GROUP = 4
STEP = 49
FIELDS = 3 * PART
WIDTH = FIELDS + POINTS
TERMS = 4 * CELLS
MIX = TERMS + RANKS * SLOTS
HIGHEST = lax.Precision.HIGHEST
NT = (((1,), (1,)), ((), ()))
MIB = 1 << 20

slater_coef = 0.7385587663820224
bound_kappa = 0.804
slope_coef = 0.2195149727645171
reduced_coef = 0.026121172985233605

VM = pl.BlockSpec(memory_space=pltpu.VMEM)
SM = pl.BlockSpec(memory_space=pltpu.SMEM)
HB = pl.BlockSpec(memory_space=pltpu.HBM)


def params(mib):
    return pltpu.CompilerParams(vmem_limit_bytes=mib * MIB)


def cost(flops, nbytes):
    return pl.CostEstimate(flops=int(flops), bytes_accessed=int(nbytes), transcendentals=0)


def lanes(index):
    return slice(index * 128, index * 128 + 128)


def first_kernel(
    band_ref, slot_cell_ref, cell_slot_ref,
    orb_hbm, occ_ref, val_hbm, nodes_hbm, shape_hbm, core_hbm, weight_hbm,
    send_hbm, node_hbm, wave_row_ref, slot_row_ref,
    orb_ref, val_ref, nodes_ref, shape_ref, field_ref, send_ref,
    wide_ref, node_ref, table_ref, spread_ref, sum_ref, count_ref, in_sem, orb_sem, out_sem, send_sem,
):
    mine = pl.ds(pl.multiple_of(band_ref[0] * PART, PART), PART)
    chunks = NODES // STEP

    def take(i):
        part = pl.ds(i * STEP, STEP)
        return pltpu.make_async_copy(orb_hbm.at[part], orb_ref.at[part], orb_sem.at[i])

    loads = [
        pltpu.make_async_copy(val_hbm, val_ref, in_sem.at[0]),
        pltpu.make_async_copy(nodes_hbm, nodes_ref, in_sem.at[1]),
        pltpu.make_async_copy(shape_hbm.at[:, mine], shape_ref, in_sem.at[2]),
        pltpu.make_async_copy(core_hbm.at[:, mine], field_ref.at[:, lanes(0)], in_sem.at[3]),
        pltpu.make_async_copy(weight_hbm.at[:, mine], field_ref.at[:, lanes(1)], in_sem.at[4]),
    ]
    for load in loads:
        load.start()
    for i in range(chunks):
        take(i).start()

    for d in range(DOMAINS + 1):
        count_ref[d] = 0
    for s in range(SLOTS):
        cell = slot_cell_ref[s]
        filled = cell >= 0
        source = jnp.where(filled, lax.shift_right_logical(cell * 10923, 18), DOMAINS)
        place = jnp.minimum(count_ref[source], CAP - 1)
        count_ref[source] = jnp.where(filled, place + 1, 0)
        slot_row_ref[s] = jnp.where(filled, source * CAP + place, ROWS)
    for d in range(DOMAINS):
        count_ref[d] = -1
    for c in range(CELLS):
        slot = cell_slot_ref[c]
        owner = lax.shift_right_logical(slot * 21846, 20)
        other = count_ref[owner]
        known = other >= 0
        first = jnp.maximum(other, 0)
        later = known & (cell_slot_ref[first] > slot)
        wave_row_ref[c] = owner * CAP + jnp.where(known & jnp.logical_not(later), 1, 0)
        target = jnp.where(later, first, c)
        wave_row_ref[target] = jnp.where(later, owner * CAP + 1, wave_row_ref[c])
        count_ref[owner] = c

    spread_ref[...] = jnp.broadcast_to(occ_ref[...], (BANDS, BANDS)).T
    table_ref[NODES - 7 :, :] = jnp.zeros((KPAD - NODES + 7, POINTS), BF16)
    wide_ref[NODES * CELLS :, :] = jnp.zeros(((KPAD - NODES) * CELLS, BANDS), F32)

    for load in loads:
        load.wait()
    table_ref[:NODES, :] = val_ref[...]
    field_ref[:, lanes(2)] = jnp.dot(
        nodes_ref[...], shape_ref[...], precision=HIGHEST, preferred_element_type=F32
    )
    for s in range(SLOTS):
        send_ref[slot_row_ref[s], :, :FIELDS] = field_ref[s : s + 1, :]

    for i in range(chunks):
        take(i).wait()
        part = orb_ref[pl.ds(i * STEP, STEP)].astype(F32)
        wide_ref[pl.ds(i * STEP * CELLS, STEP * CELLS), :] = part.reshape(STEP * CELLS, BANDS)

    def store(g):
        rows = pl.ds(g * GROUP * BANDS, GROUP * BANDS)
        return pltpu.make_async_copy(node_ref.at[rows], node_hbm.at[rows], out_sem.at[g])

    groups = CELLS // GROUP
    for g in range(groups):
        rows = slice(g * GROUP * BANDS, (g + 1) * GROUP * BANDS)
        for i in range(GROUP):
            c = g * GROUP + i
            block = wide_ref[pl.ds(c, KPAD, stride=CELLS), :]
            node_ref[c * BANDS : (c + 1) * BANDS, :] = block.T.astype(BF16)
        store(g).start()
        values = jnp.dot(node_ref[rows, :], table_ref[...], preferred_element_type=F32)
        for i in range(GROUP):
            c = g * GROUP + i
            for q in range(RANKS):
                lead = values[i * BANDS : (i + 1) * BANDS, lanes(q)]
                sum_ref[c : c + 1, lanes(q)] = jnp.sum(spread_ref[...] * lead * lead, axis=0, keepdims=True)
    for c in range(CELLS):
        send_ref[wave_row_ref[c], :, FIELDS:] = sum_ref[c : c + 1, :]
    leave = pltpu.make_async_copy(send_ref.at[pl.ds(0, ROWS)], send_hbm, send_sem)
    leave.start()
    for g in range(groups):
        store(g).wait()
    leave.wait()


def first_pass(band, slot_cell, cell_slot, orbitals, occupancy, values, nodes, shape, core, weight):
    return pl.pallas_call(
        first_kernel,
        out_shape=(
            jax.ShapeDtypeStruct((ROWS, 1, WIDTH), F32),
            jax.ShapeDtypeStruct((CELLS * BANDS, KPAD), BF16),
            jax.ShapeDtypeStruct((CELLS,), I32),
            jax.ShapeDtypeStruct((SLOTS,), I32),
        ),
        in_specs=[SM, SM, SM, HB, VM] + [HB] * 5,
        out_specs=(HB, HB, SM, SM),
        scratch_shapes=[
            pltpu.VMEM((NODES, CELLS, BANDS), BF16),
            pltpu.VMEM((NODES, POINTS), BF16),
            pltpu.VMEM((SLOTS, ENODES), F32),
            pltpu.VMEM((ENODES, PART), F32),
            pltpu.VMEM((SLOTS, FIELDS), F32),
            pltpu.VMEM((ROWS + 1, 1, WIDTH), F32),
            pltpu.VMEM((KPAD * CELLS, BANDS), F32),
            pltpu.VMEM((CELLS * BANDS, KPAD), BF16),
            pltpu.VMEM((KPAD, POINTS), BF16),
            pltpu.VMEM((BANDS, BANDS), F32),
            pltpu.VMEM((CELLS, POINTS), F32),
            pltpu.SMEM((DOMAINS + 1,), I32),
            pltpu.SemaphoreType.DMA((5,)),
            pltpu.SemaphoreType.DMA((NODES // STEP,)),
            pltpu.SemaphoreType.DMA((CELLS // GROUP,)),
            pltpu.SemaphoreType.DMA,
        ],
        compiler_params=params(60),
        cost_estimate=cost(2 * 512 * 512 * 3072, 8 * MIB),
        name="first_pass",
    )(band, slot_cell, cell_slot, orbitals, occupancy, values, nodes, shape, core, weight)


def gradient_kernel(
    band_ref, occ_ref, val_hbm, grad_hbm, node_hbm,
    part0_ref, part1_ref, part2_ref, part3_ref, table_hbm,
    val_ref, grad_ref, node_ref, table_ref, spread_ref, slab_ref, sum_ref, in_sem, node_sem, out_sem,
):
    groups = CELLS // GROUP

    def take(g):
        rows = pl.ds(g * GROUP * BANDS, GROUP * BANDS)
        return pltpu.make_async_copy(node_hbm.at[rows], node_ref.at[rows], node_sem.at[g])

    loads = [
        pltpu.make_async_copy(val_hbm, val_ref, in_sem.at[0]),
        pltpu.make_async_copy(grad_hbm, grad_ref, in_sem.at[1]),
    ]
    for load in loads:
        load.start()
    for g in range(groups):
        take(g).start()
    spread_ref[...] = jnp.broadcast_to(occ_ref[...], (BANDS, BANDS)).T
    table_ref[NODES - 7 :, :] = jnp.zeros((KPAD - NODES + 7, 4 * POINTS), BF16)
    loads[0].wait()
    table_ref[:NODES, :POINTS] = val_ref[...]
    loads[1].wait()
    for k in range(3):
        table_ref[:NODES, (k + 1) * POINTS : (k + 2) * POINTS] = grad_ref[k]
    leave = pltpu.make_async_copy(table_ref, table_hbm, out_sem)
    leave.start()

    for g in range(groups):
        slab = slab_ref.at[g % 2]
        rows = slice(g * GROUP * BANDS, (g + 1) * GROUP * BANDS)
        if g < 2:
            for later in range(g, groups if g else 1):
                take(later).wait()
        for k in range(4):
            slab[k] = jnp.dot(
                node_ref[rows, :], table_ref[:, k * POINTS : (k + 1) * POINTS], preferred_element_type=F32
            )
        for i in range(GROUP):
            c = g * GROUP + i
            bands = slice(i * BANDS, (i + 1) * BANDS)
            for q in range(RANKS):
                lead = slab[0, bands, lanes(q)]
                scaled = spread_ref[...] * lead
                sum_ref[q, 0, c : c + 1, :] = jnp.sum(scaled * lead, axis=0, keepdims=True)
                for k in range(1, 4):
                    term = slab[k, bands, lanes(q)]
                    sum_ref[q, k, c : c + 1, :] = 2.0 * jnp.sum(scaled * term, axis=0, keepdims=True)
    for d, part_ref in enumerate((part0_ref, part1_ref, part2_ref, part3_ref)):
        part_ref[...] = sum_ref[(band_ref[0] + d) & (RANKS - 1)]
    leave.wait()


def gradient_pass(band, occupancy, values, grads, cell_nodes):
    part = jax.ShapeDtypeStruct((4, CELLS, PART), F32)
    return pl.pallas_call(
        gradient_kernel,
        out_shape=(part, part, part, part, jax.ShapeDtypeStruct((KPAD, 4 * POINTS), BF16)),
        in_specs=[SM, VM] + [HB] * 3,
        out_specs=(VM, VM, VM, VM, HB),
        scratch_shapes=[
            pltpu.VMEM((NODES, POINTS), BF16),
            pltpu.VMEM((3, NODES, POINTS), BF16),
            pltpu.VMEM((CELLS * BANDS, KPAD), BF16),
            pltpu.VMEM((KPAD, 4 * POINTS), BF16),
            pltpu.VMEM((BANDS, BANDS), F32),
            pltpu.VMEM((2, 4, GROUP * BANDS, POINTS), F32),
            pltpu.VMEM((RANKS, 4, CELLS, PART), F32),
            pltpu.SemaphoreType.DMA((2,)),
            pltpu.SemaphoreType.DMA((CELLS // GROUP,)),
            pltpu.SemaphoreType.DMA,
        ],
        compiler_params=params(60),
        cost_estimate=cost(2 * 2048 * 512 * 3072, 8 * MIB),
        name="gradient_pass",
    )(band, occupancy, values, grads, cell_nodes)


def exchange_terms(density, square):
    third = jnp.exp(jnp.log(density) * (1.0 / 3.0))
    power_four = density * third
    reduced = reduced_coef * square / (power_four * power_four)
    inner = 1.0 + slope_coef * reduced / bound_kappa
    slope = slope_coef / (inner * inner)
    enhance = 1.0 + bound_kappa - bound_kappa / inner
    d_density = -slater_coef * third * ((4.0 / 3.0) * enhance - (8.0 / 3.0) * reduced * slope)
    d_square = -slater_coef * reduced_coef * slope / power_four
    return d_density, d_square


def exchange_kernel(wave_row_ref, slot_row_ref, came_ref, a_ref, b_ref, c_ref, d_ref, mix_ref, field_ref):
    for c in range(CELLS):
        row = wave_row_ref[c]
        for f in range(3):
            field_ref[f, c : c + 1, :] = came_ref[row, :, lanes(f)]
    total = [(a_ref[k] + b_ref[k]) + (c_ref[k] + d_ref[k]) for k in range(4)]
    core, weight, hartree = field_ref[0], field_ref[1], field_ref[2]
    square = total[1] * total[1] + total[2] * total[2] + total[3] * total[3]
    d_density, d_square = exchange_terms(core + total[0], square)
    mix_ref[:CELLS, :] = weight * (d_density + hartree)
    for k in range(1, 4):
        mix_ref[k * CELLS : (k + 1) * CELLS, :] = 2.0 * weight * d_square * total[k]
    for s in range(SLOTS):
        row = slot_row_ref[s]
        source = jnp.minimum(row, ROWS - 1)
        for q in range(RANKS):
            value = came_ref[source, :, FIELDS + q * PART : FIELDS + (q + 1) * PART]
            place = TERMS + q * SLOTS + s
            mix_ref[place : place + 1, :] = jnp.where(row < ROWS, value, 0.0)


def exchange(wave_rows, slot_rows, came, parts):
    return pl.pallas_call(
        exchange_kernel,
        out_shape=jax.ShapeDtypeStruct((MIX, PART), F32),
        in_specs=[SM, SM] + [VM] * 5,
        out_specs=VM,
        scratch_shapes=[pltpu.VMEM((3, CELLS, PART), F32)],
        compiler_params=params(8),
        cost_estimate=cost(1e6, MIB),
        name="exchange",
    )(wave_rows, slot_rows, came, *parts)


def second_kernel(
    band_ref, m0_ref, m1_ref, m2_ref, m3_ref, table_hbm, node_hbm, core_hbm, weight_hbm, shape_hbm, stiff_hbm,
    out_hbm, rest_hbm,
    wt_ref, node_ref, table_ref, slab_ref, prod_ref, wide_ref, out_ref,
    core_ref, weight_ref, shape_ref, stiff_ref, source_ref, in_sem, node_sem, out_sem, rest_sem,
):
    groups = CELLS // GROUP

    def take(g):
        rows = pl.ds(g * GROUP * BANDS, GROUP * BANDS)
        return pltpu.make_async_copy(node_hbm.at[rows], node_ref.at[rows], node_sem.at[g])

    load = pltpu.make_async_copy(table_hbm, table_ref, in_sem)
    load.start()
    for g in range(groups):
        take(g).start()
    rests = [
        pltpu.make_async_copy(core_hbm, core_ref, rest_sem.at[0]),
        pltpu.make_async_copy(weight_hbm, weight_ref, rest_sem.at[1]),
        pltpu.make_async_copy(shape_hbm, shape_ref, rest_sem.at[2]),
        pltpu.make_async_copy(stiff_hbm, stiff_ref, rest_sem.at[3]),
    ]
    for rest in rests:
        rest.start()
    for d, source in enumerate((m0_ref, m1_ref, m2_ref, m3_ref)):
        wt_ref[(band_ref[0] + RANKS - d) & (RANKS - 1)] = source[:TERMS, :]

    def evaluate(g, k):
        rows = slice(g * GROUP * BANDS, (g + 1) * GROUP * BANDS)
        slab_ref[g % 2, k] = jnp.dot(
            node_ref[rows, :], table_ref[:, k * POINTS : (k + 1) * POINTS], preferred_element_type=F32
        )

    def products(g, i):
        c = g * GROUP + i
        rows = slice(i * BANDS, (i + 1) * BANDS)
        for lane in range(RANKS):
            r = [wt_ref[lane, k * CELLS + c : k * CELLS + c + 1, :] for k in range(4)]
            q = [slab_ref[g % 2, k, rows, lanes(lane)] for k in range(4)]
            value = r[0] * q[0] + (r[1] * q[1] + r[2] * q[2] + r[3] * q[3])
            prod_ref[g % 2, rows, lanes(lane)] = value.astype(BF16)
            for k in range(1, 4):
                prod_ref[g % 2, rows, lanes(4 * k + lane)] = (r[k] * q[0]).astype(BF16)

    def multiply(g, pair):
        rows = slice(2 * pair * BANDS, 2 * (pair + 1) * BANDS)
        result = lax.dot_general(
            table_ref[:NODES, :], prod_ref[g % 2, rows, :], NT, preferred_element_type=F32
        )
        for i in range(2):
            c = g * GROUP + 2 * pair + i
            wide_ref[pl.ds(c, NODES, stride=CELLS), :] = result[:, i * BANDS : (i + 1) * BANDS]

    load.wait()
    take(0).wait()
    for k in range(4):
        evaluate(0, k)
    for g in range(1, groups):
        take(g).wait()
    for g in range(groups):
        for i in range(GROUP):
            if g + 1 < groups:
                evaluate(g + 1, i)
            products(g, i)
            if i % 2 == 1:
                multiply(g, i // 2)

    def leave(i):
        part = pl.ds(i * STEP, STEP)
        return pltpu.make_async_copy(out_ref.at[part], out_hbm.at[part], out_sem.at[i])

    for i in range(NODES // STEP):
        part = wide_ref[pl.ds(i * STEP * CELLS, STEP * CELLS), :].reshape(STEP, CELLS, BANDS)
        out_ref[pl.ds(i * STEP, STEP)] = part.astype(BF16)
        leave(i).start()

    for rest in rests:
        rest.wait()
    for q in range(RANKS):
        rows = slice(TERMS + q * SLOTS, TERMS + (q + 1) * SLOTS)
        dens = (m0_ref[rows, :] + m1_ref[rows, :]) + (m2_ref[rows, :] + m3_ref[rows, :])
        source_ref[:, lanes(q)] = weight_ref[:, lanes(q)] * (core_ref[:, lanes(q)] + dens)
    drawn = lax.dot_general(source_ref[...], shape_ref[...], NT, precision=HIGHEST, preferred_element_type=F32)
    stiff_ref[...] = stiff_ref[...] - drawn
    last = pltpu.make_async_copy(stiff_ref, rest_hbm, rest_sem.at[4])
    last.start()
    for i in range(NODES // STEP):
        leave(i).wait()
    last.wait()


def second_pass(band, mixes, table, cell_nodes, core, weight, shape, stiff):
    return pl.pallas_call(
        second_kernel,
        out_shape=(
            jax.ShapeDtypeStruct((NODES, CELLS, BANDS), BF16),
            jax.ShapeDtypeStruct((SLOTS, ENODES), F32),
        ),
        in_specs=[SM] + [VM] * 4 + [HB] * 6,
        out_specs=(HB, HB),
        scratch_shapes=[
            pltpu.VMEM((RANKS, TERMS, PART), F32),
            pltpu.VMEM((CELLS * BANDS, KPAD), BF16),
            pltpu.VMEM((KPAD, 4 * POINTS), BF16),
            pltpu.VMEM((2, 4, GROUP * BANDS, POINTS), F32),
            pltpu.VMEM((2, GROUP * BANDS, 4 * POINTS), BF16),
            pltpu.VMEM((NODES * CELLS, BANDS), F32),
            pltpu.VMEM((NODES, CELLS, BANDS), BF16),
            pltpu.VMEM((SLOTS, POINTS), F32),
            pltpu.VMEM((SLOTS, POINTS), F32),
            pltpu.VMEM((ENODES, POINTS), F32),
            pltpu.VMEM((SLOTS, ENODES), F32),
            pltpu.VMEM((SLOTS, POINTS), F32),
            pltpu.SemaphoreType.DMA,
            pltpu.SemaphoreType.DMA((CELLS // GROUP,)),
            pltpu.SemaphoreType.DMA((NODES // STEP,)),
            pltpu.SemaphoreType.DMA((5,)),
        ],
        compiler_params=params(60),
        cost_estimate=cost(4 * 2048 * 512 * 3072, 8 * MIB),
        name="second_pass",
    )(band, *mixes, table, cell_nodes, core, weight, shape, stiff)


def stiff_kernel(nodes_ref, stiff_ref, scale_ref, out_ref):
    product = lax.dot_general(nodes_ref[...], stiff_ref[...], NT, precision=HIGHEST, preferred_element_type=F32)
    spread = jnp.broadcast_to(scale_ref[...], (128, SLOTS)).T
    for j in range(0, ENODES, 128):
        width = min(128, ENODES - j)
        out_ref[:, j : j + width] = product[:, j : j + width] * spread[:, :width]


def stiff_part(nodes, stiffness, scale):
    return pl.pallas_call(
        stiff_kernel,
        out_shape=jax.ShapeDtypeStruct((SLOTS, ENODES), F32),
        in_specs=[VM] * 3,
        out_specs=VM,
        compiler_params=params(12),
        cost_estimate=cost(12 * SLOTS * ENODES * ENODES, 3 * MIB),
        name="stiff_part",
    )(nodes, stiffness, scale)


def shift(array, distance):
    return lax.ppermute(array, "band", [(i, (i + distance) % RANKS) for i in range(RANKS)])


def body(
    orbitals, occupancy, shape_values, shape_grads, cell_slot, slot_cell, potential_nodes,
    stiffness, stiff_scale, electro_shape, core_density, quad_weight,
):
    values, grads = shape_values.T, shape_grads.transpose(0, 2, 1)
    nodes, shape = potential_nodes.T, electro_shape.T
    occupancy = occupancy.reshape(1, BANDS)
    band = lax.axis_index("band").astype(I32).reshape(1)

    send, cell_nodes, wave_rows, slot_rows = first_pass(
        band, slot_cell, cell_slot, orbitals, occupancy, values, nodes, shape, core_density, quad_weight
    )
    came = lax.all_to_all(send, "dom", split_axis=0, concat_axis=0, tiled=True)
    *parts, table = gradient_pass(band, occupancy, values, grads, cell_nodes)
    parts = [parts[0]] + [shift(parts[d], d) for d in (1, 2, 3)]
    stiff = stiff_part(nodes, stiffness, stiff_scale.reshape(1, SLOTS))
    mix = exchange(wave_rows, slot_rows, came, parts)
    mixes = [mix] + [shift(mix, d) for d in (1, 2, 3)]
    action, rest = second_pass(band, mixes, table, cell_nodes, core_density, quad_weight, shape, stiff)
    return action, rest.T


def solution(mesh):
    return jax.shard_map(
        body,
        mesh=mesh,
        in_specs=(
            P(None, "dom", "band"), P("band"), P(), P(), P("dom"), P("dom"),
            P(None, "dom"), P(), P("dom"), P(), P("dom", None), P("dom", None),
        ),
        out_specs=(P(None, "dom", "band"), P(None, "dom")),
        check_vma=False,
    )
```

time: 93.8 us -> 71.4 us (0.76)
  the two profiles are of different devices: /device:TPU:11 before, /device:TPU:8 now
where the time goes in v2:
time: 71.4 us; the launch traced here: 71.1 us
  Pallas kernels  39 us (55%)
  starting transfers between devices  21.5 us (30%)
  waiting for transfers between devices  7.52 us (11%)
  local copies, waits for them, and re-layouts  2.13 us (3%)
  between operations  0.91 us (1%)
    pallas_call x1, Pallas kernels, second_pass(): pl.pallas_call(second_kernel, out_shape=(jax.ShapeDtypeStruct((NODES, CEL...  19 us
    all_to_all x1, starting transfers between devices, body(): came = lax.all_to_all(send, 'dom', split_axis=0, concat_axis=0, tiled=True)  12.1 us
    pallas_call x1, Pallas kernels, gradient_pass(): pl.pallas_call(gradient_kernel, out_shape=(part, part, part, part, jax.Sh...  10.5 us
    ppermute x6, starting transfers between devices, shift(): lax.ppermute(array, 'band', [(i, (i + distance) % RANKS) for i in range(R...  9.4 us
    ppermute x6, waiting for transfers between devices, shift(): lax.ppermute(array, 'band', [(i, (i + distance) % RANKS) for i in range(R...  7.52 us
    pallas_call x1, Pallas kernels, first_pass(): pl.pallas_call(first_kernel, out_shape=(jax.ShapeDtypeStruct((ROWS, 1, WI...  6.78 us
    unnamed x22, local copies, waits for them, and re-layouts  2.13 us
    pallas_call x1, Pallas kernels, stiff_part(): pl.pallas_call(stiff_kernel, out_shape=jax.ShapeDtypeStruct((SLOTS, ENODE...  2.02 us
  transfers between devices with their start and end apart: 7, of which 5 were waited for; matrix products, arithmetic and copies ran while one was open for 0% of the time, Pallas kernels for 18%

profile of v2, /device:TPU:8, one launch (start us, length us, event | category | flops | bytes accessed | tf_op | source)
XLA Modules:
  0.0 71.1 jit_solution(18184961799916673877)
XLA Ops:
  0.6 6.8 %first_pass.1 = (f32[128,1,896]{2,1,0:T(1,128)}, bf16[3072,384]{1,0:T(8,128)(2,1)}, s32[24]{0:T(128)}, s32[48]{0:T(128)}) custom-call(s32[1]{0:T(128)} %bitcast.band_ref, s32[48]{0:T(128)} %slot_cell_ref.1, s32[24]{0:T(128)} %cell_slot_ref.1, bf16[343,24,128]{2,1,0:T(8,128)(2,1)} %orb_hbm.1, f32[1,128]{1,0:T(1,128)} %bitcast.16, bf16[343,512]{1,0:T(8,128)(2,1)} %bitcast.14, ...), custom_call_target="tpu_custom_call" | custom-call | flops 1610612736 | bytes 8388608 | tf_op jit(solution)/shard_map/first_pass/pallas_call | solution.py:143
  7.4 12.1 %all-to-all-start = ((f32[128,1,896]{2,1,0:T(1,128)}), f32[128,1,896]{2,1,0:T(1,128)S(1)}, u32[]{:S(2)}, u32[]{:S(2)}) async-start(f32[128,1,896]{2,1,0:T(1,128)} %get-tuple-element.15), calls=%async_computation | async-start | bytes 917504 | tf_op jit(solution)/shard_map/all_to_all | solution.py:462
  19.6 0.0 copy-start
  19.6 0.0 copy-start.1
  19.6 0.0 copy-start.7
  19.6 10.5 %gradient_pass.1 = (f32[4,24,128]{2,1,0:T(8,128)}, f32[4,24,128]{2,1,0:T(8,128)}, f32[4,24,128]{2,1,0:T(8,128)}, f32[4,24,128]{2,1,0:T(8,128)}, bf16[384,2048]{1,0:T(8,128)(2,1)}) custom-call(s32[1]{0:T(128)} %bitcast.band_ref, f32[1,128]{1,0:T(1,128)} %bitcast.17, bf16[343,512]{1,0:T(8,128)(2,1)} %bitcast.15, bf16[3,343,512]{2,1,0:T(8,128)(2,1)} %bitcast.13, ...), custom_call_target="tpu_custom_call" | custom-call | flops 6442450944 | bytes 8388608 | tf_op jit(solution)/shard_map/gradient_pass/pallas_call | solution.py:233
  30.1 1.6 %collective-permute-start = (f32[4,24,128]{2,1,0:T(8,128)}, f32[4,24,128]{2,1,0:T(8,128)S(1)}, u32[]{:S(2)}, u32[]{:S(2)}) collective-permute-start(f32[4,24,128]{2,1,0:T(8,128)} %get-tuple-element.18), channel_id=1, source_target_pairs={{0,64},{64,128},{128,192},{192,0},{1,65},{65,129},{129,193},{193,1... | collective-permute-start | bytes 147464 | tf_op jit(solution)/shard_map/ppermute | solution.py:447
  31.7 2.7 %collective-permute-start.1 = (f32[4,24,128]{2,1,0:T(8,128)}, f32[4,24,128]{2,1,0:T(8,128)S(1)}, u32[]{:S(2)}, u32[]{:S(2)}) collective-permute-start(f32[4,24,128]{2,1,0:T(8,128)} %get-tuple-element.19), channel_id=1, source_target_pairs={{0,128},{64,192},{128,0},{192,64},{1,129},{65,193},{129,1},{193,65... | collective-permute-start | bytes 147464 | tf_op jit(solution)/shard_map/ppermute | solution.py:447
  34.4 1.4 %collective-permute-start.2 = (f32[4,24,128]{2,1,0:T(8,128)}, f32[4,24,128]{2,1,0:T(8,128)S(1)}, u32[]{:S(2)}, u32[]{:S(2)}) collective-permute-start(f32[4,24,128]{2,1,0:T(8,128)} %get-tuple-element.20), channel_id=1, source_target_pairs={{0,192},{64,0},{128,64},{192,128},{1,193},{65,1},{129,65},{193,129... | collective-permute-start | bytes 147464 | tf_op jit(solution)/shard_map/ppermute | solution.py:447
  35.8 0.0 collective-permute-done.b_ref
  35.8 1.6 %collective-permute-done.1.c_ref = f32[4,24,128]{2,1,0:T(8,128)S(1)} collective-permute-done((f32[4,24,128]{2,1,0:T(8,128)}, f32[4,24,128]{2,1,0:T(8,128)S(1)}, u32[]{:S(2)}, u32[]{:S(2)}) %collective-permute-start.1) | collective-permute-done | bytes 49184 | tf_op jit(solution)/shard_map/ppermute | solution.py:447
  37.5 1.2 %collective-permute-done.2.d_ref = f32[4,24,128]{2,1,0:T(8,128)S(1)} collective-permute-done((f32[4,24,128]{2,1,0:T(8,128)}, f32[4,24,128]{2,1,0:T(8,128)S(1)}, u32[]{:S(2)}, u32[]{:S(2)}) %collective-permute-start.2) | collective-permute-done | bytes 49184 | tf_op jit(solution)/shard_map/ppermute | solution.py:447
  38.7 0.0 copy-start.4
  38.8 0.8 %copy-done.4 = f32[4,24,128]{2,1,0:T(8,128)S(1)} copy-done((f32[4,24,128]{2,1,0:T(8,128)S(1)}, f32[4,24,128]{2,1,0:T(8,128)}, u32[]{:S(2)}) %copy-start.4) | copy-done | bytes 49176
  39.5 0.7 %exchange.1.m0_ref = f32[288,128]{1,0:T(8,128)S(1)} custom-call(s32[24]{0:T(128)S(1)} %copy-done.5, s32[48]{0:T(128)S(1)} %copy-done.6, f32[128,1,896]{2,1,0:T(1,128)S(1)} %all-to-all-done.came_ref, f32[4,24,128]{2,1,0:T(8,128)S(1)} %copy-done.4, f32[4,24,128]{2,1,0:T(8,128)S(1)} %collective-permute-done.b_ref, ...), custom_call_target="tpu_custom_call" | custom-call | flops 1000000 | bytes 1048576 | tf_op jit(solution)/shard_map/exchange/pallas_call | solution.py:290
  40.3 2.7 %collective-permute-start.5 = (f32[288,128]{1,0:T(8,128)S(1)}, f32[288,128]{1,0:T(8,128)S(1)}, u32[]{:S(2)}, u32[]{:S(2)}) collective-permute-start(f32[288,128]{1,0:T(8,128)S(1)} %exchange.1.m0_ref), channel_id=1, source_target_pairs={{0,192},{64,0},{128,64},{192,128},{1,193},{65,1},{129,65},{193,129... | collective-permute-start | bytes 442376 | tf_op jit(solution)/shard_map/ppermute | solution.py:447
  43.0 1.0 %collective-permute-start.3 = (f32[288,128]{1,0:T(8,128)S(1)}, f32[288,128]{1,0:T(8,128)S(1)}, u32[]{:S(2)}, u32[]{:S(2)}) collective-permute-start(f32[288,128]{1,0:T(8,128)S(1)} %exchange.1.m0_ref), channel_id=1, source_target_pairs={{0,64},{64,128},{128,192},{192,0},{1,65},{65,129},{129,193},{193,1... | collective-permute-start | bytes 442376 | tf_op jit(solution)/shard_map/ppermute | solution.py:447
  44.0 2.0 %stiff_part.1.stiff_hbm = f32[48,729]{1,0:T(8,128)S(1)} custom-call(f32[48,729]{1,0:T(8,128)S(1)} %bitcast.9, f32[729,729]{1,0:T(8,128)S(1)} %copy-done, f32[1,48]{1,0:T(1,128)S(1)} %bitcast.10), custom_call_target="tpu_custom_call" | custom-call | flops 306110016 | bytes 3145728 | tf_op jit(solution)/shard_map/stiff_part/pallas_call | solution.py:435
  46.0 0.6 copy-done.2
  46.6 1.3 %collective-permute-done.5.m3_ref = f32[288,128]{1,0:T(8,128)S(1)} collective-permute-done((f32[288,128]{1,0:T(8,128)S(1)}, f32[288,128]{1,0:T(8,128)S(1)}, u32[]{:S(2)}, u32[]{:S(2)}) %collective-permute-start.5) | collective-permute-done | bytes 147488 | tf_op jit(solution)/shard_map/ppermute | solution.py:447
  47.9 2.2 %collective-permute-done.4.m2_ref = f32[288,128]{1,0:T(8,128)S(1)} collective-permute-done((f32[288,128]{1,0:T(8,128)S(1)}, f32[288,128]{1,0:T(8,128)S(1)}, u32[]{:S(2)}, u32[]{:S(2)}) %collective-permute-start.4) | collective-permute-done | bytes 147488 | tf_op jit(solution)/shard_map/ppermute | solution.py:447
  50.1 1.1 %collective-permute-done.3.m1_ref = f32[288,128]{1,0:T(8,128)S(1)} collective-permute-done((f32[288,128]{1,0:T(8,128)S(1)}, f32[288,128]{1,0:T(8,128)S(1)}, u32[]{:S(2)}, u32[]{:S(2)}) %collective-permute-start.3) | collective-permute-done | bytes 147488 | tf_op jit(solution)/shard_map/ppermute | solution.py:447
  51.3 0.6 copy-done.10
  51.9 19.0 %second_pass.1 = (bf16[343,24,128]{2,1,0:T(8,128)(2,1)}, f32[48,729]{1,0:T(8,128)}) custom-call(s32[1]{0:T(128)} %bitcast.band_ref, f32[288,128]{1,0:T(8,128)} %copy-done.3, f32[288,128]{1,0:T(8,128)} %copy-done.10, f32[288,128]{1,0:T(8,128)} %copy-done.9, f32[288,128]{1,0:T(8,128)} %copy-done.8, bf16[384,2048]{1,0:T(8,128)(2,1)} %get-tuple-element.21.table_hbm, ...), custom_call_target="tpu_custom_call" | custom-call | flops 12884901888 | bytes 8388608 | tf_op jit(solution)/shard_map/second_pass/pallas_call | solution.py:394
  (17 shorter events, 0.0 us)
Async XLA Ops:
  7.4 31.3 %all-to-all-start = ((f32[128,1,896]{2,1,0:T(1,128)}), f32[128,1,896]{2,1,0:T(1,128)S(1)}, u32[]{:S(2)}, u32[]{:S(2)}) async-start(f32[128,1,896]{2,1,0:T(1,128)} %get-tuple-element.15), calls=%async_computation | async-start | bytes 917504 | tf_op jit(solution)/shard_map/all_to_all | solution.py:462
  19.5 19.2 %copy-start.5 = (s32[24]{0:T(128)S(1)}, s32[24]{0:T(128)}, u32[]{:S(2)}) copy-start(s32[24]{0:T(128)} %get-tuple-element.13.wave_row_ref) | copy-start | bytes 292
  19.6 19.2 %copy-start.6 = (s32[48]{0:T(128)S(1)}, s32[48]{0:T(128)}, u32[]{:S(2)}) copy-start(s32[48]{0:T(128)} %get-tuple-element.14.slot_row_ref) | copy-start | bytes 580
  19.6 24.4 %copy-start = (f32[729,729]{1,0:T(8,128)S(1)}, f32[729,729]{1,0:T(8,128)}, u32[]{:S(2)}) copy-start(f32[729,729]{1,0:T(8,128)} %stiff_ref.1) | copy-start | bytes 6377296
  19.6 24.4 %copy-start.1 = (f32[729,48]{0,1:T(8,128)S(1)}, f32[729,48]{0,1:T(8,128)}, u32[]{:S(2)}) copy-start(f32[729,48]{0,1:T(8,128)} %param.18) | copy-start | bytes 419908
  19.6 24.4 %copy-start.7 = (f32[48]{0:T(128)S(1)}, f32[48]{0:T(128)}, u32[]{:S(2)}) copy-start(f32[48]{0:T(128)} %param.20) | copy-start | bytes 580
  30.1 5.7 %collective-permute-start = (f32[4,24,128]{2,1,0:T(8,128)}, f32[4,24,128]{2,1,0:T(8,128)S(1)}, u32[]{:S(2)}, u32[]{:S(2)}) collective-permute-start(f32[4,24,128]{2,1,0:T(8,128)} %get-tuple-element.18), channel_id=1, source_target_pairs={{0,64},{64,128},{128,192},{192,0},{1,65},{65,129},{129,193},{193,1... | collective-permute-start | bytes 147464 | tf_op jit(solution)/shard_map/ppermute | solution.py:447
  31.7 5.8 %collective-permute-start.1 = (f32[4,24,128]{2,1,0:T(8,128)}, f32[4,24,128]{2,1,0:T(8,128)S(1)}, u32[]{:S(2)}, u32[]{:S(2)}) collective-permute-start(f32[4,24,128]{2,1,0:T(8,128)} %get-tuple-element.19), channel_id=1, source_target_pairs={{0,128},{64,192},{128,0},{192,64},{1,129},{65,193},{129,1},{193,65... | collective-permute-start | bytes 147464 | tf_op jit(solution)/shard_map/ppermute | solution.py:447
  34.4 4.3 %collective-permute-start.2 = (f32[4,24,128]{2,1,0:T(8,128)}, f32[4,24,128]{2,1,0:T(8,128)S(1)}, u32[]{:S(2)}, u32[]{:S(2)}) collective-permute-start(f32[4,24,128]{2,1,0:T(8,128)} %get-tuple-element.20), channel_id=1, source_target_pairs={{0,192},{64,0},{128,64},{192,128},{1,193},{65,1},{129,65},{193,129... | collective-permute-start | bytes 147464 | tf_op jit(solution)/shard_map/ppermute | solution.py:447
  38.7 0.8 %copy-start.4 = (f32[4,24,128]{2,1,0:T(8,128)S(1)}, f32[4,24,128]{2,1,0:T(8,128)}, u32[]{:S(2)}) copy-start(f32[4,24,128]{2,1,0:T(8,128)} %get-tuple-element.17.a_ref) | copy-start | bytes 147460
  40.3 11.0 %copy-start.3 = (f32[288,128]{1,0:T(8,128)}, f32[288,128]{1,0:T(8,128)S(1)}, u32[]{:S(2)}) copy-start(f32[288,128]{1,0:T(8,128)S(1)} %exchange.1.m0_ref) | copy-start | bytes 442372
  40.3 7.6 %collective-permute-start.5 = (f32[288,128]{1,0:T(8,128)S(1)}, f32[288,128]{1,0:T(8,128)S(1)}, u32[]{:S(2)}, u32[]{:S(2)}) collective-permute-start(f32[288,128]{1,0:T(8,128)S(1)} %exchange.1.m0_ref), channel_id=1, source_target_pairs={{0,192},{64,0},{128,64},{192,128},{1,193},{65,1},{129,65},{193,129... | collective-permute-start | bytes 442376 | tf_op jit(solution)/shard_map/ppermute | solution.py:447
  43.0 7.1 %collective-permute-start.4 = (f32[288,128]{1,0:T(8,128)S(1)}, f32[288,128]{1,0:T(8,128)S(1)}, u32[]{:S(2)}, u32[]{:S(2)}) collective-permute-start(f32[288,128]{1,0:T(8,128)S(1)} %exchange.1.m0_ref), channel_id=1, source_target_pairs={{0,128},{64,192},{128,0},{192,64},{1,129},{65,193},{129,1},{193,65... | collective-permute-start | bytes 442376 | tf_op jit(solution)/shard_map/ppermute | solution.py:447
  43.0 8.3 %collective-permute-start.3 = (f32[288,128]{1,0:T(8,128)S(1)}, f32[288,128]{1,0:T(8,128)S(1)}, u32[]{:S(2)}, u32[]{:S(2)}) collective-permute-start(f32[288,128]{1,0:T(8,128)S(1)} %exchange.1.m0_ref), channel_id=1, source_target_pairs={{0,64},{64,128},{128,192},{192,0},{1,65},{65,129},{129,193},{193,1... | collective-permute-start | bytes 442376 | tf_op jit(solution)/shard_map/ppermute | solution.py:447
  46.0 0.7 copy-start.2
  47.9 3.4 %copy-start.8 = (f32[288,128]{1,0:T(8,128)}, f32[288,128]{1,0:T(8,128)S(1)}, u32[]{:S(2)}) copy-start(f32[288,128]{1,0:T(8,128)S(1)} %collective-permute-done.5.m3_ref) | copy-start | bytes 442372
  50.1 1.2 %copy-start.9 = (f32[288,128]{1,0:T(8,128)}, f32[288,128]{1,0:T(8,128)S(1)}, u32[]{:S(2)}) copy-start(f32[288,128]{1,0:T(8,128)S(1)} %collective-permute-done.4.m2_ref) | copy-start | bytes 442372
  51.3 0.7 copy-start.10

commit v3 on v2

--- a/solution.py
+++ b/solution.py
@@ -19,7 +19,7 @@
 WIDTH = FIELDS + POINTS
 TERMS = 4 * CELLS
 MIX = TERMS + RANKS * SLOTS
-HIGHEST = lax.Precision.HIGHEST
+EXACT = lax.Precision.HIGH
 NT = (((1,), (1,)), ((), ()))
 MIB = 1 << 20
 
@@ -102,7 +102,7 @@
         load.wait()
     table_ref[:NODES, :] = val_ref[...]
     field_ref[:, lanes(2)] = jnp.dot(
-        nodes_ref[...], shape_ref[...], precision=HIGHEST, preferred_element_type=F32
+        nodes_ref[...], shape_ref[...], precision=EXACT, preferred_element_type=F32
     )
     for s in range(SLOTS):
         send_ref[slot_row_ref[s], :, :FIELDS] = field_ref[s : s + 1, :]
@@ -176,8 +176,8 @@
 
 def gradient_kernel(
     band_ref, occ_ref, val_hbm, grad_hbm, node_hbm,
-    part0_ref, part1_ref, part2_ref, part3_ref, table_hbm,
-    val_ref, grad_ref, node_ref, table_ref, spread_ref, slab_ref, sum_ref, in_sem, node_sem, out_sem,
+    part0_ref, part1_ref, part2_ref, part3_ref,
+    table_ref, node_ref, spread_ref, slab_ref, sum_ref, table_sem, node_sem,
 ):
     groups = CELLS // GROUP
 
@@ -185,34 +185,28 @@
         rows = pl.ds(g * GROUP * BANDS, GROUP * BANDS)
         return pltpu.make_async_copy(node_hbm.at[rows], node_ref.at[rows], node_sem.at[g])
 
-    loads = [
-        pltpu.make_async_copy(val_hbm, val_ref, in_sem.at[0]),
-        pltpu.make_async_copy(grad_hbm, grad_ref, in_sem.at[1]),
-    ]
-    for load in loads:
-        load.start()
-    for g in range(groups):
+    tables = [pltpu.make_async_copy(val_hbm, table_ref.at[0], table_sem.at[0])]
+    for k in range(3):
+        tables.append(pltpu.make_async_copy(grad_hbm.at[k], table_ref.at[k + 1], table_sem.at[k + 1]))
+    tables[0].start()
+    take(0).start()
+    for k in range(1, 4):
+        tables[k].start()
+    for g in range(1, groups):
         take(g).start()
     spread_ref[...] = jnp.broadcast_to(occ_ref[...], (BANDS, BANDS)).T
-    table_ref[NODES - 7 :, :] = jnp.zeros((KPAD - NODES + 7, 4 * POINTS), BF16)
-    loads[0].wait()
-    table_ref[:NODES, :POINTS] = val_ref[...]
-    loads[1].wait()
-    for k in range(3):
-        table_ref[:NODES, (k + 1) * POINTS : (k + 2) * POINTS] = grad_ref[k]
-    leave = pltpu.make_async_copy(table_ref, table_hbm, out_sem)
-    leave.start()
+    take(0).wait()
 
     for g in range(groups):
         slab = slab_ref.at[g % 2]
         rows = slice(g * GROUP * BANDS, (g + 1) * GROUP * BANDS)
-        if g < 2:
-            for later in range(g, groups if g else 1):
+        if g == 1:
+            for later in range(1, groups):
                 take(later).wait()
         for k in range(4):
-            slab[k] = jnp.dot(
-                node_ref[rows, :], table_ref[:, k * POINTS : (k + 1) * POINTS], preferred_element_type=F32
-            )
+            if g == 0:
+                tables[k].wait()
+            slab[k] = jnp.dot(node_ref[rows, :NODES], table_ref[k], preferred_element_type=F32)
         for i in range(GROUP):
             c = g * GROUP + i
             bands = slice(i * BANDS, (i + 1) * BANDS)
@@ -225,27 +219,23 @@
                     sum_ref[q, k, c : c + 1, :] = 2.0 * jnp.sum(scaled * term, axis=0, keepdims=True)
     for d, part_ref in enumerate((part0_ref, part1_ref, part2_ref, part3_ref)):
         part_ref[...] = sum_ref[(band_ref[0] + d) & (RANKS - 1)]
-    leave.wait()
 
 
 def gradient_pass(band, occupancy, values, grads, cell_nodes):
     part = jax.ShapeDtypeStruct((4, CELLS, PART), F32)
     return pl.pallas_call(
         gradient_kernel,
-        out_shape=(part, part, part, part, jax.ShapeDtypeStruct((KPAD, 4 * POINTS), BF16)),
+        out_shape=(part, part, part, part),
         in_specs=[SM, VM] + [HB] * 3,
-        out_specs=(VM, VM, VM, VM, HB),
+        out_specs=(VM, VM, VM, VM),
         scratch_shapes=[
-            pltpu.VMEM((NODES, POINTS), BF16),
-            pltpu.VMEM((3, NODES, POINTS), BF16),
+            pltpu.VMEM((4, NODES, POINTS), BF16),
             pltpu.VMEM((CELLS * BANDS, KPAD), BF16),
-            pltpu.VMEM((KPAD, 4 * POINTS), BF16),
             pltpu.VMEM((BANDS, BANDS), F32),
             pltpu.VMEM((2, 4, GROUP * BANDS, POINTS), F32),
             pltpu.VMEM((RANKS, 4, CELLS, PART), F32),
-            pltpu.SemaphoreType.DMA((2,)),
+            pltpu.SemaphoreType.DMA((4,)),
             pltpu.SemaphoreType.DMA((CELLS // GROUP,)),
-            pltpu.SemaphoreType.DMA,
         ],
         compiler_params=params(60),
         cost_estimate=cost(2 * 2048 * 512 * 3072, 8 * MIB),
@@ -265,71 +255,82 @@
     return d_density, d_square
 
 
-def exchange_kernel(wave_row_ref, slot_row_ref, came_ref, a_ref, b_ref, c_ref, d_ref, mix_ref, field_ref):
+def gather_kernel(wave_row_ref, slot_row_ref, came_ref, field_ref, dens_ref):
     for c in range(CELLS):
         row = wave_row_ref[c]
         for f in range(3):
-            field_ref[f, c : c + 1, :] = came_ref[row, :, lanes(f)]
+            place = f * CELLS + c
+            field_ref[place : place + 1, :] = came_ref[row, :, lanes(f)]
+    for s in range(SLOTS):
+        row = slot_row_ref[s]
+        source = jnp.minimum(row, ROWS - 1)
+        for q in range(RANKS):
+            value = came_ref[source, :, FIELDS + q * PART : FIELDS + (q + 1) * PART]
+            place = q * SLOTS + s
+            dens_ref[place : place + 1, :] = jnp.where(row < ROWS, value, 0.0)
+
+
+def gather(wave_rows, slot_rows, came):
+    return pl.pallas_call(
+        gather_kernel,
+        out_shape=(
+            jax.ShapeDtypeStruct((3 * CELLS, PART), F32),
+            jax.ShapeDtypeStruct((RANKS * SLOTS, PART), F32),
+        ),
+        in_specs=[SM, SM, VM],
+        out_specs=(VM, VM),
+        compiler_params=params(8),
+        cost_estimate=cost(1e6, MIB),
+        name="gather",
+    )(wave_rows, slot_rows, came)
+
+
+def exchange_kernel(field_ref, dens_ref, a_ref, b_ref, c_ref, d_ref, mix_ref):
     total = [(a_ref[k] + b_ref[k]) + (c_ref[k] + d_ref[k]) for k in range(4)]
-    core, weight, hartree = field_ref[0], field_ref[1], field_ref[2]
+    core, weight, hartree = [field_ref[f * CELLS : (f + 1) * CELLS, :] for f in range(3)]
     square = total[1] * total[1] + total[2] * total[2] + total[3] * total[3]
     d_density, d_square = exchange_terms(core + total[0], square)
     mix_ref[:CELLS, :] = weight * (d_density + hartree)
     for k in range(1, 4):
         mix_ref[k * CELLS : (k + 1) * CELLS, :] = 2.0 * weight * d_square * total[k]
-    for s in range(SLOTS):
-        row = slot_row_ref[s]
-        source = jnp.minimum(row, ROWS - 1)
-        for q in range(RANKS):
-            value = came_ref[source, :, FIELDS + q * PART : FIELDS + (q + 1) * PART]
-            place = TERMS + q * SLOTS + s
-            mix_ref[place : place + 1, :] = jnp.where(row < ROWS, value, 0.0)
-
-
-def exchange(wave_rows, slot_rows, came, parts):
+    mix_ref[TERMS:, :] = dens_ref[...]
+
+
+def exchange(field, dens, parts):
     return pl.pallas_call(
         exchange_kernel,
         out_shape=jax.ShapeDtypeStruct((MIX, PART), F32),
-        in_specs=[SM, SM] + [VM] * 5,
+        in_specs=[VM] * 6,
         out_specs=VM,
-        scratch_shapes=[pltpu.VMEM((3, CELLS, PART), F32)],
         compiler_params=params(8),
         cost_estimate=cost(1e6, MIB),
         name="exchange",
-    )(wave_rows, slot_rows, came, *parts)
+    )(field, dens, *parts)
 
 
 def second_kernel(
-    band_ref, m0_ref, m1_ref, m2_ref, m3_ref, table_hbm, node_hbm, core_hbm, weight_hbm, shape_hbm, stiff_hbm,
-    out_hbm, rest_hbm,
-    wt_ref, node_ref, table_ref, slab_ref, prod_ref, wide_ref, out_ref,
-    core_ref, weight_ref, shape_ref, stiff_ref, source_ref, in_sem, node_sem, out_sem, rest_sem,
+    band_ref, m0_ref, m1_ref, m2_ref, m3_ref, val_ref, grad_ref, node_ref,
+    core_ref, weight_ref, shape_ref, stiff_ref, val_hbm, grad_hbm,
+    out_hbm, rest_ref,
+    wt_ref, table_ref, slab_ref, prod_ref, wide_ref, out_ref, source_ref, table_sem, out_sem,
 ):
     groups = CELLS // GROUP
-
-    def take(g):
-        rows = pl.ds(g * GROUP * BANDS, GROUP * BANDS)
-        return pltpu.make_async_copy(node_hbm.at[rows], node_ref.at[rows], node_sem.at[g])
-
-    load = pltpu.make_async_copy(table_hbm, table_ref, in_sem)
-    load.start()
-    for g in range(groups):
-        take(g).start()
-    rests = [
-        pltpu.make_async_copy(core_hbm, core_ref, rest_sem.at[0]),
-        pltpu.make_async_copy(weight_hbm, weight_ref, rest_sem.at[1]),
-        pltpu.make_async_copy(shape_hbm, shape_ref, rest_sem.at[2]),
-        pltpu.make_async_copy(stiff_hbm, stiff_ref, rest_sem.at[3]),
-    ]
-    for rest in rests:
-        rest.start()
+    tables = [pltpu.make_async_copy(val_hbm, table_ref.at[:, :POINTS], table_sem.at[0])]
+    for k in range(3):
+        tables.append(
+            pltpu.make_async_copy(
+                grad_hbm.at[k], table_ref.at[:, (k + 1) * POINTS : (k + 2) * POINTS], table_sem.at[k + 1]
+            )
+        )
+    for table in tables:
+        table.start()
     for d, source in enumerate((m0_ref, m1_ref, m2_ref, m3_ref)):
         wt_ref[(band_ref[0] + RANKS - d) & (RANKS - 1)] = source[:TERMS, :]
 
     def evaluate(g, k):
         rows = slice(g * GROUP * BANDS, (g + 1) * GROUP * BANDS)
         slab_ref[g % 2, k] = jnp.dot(
-            node_ref[rows, :], table_ref[:, k * POINTS : (k + 1) * POINTS], preferred_element_type=F32
+            node_ref[rows, :NODES], grad_ref[k - 1] if k else val_ref[...], preferred_element_type=F32
         )
 
     def products(g, i):
@@ -346,18 +347,16 @@
     def multiply(g, pair):
         rows = slice(2 * pair * BANDS, 2 * (pair + 1) * BANDS)
         result = lax.dot_general(
-            table_ref[:NODES, :], prod_ref[g % 2, rows, :], NT, preferred_element_type=F32
+            table_ref[...], prod_ref[g % 2, rows, :], NT, preferred_element_type=F32
         )
         for i in range(2):
             c = g * GROUP + 2 * pair + i
             wide_ref[pl.ds(c, NODES, stride=CELLS), :] = result[:, i * BANDS : (i + 1) * BANDS]
 
-    load.wait()
-    take(0).wait()
     for k in range(4):
         evaluate(0, k)
-    for g in range(1, groups):
-        take(g).wait()
+    for table in tables:
+        table.wait()
     for g in range(groups):
         for i in range(GROUP):
             if g + 1 < groups:
@@ -375,56 +374,44 @@
         out_ref[pl.ds(i * STEP, STEP)] = part.astype(BF16)
         leave(i).start()
 
-    for rest in rests:
-        rest.wait()
     for q in range(RANKS):
         rows = slice(TERMS + q * SLOTS, TERMS + (q + 1) * SLOTS)
         dens = (m0_ref[rows, :] + m1_ref[rows, :]) + (m2_ref[rows, :] + m3_ref[rows, :])
         source_ref[:, lanes(q)] = weight_ref[:, lanes(q)] * (core_ref[:, lanes(q)] + dens)
-    drawn = lax.dot_general(source_ref[...], shape_ref[...], NT, precision=HIGHEST, preferred_element_type=F32)
-    stiff_ref[...] = stiff_ref[...] - drawn
-    last = pltpu.make_async_copy(stiff_ref, rest_hbm, rest_sem.at[4])
-    last.start()
+    drawn = lax.dot_general(source_ref[...], shape_ref[...], NT, precision=EXACT, preferred_element_type=F32)
+    rest_ref[...] = stiff_ref[...] - drawn
     for i in range(NODES // STEP):
         leave(i).wait()
-    last.wait()
-
-
-def second_pass(band, mixes, table, cell_nodes, core, weight, shape, stiff):
+
+
+def second_pass(band, mixes, values, grads, cell_nodes, core, weight, shape, stiff):
     return pl.pallas_call(
         second_kernel,
         out_shape=(
             jax.ShapeDtypeStruct((NODES, CELLS, BANDS), BF16),
             jax.ShapeDtypeStruct((SLOTS, ENODES), F32),
         ),
-        in_specs=[SM] + [VM] * 4 + [HB] * 6,
-        out_specs=(HB, HB),
+        in_specs=[SM] + [VM] * 11 + [HB] * 2,
+        out_specs=(HB, VM),
         scratch_shapes=[
             pltpu.VMEM((RANKS, TERMS, PART), F32),
-            pltpu.VMEM((CELLS * BANDS, KPAD), BF16),
-            pltpu.VMEM((KPAD, 4 * POINTS), BF16),
+            pltpu.VMEM((NODES, 4 * POINTS), BF16),
             pltpu.VMEM((2, 4, GROUP * BANDS, POINTS), F32),
             pltpu.VMEM((2, GROUP * BANDS, 4 * POINTS), BF16),
             pltpu.VMEM((NODES * CELLS, BANDS), F32),
             pltpu.VMEM((NODES, CELLS, BANDS), BF16),
             pltpu.VMEM((SLOTS, POINTS), F32),
-            pltpu.VMEM((SLOTS, POINTS), F32),
-            pltpu.VMEM((ENODES, POINTS), F32),
-            pltpu.VMEM((SLOTS, ENODES), F32),
-            pltpu.VMEM((SLOTS, POINTS), F32),
-            pltpu.SemaphoreType.DMA,
-            pltpu.SemaphoreType.DMA((CELLS // GROUP,)),
+            pltpu.SemaphoreType.DMA((4,)),
             pltpu.SemaphoreType.DMA((NODES // STEP,)),
-            pltpu.SemaphoreType.DMA((5,)),
         ],
-        compiler_params=params(60),
+        compiler_params=params(36),
         cost_estimate=cost(4 * 2048 * 512 * 3072, 8 * MIB),
         name="second_pass",
-    )(band, *mixes, table, cell_nodes, core, weight, shape, stiff)
+    )(band, *mixes, values, grads, cell_nodes, core, weight, shape, stiff, values, grads)
 
 
 def stiff_kernel(nodes_ref, stiff_ref, scale_ref, out_ref):
-    product = lax.dot_general(nodes_ref[...], stiff_ref[...], NT, precision=HIGHEST, preferred_element_type=F32)
+    product = lax.dot_general(nodes_ref[...], stiff_ref[...], NT, precision=EXACT, preferred_element_type=F32)
     spread = jnp.broadcast_to(scale_ref[...], (128, SLOTS)).T
     for j in range(0, ENODES, 128):
         width = min(128, ENODES - j)
@@ -460,12 +447,15 @@
         band, slot_cell, cell_slot, orbitals, occupancy, values, nodes, shape, core_density, quad_weight
     )
     came = lax.all_to_all(send, "dom", split_axis=0, concat_axis=0, tiled=True)
-    *parts, table = gradient_pass(band, occupancy, values, grads, cell_nodes)
+    parts = gradient_pass(band, occupancy, values, grads, cell_nodes)
     parts = [parts[0]] + [shift(parts[d], d) for d in (1, 2, 3)]
     stiff = stiff_part(nodes, stiffness, stiff_scale.reshape(1, SLOTS))
-    mix = exchange(wave_rows, slot_rows, came, parts)
+    field, dens = gather(wave_rows, slot_rows, came)
+    mix = exchange(field, dens, parts)
     mixes = [mix] + [shift(mix, d) for d in (1, 2, 3)]
-    action, rest = second_pass(band, mixes, table, cell_nodes, core_density, quad_weight, shape, stiff)
+    action, rest = second_pass(
+        band, mixes, values, grads, cell_nodes, core_density, quad_weight, shape, stiff
+    )
     return action, rest.T
 
 

time: 71.4 us -> 67.8 us (0.950)
  Pallas kernels: 39 us -> 33.9 us
  waiting for transfers between devices: 7.52 us -> 8.58 us
    pallas_call x1, Pallas kernels: 19 us -> 15.1 us  [second_pass(): pl.pallas_call(second_kernel, out_shape=(jax.ShapeDtypeStruct((NODES, CEL...]
    ppermute x6, waiting for transfers between devices: 7.52 us -> 8.57 us  [shift(): lax.ppermute(array, 'band', [(i, (i + distance) % RANKS) for i in range(R...]
    pallas_call x1, Pallas kernels: 2.02 us -> 1.09 us  [stiff_part(): pl.pallas_call(stiff_kernel, out_shape=jax.ShapeDtypeStruct((SLOTS, ENODE...]
    pallas_call x1 -> x2, Pallas kernels: 10.5 us -> 11 us  [the longest x1 10.3 us: gradient_pass(): pl.pallas_call(gradient_kernel, out_shape=(part, part, part, part), in_sp...]
    unnamed x22 -> x24, local copies, waits for them, and re-layouts: 2.13 us -> 2.51 us
where the time goes in v3:
time: 67.8 us; the launch traced here: 67.5 us
  Pallas kernels  33.9 us (50%)
  starting transfers between devices  21.5 us (32%)
  waiting for transfers between devices  8.58 us (13%)
  local copies, waits for them, and re-layouts  2.51 us (4%)
  between operations  0.96 us (1%)
    pallas_call x1, Pallas kernels, second_pass(): pl.pallas_call(second_kernel, out_shape=(jax.ShapeDtypeStruct((NODES, CEL...  15.1 us
    all_to_all x1, starting transfers between devices, body(): came = lax.all_to_all(send, 'dom', split_axis=0, concat_axis=0, tiled=True)  12.1 us
    pallas_call x1, Pallas kernels, gradient_pass(): pl.pallas_call(gradient_kernel, out_shape=(part, part, part, part), in_sp...  10.3 us
    ppermute x6, starting transfers between devices, shift(): lax.ppermute(array, 'band', [(i, (i + distance) % RANKS) for i in range(R...  9.41 us
    ppermute x6, waiting for transfers between devices, shift(): lax.ppermute(array, 'band', [(i, (i + distance) % RANKS) for i in range(R...  8.57 us
    pallas_call x1, Pallas kernels, first_pass(): pl.pallas_call(first_kernel, out_shape=(jax.ShapeDtypeStruct((ROWS, 1, WI...  6.6 us
    unnamed x24, local copies, waits for them, and re-layouts  2.51 us
  transfers between devices with their start and end apart: 7, of which 5 were waited for; matrix products, arithmetic and copies ran while one was open for 0% of the time, Pallas kernels for 18%

profile of v3, /device:TPU:8, one launch (start us, length us, event | category | flops | bytes accessed | tf_op | source)
XLA Modules:
  0.0 67.5 jit_solution(8181029231018881726)
XLA Ops:
  0.6 6.6 %first_pass.1 = (f32[128,1,896]{2,1,0:T(1,128)}, bf16[3072,384]{1,0:T(8,128)(2,1)}, s32[24]{0:T(128)}, s32[48]{0:T(128)}) custom-call(s32[1]{0:T(128)} %bitcast.band_ref, s32[48]{0:T(128)} %slot_cell_ref.1, s32[24]{0:T(128)} %cell_slot_ref.1, bf16[343,24,128]{2,1,0:T(8,128)(2,1)} %orb_hbm.1, f32[1,128]{1,0:T(1,128)} %bitcast.20, bf16[343,512]{1,0:T(8,128)(2,1)} %bitcast.16, ...), custom_call_target="tpu_custom_call" | custom-call | flops 1610612736 | bytes 8388608 | tf_op jit(solution)/shard_map/first_pass/pallas_call | solution.py:143
  7.2 12.1 %all-to-all-start = ((f32[128,1,896]{2,1,0:T(1,128)}), f32[128,1,896]{2,1,0:T(1,128)S(1)}, u32[]{:S(2)}, u32[]{:S(2)}) async-start(f32[128,1,896]{2,1,0:T(1,128)} %get-tuple-element.16), calls=%async_computation | async-start | bytes 917504 | tf_op jit(solution)/shard_map/all_to_all | solution.py:449
  19.4 0.0 copy-start
  19.4 0.0 copy-start.1
  19.4 0.0 copy-start.5
  19.4 10.3 %gradient_pass.1 = (f32[4,24,128]{2,1,0:T(8,128)}, f32[4,24,128]{2,1,0:T(8,128)}, f32[4,24,128]{2,1,0:T(8,128)}, f32[4,24,128]{2,1,0:T(8,128)}) custom-call(s32[1]{0:T(128)} %bitcast.band_ref, f32[1,128]{1,0:T(1,128)} %bitcast.21, bf16[343,512]{1,0:T(8,128)(2,1)} %bitcast.17, bf16[3,343,512]{2,1,0:T(8,128)(2,1)} %bitcast.13, ...), custom_call_target="tpu_custom_call" | custom-call | flops 6442450944 | bytes 8388608 | tf_op jit(solution)/shard_map/gradient_pass/pallas_call | solution.py:226
  29.7 0.0 copy-start.8
  29.8 1.6 %collective-permute-start = (f32[4,24,128]{2,1,0:T(8,128)}, f32[4,24,128]{2,1,0:T(8,128)S(1)}, u32[]{:S(2)}, u32[]{:S(2)}) collective-permute-start(f32[4,24,128]{2,1,0:T(8,128)} %get-tuple-element.21), channel_id=1, source_target_pairs={{0,64},{64,128},{128,192},{192,0},{1,65},{65,129},{129,193},{193,1... | collective-permute-start | bytes 147464 | tf_op jit(solution)/shard_map/ppermute | solution.py:434
  31.4 2.7 %collective-permute-start.1 = (f32[4,24,128]{2,1,0:T(8,128)}, f32[4,24,128]{2,1,0:T(8,128)S(1)}, u32[]{:S(2)}, u32[]{:S(2)}) collective-permute-start(f32[4,24,128]{2,1,0:T(8,128)} %get-tuple-element.22), channel_id=1, source_target_pairs={{0,128},{64,192},{128,0},{192,64},{1,129},{65,193},{129,1},{193,65... | collective-permute-start | bytes 147464 | tf_op jit(solution)/shard_map/ppermute | solution.py:434
  34.1 1.4 %collective-permute-start.2 = (f32[4,24,128]{2,1,0:T(8,128)}, f32[4,24,128]{2,1,0:T(8,128)S(1)}, u32[]{:S(2)}, u32[]{:S(2)}) collective-permute-start(f32[4,24,128]{2,1,0:T(8,128)} %get-tuple-element.23), channel_id=1, source_target_pairs={{0,192},{64,0},{128,64},{192,128},{1,193},{65,1},{129,65},{193,129... | collective-permute-start | bytes 147464 | tf_op jit(solution)/shard_map/ppermute | solution.py:434
  35.5 0.0 all-to-all-done.came_ref
  35.5 0.7 %gather.1 = (f32[72,128]{1,0:T(8,128)S(1)}, f32[192,128]{1,0:T(8,128)S(1)}) custom-call(s32[24]{0:T(128)S(1)} %copy-done.3, s32[48]{0:T(128)S(1)} %copy-done.4, f32[128,1,896]{2,1,0:T(1,128)S(1)} %all-to-all-done.came_ref), custom_call_target="tpu_custom_call" | custom-call | flops 1000000 | bytes 1048576 | tf_op jit(solution)/shard_map/gather/pallas_call | solution.py:274
  36.3 0.9 %collective-permute-done.1.c_ref = f32[4,24,128]{2,1,0:T(8,128)S(1)} collective-permute-done((f32[4,24,128]{2,1,0:T(8,128)}, f32[4,24,128]{2,1,0:T(8,128)S(1)}, u32[]{:S(2)}, u32[]{:S(2)}) %collective-permute-start.1) | collective-permute-done | bytes 49184 | tf_op jit(solution)/shard_map/ppermute | solution.py:434
  37.2 1.2 %collective-permute-done.2.d_ref = f32[4,24,128]{2,1,0:T(8,128)S(1)} collective-permute-done((f32[4,24,128]{2,1,0:T(8,128)}, f32[4,24,128]{2,1,0:T(8,128)S(1)}, u32[]{:S(2)}, u32[]{:S(2)}) %collective-permute-start.2) | collective-permute-done | bytes 49184 | tf_op jit(solution)/shard_map/ppermute | solution.py:434
  38.4 0.8 %copy-done.2 = f32[4,24,128]{2,1,0:T(8,128)S(1)} copy-done((f32[4,24,128]{2,1,0:T(8,128)S(1)}, f32[4,24,128]{2,1,0:T(8,128)}, u32[]{:S(2)}) %copy-start.2) | copy-done | bytes 49176
  39.2 0.1 exchange.1.m0_ref
  39.2 2.7 %collective-permute-start.5 = (f32[288,128]{1,0:T(8,128)S(1)}, f32[288,128]{1,0:T(8,128)S(1)}, u32[]{:S(2)}, u32[]{:S(2)}) collective-permute-start(f32[288,128]{1,0:T(8,128)S(1)} %exchange.1.m0_ref), channel_id=1, source_target_pairs={{0,192},{64,0},{128,64},{192,128},{1,193},{65,1},{129,65},{193,129... | collective-permute-start | bytes 442376 | tf_op jit(solution)/shard_map/ppermute | solution.py:434
  42.0 1.0 %collective-permute-start.3 = (f32[288,128]{1,0:T(8,128)S(1)}, f32[288,128]{1,0:T(8,128)S(1)}, u32[]{:S(2)}, u32[]{:S(2)}) collective-permute-start(f32[288,128]{1,0:T(8,128)S(1)} %exchange.1.m0_ref), channel_id=1, source_target_pairs={{0,64},{64,128},{128,192},{192,0},{1,65},{65,129},{129,193},{193,1... | collective-permute-start | bytes 442376 | tf_op jit(solution)/shard_map/ppermute | solution.py:434
  42.9 1.1 %stiff_part.1.stiff_ref = f32[48,729]{1,0:T(8,128)S(1)} custom-call(f32[48,729]{1,0:T(8,128)S(1)} %bitcast.9, f32[729,729]{1,0:T(8,128)S(1)} %copy-done, f32[1,48]{1,0:T(1,128)S(1)} %bitcast.10), custom_call_target="tpu_custom_call" | custom-call | flops 306110016 | bytes 3145728 | tf_op jit(solution)/shard_map/stiff_part/pallas_call | solution.py:422
  44.0 2.8 %collective-permute-done.5.m3_ref = f32[288,128]{1,0:T(8,128)S(1)} collective-permute-done((f32[288,128]{1,0:T(8,128)S(1)}, f32[288,128]{1,0:T(8,128)S(1)}, u32[]{:S(2)}, u32[]{:S(2)}) %collective-permute-start.5) | collective-permute-done | bytes 147488 | tf_op jit(solution)/shard_map/ppermute | solution.py:434
  46.9 2.2 %collective-permute-done.4.m2_ref = f32[288,128]{1,0:T(8,128)S(1)} collective-permute-done((f32[288,128]{1,0:T(8,128)S(1)}, f32[288,128]{1,0:T(8,128)S(1)}, u32[]{:S(2)}, u32[]{:S(2)}) %collective-permute-start.4) | collective-permute-done | bytes 147488 | tf_op jit(solution)/shard_map/ppermute | solution.py:434
  49.1 1.4 %collective-permute-done.3.m1_ref = f32[288,128]{1,0:T(8,128)S(1)} collective-permute-done((f32[288,128]{1,0:T(8,128)S(1)}, f32[288,128]{1,0:T(8,128)S(1)}, u32[]{:S(2)}, u32[]{:S(2)}) %collective-permute-start.3) | collective-permute-done | bytes 147488 | tf_op jit(solution)/shard_map/ppermute | solution.py:434
  50.5 1.7 %copy-done.11 = bf16[3072,384]{1,0:T(8,128)(2,1)S(1)} copy-done((bf16[3072,384]{1,0:T(8,128)(2,1)S(1)}, bf16[3072,384]{1,0:T(8,128)(2,1)}, u32[]{:S(2)}) %copy-start.11) | copy-done | bytes 2359320
  52.2 15.1 %second_pass.1 = (bf16[343,24,128]{2,1,0:T(8,128)(2,1)}, f32[48,729]{1,0:T(8,128)}) custom-call(s32[1]{0:T(128)} %bitcast.band_ref, f32[288,128]{1,0:T(8,128)S(1)} %exchange.1.m0_ref, f32[288,128]{1,0:T(8,128)S(1)} %collective-permute-done.3.m1_ref, f32[288,128]{1,0:T(8,128)S(1)} %collective-permute-done.4.m2_ref, ...), custom_call_target="tpu_custom_call" | custom-call | flops 12884901888 | bytes 8388608 | tf_op jit(solution)/shard_map/second_pass/pallas_call | solution.py:388
  (20 shorter events, 0.0 us)
Async XLA Ops:
  7.2 28.3 %all-to-all-start = ((f32[128,1,896]{2,1,0:T(1,128)}), f32[128,1,896]{2,1,0:T(1,128)S(1)}, u32[]{:S(2)}, u32[]{:S(2)}) async-start(f32[128,1,896]{2,1,0:T(1,128)} %get-tuple-element.16), calls=%async_computation | async-start | bytes 917504 | tf_op jit(solution)/shard_map/all_to_all | solution.py:449
  19.4 16.2 %copy-start.3 = (s32[24]{0:T(128)S(1)}, s32[24]{0:T(128)}, u32[]{:S(2)}) copy-start(s32[24]{0:T(128)} %get-tuple-element.14.wave_row_ref) | copy-start | bytes 292
  19.4 16.1 %copy-start.4 = (s32[48]{0:T(128)S(1)}, s32[48]{0:T(128)}, u32[]{:S(2)}) copy-start(s32[48]{0:T(128)} %get-tuple-element.15.slot_row_ref) | copy-start | bytes 580
  19.4 23.5 %copy-start = (f32[729,729]{1,0:T(8,128)S(1)}, f32[729,729]{1,0:T(8,128)}, u32[]{:S(2)}) copy-start(f32[729,729]{1,0:T(8,128)} %stiff_ref.1) | copy-start | bytes 6377296
  19.4 23.5 %copy-start.1 = (f32[729,48]{0,1:T(8,128)S(1)}, f32[729,48]{0,1:T(8,128)}, u32[]{:S(2)}) copy-start(f32[729,48]{0,1:T(8,128)} %param.18) | copy-start | bytes 419908
  19.4 23.5 %copy-start.5 = (f32[48]{0:T(128)S(1)}, f32[48]{0:T(128)}, u32[]{:S(2)}) copy-start(f32[48]{0:T(128)} %param.20) | copy-start | bytes 580
  29.7 20.7 %copy-start.8 = (bf16[512,343]{0,1:T(8,128)(2,1)S(1)}, bf16[512,343]{0,1:T(8,128)(2,1)}, u32[]{:S(2)}) copy-start(bf16[512,343]{0,1:T(8,128)(2,1)} %param.14) | copy-start | bytes 1053700
  29.8 20.7 %copy-start.9 = (f32[48,512]{1,0:T(8,128)S(1)}, f32[48,512]{1,0:T(8,128)}, u32[]{:S(2)}) copy-start(f32[48,512]{1,0:T(8,128)} %core_ref.1) | copy-start | bytes 294916
  29.8 6.5 %collective-permute-start = (f32[4,24,128]{2,1,0:T(8,128)}, f32[4,24,128]{2,1,0:T(8,128)S(1)}, u32[]{:S(2)}, u32[]{:S(2)}) collective-permute-start(f32[4,24,128]{2,1,0:T(8,128)} %get-tuple-element.21), channel_id=1, source_target_pairs={{0,64},{64,128},{128,192},{192,0},{1,65},{65,129},{129,193},{193,1... | collective-permute-start | bytes 147464 | tf_op jit(solution)/shard_map/ppermute | solution.py:434
  31.4 5.8 %collective-permute-start.1 = (f32[4,24,128]{2,1,0:T(8,128)}, f32[4,24,128]{2,1,0:T(8,128)S(1)}, u32[]{:S(2)}, u32[]{:S(2)}) collective-permute-start(f32[4,24,128]{2,1,0:T(8,128)} %get-tuple-element.22), channel_id=1, source_target_pairs={{0,128},{64,192},{128,0},{192,64},{1,129},{65,193},{129,1},{193,65... | collective-permute-start | bytes 147464 | tf_op jit(solution)/shard_map/ppermute | solution.py:434
  34.1 4.3 %collective-permute-start.2 = (f32[4,24,128]{2,1,0:T(8,128)}, f32[4,24,128]{2,1,0:T(8,128)S(1)}, u32[]{:S(2)}, u32[]{:S(2)}) collective-permute-start(f32[4,24,128]{2,1,0:T(8,128)} %get-tuple-element.23), channel_id=1, source_target_pairs={{0,192},{64,0},{128,64},{192,128},{1,193},{65,1},{129,65},{193,129... | collective-permute-start | bytes 147464 | tf_op jit(solution)/shard_map/ppermute | solution.py:434
  38.4 0.8 %copy-start.2 = (f32[4,24,128]{2,1,0:T(8,128)S(1)}, f32[4,24,128]{2,1,0:T(8,128)}, u32[]{:S(2)}) copy-start(f32[4,24,128]{2,1,0:T(8,128)} %get-tuple-element.20.a_ref) | copy-start | bytes 147460
  39.2 11.3 %copy-start.6 = (f32[512,729]{0,1:T(8,128)S(1)}, f32[512,729]{0,1:T(8,128)}, u32[]{:S(2)}) copy-start(f32[512,729]{0,1:T(8,128)} %param.21) | copy-start | bytes 4478980
  39.2 11.3 %copy-start.7 = (bf16[3,512,343]{1,2,0:T(8,128)(2,1)S(1)}, bf16[3,512,343]{1,2,0:T(8,128)(2,1)}, u32[]{:S(2)}) copy-start(bf16[3,512,343]{1,2,0:T(8,128)(2,1)} %param.15) | copy-start | bytes 3161092
  39.2 11.3 %copy-start.10 = (f32[48,512]{1,0:T(8,128)S(1)}, f32[48,512]{1,0:T(8,128)}, u32[]{:S(2)}) copy-start(f32[48,512]{1,0:T(8,128)} %weight_ref.1) | copy-start | bytes 294916
  39.2 7.6 %collective-permute-start.5 = (f32[288,128]{1,0:T(8,128)S(1)}, f32[288,128]{1,0:T(8,128)S(1)}, u32[]{:S(2)}, u32[]{:S(2)}) collective-permute-start(f32[288,128]{1,0:T(8,128)S(1)} %exchange.1.m0_ref), channel_id=1, source_target_pairs={{0,192},{64,0},{128,64},{192,128},{1,193},{65,1},{129,65},{193,129... | collective-permute-start | bytes 442376 | tf_op jit(solution)/shard_map/ppermute | solution.py:434
  42.0 7.1 %collective-permute-start.4 = (f32[288,128]{1,0:T(8,128)S(1)}, f32[288,128]{1,0:T(8,128)S(1)}, u32[]{:S(2)}, u32[]{:S(2)}) collective-permute-start(f32[288,128]{1,0:T(8,128)S(1)} %exchange.1.m0_ref), channel_id=1, source_target_pairs={{0,128},{64,192},{128,0},{192,64},{1,129},{65,193},{129,1},{193,65... | collective-permute-start | bytes 442376 | tf_op jit(solution)/shard_map/ppermute | solution.py:434
  42.0 8.5 %collective-permute-start.3 = (f32[288,128]{1,0:T(8,128)S(1)}, f32[288,128]{1,0:T(8,128)S(1)}, u32[]{:S(2)}, u32[]{:S(2)}) collective-permute-start(f32[288,128]{1,0:T(8,128)S(1)} %exchange.1.m0_ref), channel_id=1, source_target_pairs={{0,64},{64,128},{128,192},{192,0},{1,65},{65,129},{129,193},{193,1... | collective-permute-start | bytes 442376 | tf_op jit(solution)/shard_map/ppermute | solution.py:434
  50.5 1.7 %copy-start.11 = (bf16[3072,384]{1,0:T(8,128)(2,1)S(1)}, bf16[3072,384]{1,0:T(8,128)(2,1)}, u32[]{:S(2)}) copy-start(bf16[3072,384]{1,0:T(8,128)(2,1)} %get-tuple-element.19.node_hbm.node_ref) | copy-start | bytes 7077892

commit v4 on v3

--- a/solution.py
+++ b/solution.py
@@ -17,8 +17,8 @@
 STEP = 49
 FIELDS = 3 * PART
 WIDTH = FIELDS + POINTS
-TERMS = 4 * CELLS
-MIX = TERMS + RANKS * SLOTS
+HELD = 3 * CELLS
+MIX = HELD + RANKS * SLOTS
 EXACT = lax.Precision.HIGH
 NT = (((1,), (1,)), ((), ()))
 MIB = 1 << 20
@@ -175,9 +175,8 @@
 
 
 def gradient_kernel(
-    band_ref, occ_ref, val_hbm, grad_hbm, node_hbm,
-    part0_ref, part1_ref, part2_ref, part3_ref,
-    table_ref, node_ref, spread_ref, slab_ref, sum_ref, table_sem, node_sem,
+    occ_ref, val_hbm, grad_hbm, node_hbm, part_ref,
+    table_ref, node_ref, spread_ref, slab_ref, table_sem, node_sem,
 ):
     groups = CELLS // GROUP
 
@@ -197,50 +196,78 @@
     spread_ref[...] = jnp.broadcast_to(occ_ref[...], (BANDS, BANDS)).T
     take(0).wait()
 
+    def evaluate(g, k):
+        rows = slice(g * GROUP * BANDS, (g + 1) * GROUP * BANDS)
+        slab_ref[g % 2, k] = jnp.dot(node_ref[rows, :NODES], table_ref[k], preferred_element_type=F32)
+
+    def reduce(g, i):
+        c = g * GROUP + i
+        bands = slice(i * BANDS, (i + 1) * BANDS)
+        for q in range(RANKS):
+            lead = slab_ref[g % 2, 0, bands, lanes(q)]
+            scaled = spread_ref[...] * lead
+            part_ref[0, c : c + 1, lanes(q)] = jnp.sum(scaled * lead, axis=0, keepdims=True)
+            for k in range(1, 4):
+                term = slab_ref[g % 2, k, bands, lanes(q)]
+                part_ref[k, c : c + 1, lanes(q)] = 2.0 * jnp.sum(scaled * term, axis=0, keepdims=True)
+
+    for k in range(4):
+        tables[k].wait()
+        evaluate(0, k)
+    for g in range(1, groups):
+        take(g).wait()
     for g in range(groups):
-        slab = slab_ref.at[g % 2]
-        rows = slice(g * GROUP * BANDS, (g + 1) * GROUP * BANDS)
-        if g == 1:
-            for later in range(1, groups):
-                take(later).wait()
-        for k in range(4):
-            if g == 0:
-                tables[k].wait()
-            slab[k] = jnp.dot(node_ref[rows, :NODES], table_ref[k], preferred_element_type=F32)
         for i in range(GROUP):
-            c = g * GROUP + i
-            bands = slice(i * BANDS, (i + 1) * BANDS)
-            for q in range(RANKS):
-                lead = slab[0, bands, lanes(q)]
-                scaled = spread_ref[...] * lead
-                sum_ref[q, 0, c : c + 1, :] = jnp.sum(scaled * lead, axis=0, keepdims=True)
-                for k in range(1, 4):
-                    term = slab[k, bands, lanes(q)]
-                    sum_ref[q, k, c : c + 1, :] = 2.0 * jnp.sum(scaled * term, axis=0, keepdims=True)
-    for d, part_ref in enumerate((part0_ref, part1_ref, part2_ref, part3_ref)):
-        part_ref[...] = sum_ref[(band_ref[0] + d) & (RANKS - 1)]
-
-
-def gradient_pass(band, occupancy, values, grads, cell_nodes):
-    part = jax.ShapeDtypeStruct((4, CELLS, PART), F32)
+            if g + 1 < groups:
+                evaluate(g + 1, i)
+            reduce(g, i)
+
+
+def gradient_pass(occupancy, values, grads, cell_nodes):
     return pl.pallas_call(
         gradient_kernel,
-        out_shape=(part, part, part, part),
-        in_specs=[SM, VM] + [HB] * 3,
-        out_specs=(VM, VM, VM, VM),
+        out_shape=jax.ShapeDtypeStruct((4, CELLS, POINTS), F32),
+        in_specs=[VM] + [HB] * 3,
+        out_specs=VM,
         scratch_shapes=[
             pltpu.VMEM((4, NODES, POINTS), BF16),
             pltpu.VMEM((CELLS * BANDS, KPAD), BF16),
             pltpu.VMEM((BANDS, BANDS), F32),
             pltpu.VMEM((2, 4, GROUP * BANDS, POINTS), F32),
-            pltpu.VMEM((RANKS, 4, CELLS, PART), F32),
             pltpu.SemaphoreType.DMA((4,)),
             pltpu.SemaphoreType.DMA((CELLS // GROUP,)),
         ],
         compiler_params=params(60),
         cost_estimate=cost(2 * 2048 * 512 * 3072, 8 * MIB),
         name="gradient_pass",
-    )(band, occupancy, values, grads, cell_nodes)
+    )(occupancy, values, grads, cell_nodes)
+
+
+def gather_kernel(wave_row_ref, slot_row_ref, came_ref, mix_ref):
+    for c in range(CELLS):
+        row = wave_row_ref[c]
+        for f in range(3):
+            place = f * CELLS + c
+            mix_ref[place : place + 1, :] = came_ref[row, :, lanes(f)]
+    for s in range(SLOTS):
+        row = slot_row_ref[s]
+        source = jnp.minimum(row, ROWS - 1)
+        for q in range(RANKS):
+            value = came_ref[source, :, FIELDS + q * PART : FIELDS + (q + 1) * PART]
+            place = HELD + q * SLOTS + s
+            mix_ref[place : place + 1, :] = jnp.where(row < ROWS, value, 0.0)
+
+
+def gather(wave_rows, slot_rows, came):
+    return pl.pallas_call(
+        gather_kernel,
+        out_shape=jax.ShapeDtypeStruct((MIX, PART), F32),
+        in_specs=[SM, SM, VM],
+        out_specs=VM,
+        compiler_params=params(8),
+        cost_estimate=cost(1e6, MIB),
+        name="gather",
+    )(wave_rows, slot_rows, came)
 
 
 def exchange_terms(density, square):
@@ -255,64 +282,11 @@
     return d_density, d_square
 
 
-def gather_kernel(wave_row_ref, slot_row_ref, came_ref, field_ref, dens_ref):
-    for c in range(CELLS):
-        row = wave_row_ref[c]
-        for f in range(3):
-            place = f * CELLS + c
-            field_ref[place : place + 1, :] = came_ref[row, :, lanes(f)]
-    for s in range(SLOTS):
-        row = slot_row_ref[s]
-        source = jnp.minimum(row, ROWS - 1)
-        for q in range(RANKS):
-            value = came_ref[source, :, FIELDS + q * PART : FIELDS + (q + 1) * PART]
-            place = q * SLOTS + s
-            dens_ref[place : place + 1, :] = jnp.where(row < ROWS, value, 0.0)
-
-
-def gather(wave_rows, slot_rows, came):
-    return pl.pallas_call(
-        gather_kernel,
-        out_shape=(
-            jax.ShapeDtypeStruct((3 * CELLS, PART), F32),
-            jax.ShapeDtypeStruct((RANKS * SLOTS, PART), F32),
-        ),
-        in_specs=[SM, SM, VM],
-        out_specs=(VM, VM),
-        compiler_params=params(8),
-        cost_estimate=cost(1e6, MIB),
-        name="gather",
-    )(wave_rows, slot_rows, came)
-
-
-def exchange_kernel(field_ref, dens_ref, a_ref, b_ref, c_ref, d_ref, mix_ref):
-    total = [(a_ref[k] + b_ref[k]) + (c_ref[k] + d_ref[k]) for k in range(4)]
-    core, weight, hartree = [field_ref[f * CELLS : (f + 1) * CELLS, :] for f in range(3)]
-    square = total[1] * total[1] + total[2] * total[2] + total[3] * total[3]
-    d_density, d_square = exchange_terms(core + total[0], square)
-    mix_ref[:CELLS, :] = weight * (d_density + hartree)
-    for k in range(1, 4):
-        mix_ref[k * CELLS : (k + 1) * CELLS, :] = 2.0 * weight * d_square * total[k]
-    mix_ref[TERMS:, :] = dens_ref[...]
-
-
-def exchange(field, dens, parts):
-    return pl.pallas_call(
-        exchange_kernel,
-        out_shape=jax.ShapeDtypeStruct((MIX, PART), F32),
-        in_specs=[VM] * 6,
-        out_specs=VM,
-        compiler_params=params(8),
-        cost_estimate=cost(1e6, MIB),
-        name="exchange",
-    )(field, dens, *parts)
-
-
 def second_kernel(
-    band_ref, m0_ref, m1_ref, m2_ref, m3_ref, val_ref, grad_ref, node_ref,
-    core_ref, weight_ref, shape_ref, stiff_ref, val_hbm, grad_hbm,
+    band_ref, m0_ref, m1_ref, m2_ref, m3_ref, a_ref, b_ref, c_ref, d_ref, val_ref, grad_ref,
+    core_ref, weight_ref, shape_ref, stiff_ref, node_hbm, val_hbm, grad_hbm,
     out_hbm, rest_ref,
-    wt_ref, table_ref, slab_ref, prod_ref, wide_ref, out_ref, source_ref, table_sem, out_sem,
+    field_ref, wt_ref, node_ref, table_ref, slab_ref, prod_ref, wide_ref, out_ref, source_ref, node_sem, table_sem, out_sem,
 ):
     groups = CELLS // GROUP
     tables = [pltpu.make_async_copy(val_hbm, table_ref.at[:, :POINTS], table_sem.at[0])]
@@ -322,10 +296,26 @@
                 grad_hbm.at[k], table_ref.at[:, (k + 1) * POINTS : (k + 2) * POINTS], table_sem.at[k + 1]
             )
         )
+
+    def take(g):
+        rows = pl.ds(g * GROUP * BANDS, GROUP * BANDS)
+        return pltpu.make_async_copy(node_hbm.at[rows], node_ref.at[rows], node_sem.at[g])
+
+    for g in range(groups):
+        take(g).start()
     for table in tables:
         table.start()
     for d, source in enumerate((m0_ref, m1_ref, m2_ref, m3_ref)):
-        wt_ref[(band_ref[0] + RANKS - d) & (RANKS - 1)] = source[:TERMS, :]
+        field_ref[(band_ref[0] + RANKS - d) & (RANKS - 1)] = source[:HELD, :]
+    for q in range(RANKS):
+        cols = lanes(q)
+        total = [(a_ref[k, :, cols] + b_ref[k, :, cols]) + (c_ref[k, :, cols] + d_ref[k, :, cols]) for k in range(4)]
+        core, weight, hartree = [field_ref[q, f * CELLS : (f + 1) * CELLS, :] for f in range(3)]
+        square = total[1] * total[1] + total[2] * total[2] + total[3] * total[3]
+        d_density, d_square = exchange_terms(core + total[0], square)
+        wt_ref[q, :CELLS, :] = weight * (d_density + hartree)
+        for k in range(1, 4):
+            wt_ref[q, k * CELLS : (k + 1) * CELLS, :] = 2.0 * weight * d_square * total[k]
 
     def evaluate(g, k):
         rows = slice(g * GROUP * BANDS, (g + 1) * GROUP * BANDS)
@@ -353,8 +343,11 @@
             c = g * GROUP + 2 * pair + i
             wide_ref[pl.ds(c, NODES, stride=CELLS), :] = result[:, i * BANDS : (i + 1) * BANDS]
 
+    take(0).wait()
     for k in range(4):
         evaluate(0, k)
+    for g in range(1, groups):
+        take(g).wait()
     for table in tables:
         table.wait()
     for g in range(groups):
@@ -375,7 +368,7 @@
         leave(i).start()
 
     for q in range(RANKS):
-        rows = slice(TERMS + q * SLOTS, TERMS + (q + 1) * SLOTS)
+        rows = slice(HELD + q * SLOTS, HELD + (q + 1) * SLOTS)
         dens = (m0_ref[rows, :] + m1_ref[rows, :]) + (m2_ref[rows, :] + m3_ref[rows, :])
         source_ref[:, lanes(q)] = weight_ref[:, lanes(q)] * (core_ref[:, lanes(q)] + dens)
     drawn = lax.dot_general(source_ref[...], shape_ref[...], NT, precision=EXACT, preferred_element_type=F32)
@@ -384,30 +377,33 @@
         leave(i).wait()
 
 
-def second_pass(band, mixes, values, grads, cell_nodes, core, weight, shape, stiff):
+def second_pass(band, mixes, parts, values, grads, cell_nodes, core, weight, shape, stiff):
     return pl.pallas_call(
         second_kernel,
         out_shape=(
             jax.ShapeDtypeStruct((NODES, CELLS, BANDS), BF16),
             jax.ShapeDtypeStruct((SLOTS, ENODES), F32),
         ),
-        in_specs=[SM] + [VM] * 11 + [HB] * 2,
+        in_specs=[SM] + [VM] * 14 + [HB] * 3,
         out_specs=(HB, VM),
         scratch_shapes=[
-            pltpu.VMEM((RANKS, TERMS, PART), F32),
+            pltpu.VMEM((RANKS, HELD, PART), F32),
+            pltpu.VMEM((RANKS, 4 * CELLS, PART), F32),
+            pltpu.VMEM((CELLS * BANDS, KPAD), BF16),
             pltpu.VMEM((NODES, 4 * POINTS), BF16),
             pltpu.VMEM((2, 4, GROUP * BANDS, POINTS), F32),
             pltpu.VMEM((2, GROUP * BANDS, 4 * POINTS), BF16),
             pltpu.VMEM((NODES * CELLS, BANDS), F32),
             pltpu.VMEM((NODES, CELLS, BANDS), BF16),
             pltpu.VMEM((SLOTS, POINTS), F32),
+            pltpu.SemaphoreType.DMA((CELLS // GROUP,)),
             pltpu.SemaphoreType.DMA((4,)),
             pltpu.SemaphoreType.DMA((NODES // STEP,)),
         ],
         compiler_params=params(36),
         cost_estimate=cost(4 * 2048 * 512 * 3072, 8 * MIB),
         name="second_pass",
-    )(band, *mixes, values, grads, cell_nodes, core, weight, shape, stiff, values, grads)
+    )(band, *mixes, *parts, values, grads, core, weight, shape, stiff, cell_nodes, values, grads)
 
 
 def stiff_kernel(nodes_ref, stiff_ref, scale_ref, out_ref):
@@ -447,14 +443,13 @@
         band, slot_cell, cell_slot, orbitals, occupancy, values, nodes, shape, core_density, quad_weight
     )
     came = lax.all_to_all(send, "dom", split_axis=0, concat_axis=0, tiled=True)
-    parts = gradient_pass(band, occupancy, values, grads, cell_nodes)
-    parts = [parts[0]] + [shift(parts[d], d) for d in (1, 2, 3)]
+    part = gradient_pass(occupancy, values, grads, cell_nodes)
+    parts = [part] + [shift(part, d) for d in (1, 2, 3)]
+    mix = gather(wave_rows, slot_rows, came)
+    mixes = [mix] + [shift(mix, d) for d in (1, 2, 3)]
     stiff = stiff_part(nodes, stiffness, stiff_scale.reshape(1, SLOTS))
-    field, dens = gather(wave_rows, slot_rows, came)
-    mix = exchange(field, dens, parts)
-    mixes = [mix] + [shift(mix, d) for d in (1, 2, 3)]
     action, rest = second_pass(
-        band, mixes, values, grads, cell_nodes, core_density, quad_weight, shape, stiff
+        band, mixes, parts, values, grads, cell_nodes, core_density, quad_weight, shape, stiff
     )
     return action, rest.T
 

time: 67.8 us -> 72 us (1.062)
  waiting for transfers between devices: 8.58 us -> 11.2 us
  Pallas kernels: 33.9 us -> 36.2 us
  starting transfers between devices: 21.5 us -> 20.3 us
    pallas_call x1, Pallas kernels: 15.1 us -> 17.2 us  [second_pass(): pl.pallas_call(second_kernel, out_shape=(jax.ShapeDtypeStruct((NODES, CEL...]
    ppermute x6, waiting for transfers between devices: 8.57 us -> 10.3 us  [shift(): lax.ppermute(array, 'band', [(i, (i + distance) % RANKS) for i in range(R...]
    ppermute x6, starting transfers between devices: 9.41 us -> 8.15 us  [shift(): lax.ppermute(array, 'band', [(i, (i + distance) % RANKS) for i in range(R...]
    all_to_all x1, waiting for transfers between devices: 0.01 us -> 0.96 us  [body(): came = lax.all_to_all(send, 'dom', split_axis=0, concat_axis=0, tiled=True)]
    pallas_call x3 -> x2, Pallas kernels: 11.1 us -> 11.3 us  [the longest x1 10.6 us: gradient_pass(): pl.pallas_call(gradient_kernel, out_shape=jax.ShapeDtypeStruct((4, CELLS,...]
  transfers between devices with their start and end apart: 7 -> 7, of which waited for: 5 -> 6; matrix products, arithmetic and copies ran while one was open for 0% -> 0% of each run, Pallas kernels for 18% -> 17%
where the time goes in v4:
time: 72 us; the launch traced here: 71.3 us
  Pallas kernels  36.2 us (50%)
  starting transfers between devices  20.3 us (28%)
  waiting for transfers between devices  11.2 us (16%)
  local copies, waits for them, and re-layouts  2.61 us (4%)
  between operations  0.97 us (1%)
    pallas_call x1, Pallas kernels, second_pass(): pl.pallas_call(second_kernel, out_shape=(jax.ShapeDtypeStruct((NODES, CEL...  17.2 us
    all_to_all x1, starting transfers between devices, body(): came = lax.all_to_all(send, 'dom', split_axis=0, concat_axis=0, tiled=True)  12.1 us
    pallas_call x1, Pallas kernels, gradient_pass(): pl.pallas_call(gradient_kernel, out_shape=jax.ShapeDtypeStruct((4, CELLS,...  10.6 us
    ppermute x6, waiting for transfers between devices, shift(): lax.ppermute(array, 'band', [(i, (i + distance) % RANKS) for i in range(R...  10.3 us
    ppermute x6, starting transfers between devices, shift(): lax.ppermute(array, 'band', [(i, (i + distance) % RANKS) for i in range(R...  8.15 us
    pallas_call x1, Pallas kernels, first_pass(): pl.pallas_call(first_kernel, out_shape=(jax.ShapeDtypeStruct((ROWS, 1, WI...  6.6 us
    unnamed x24, local copies, waits for them, and re-layouts  2.61 us
  transfers between devices with their start and end apart: 7, of which 6 were waited for; matrix products, arithmetic and copies ran while one was open for 0% of the time, Pallas kernels for 17%

profile of v4, /device:TPU:8, one launch (start us, length us, event | category | flops | bytes accessed | tf_op | source)
XLA Modules:
  0.0 71.3 jit_solution(9329542838885425698)
XLA Ops:
  0.6 6.6 %first_pass.1 = (f32[128,1,896]{2,1,0:T(1,128)}, bf16[3072,384]{1,0:T(8,128)(2,1)}, s32[24]{0:T(128)}, s32[48]{0:T(128)}) custom-call(s32[1]{0:T(128)} %bitcast.band_ref, s32[48]{0:T(128)} %slot_cell_ref.1, s32[24]{0:T(128)} %cell_slot_ref.1, bf16[343,24,128]{2,1,0:T(8,128)(2,1)} %orb_hbm.1, f32[1,128]{1,0:T(1,128)} %bitcast.20, bf16[343,512]{1,0:T(8,128)(2,1)} %bitcast.16, ...), custom_call_target="tpu_custom_call" | custom-call | flops 1610612736 | bytes 8388608 | tf_op jit(solution)/shard_map/first_pass/pallas_call | solution.py:143
  7.2 12.1 %all-to-all-start = ((f32[128,1,896]{2,1,0:T(1,128)}), f32[128,1,896]{2,1,0:T(1,128)S(1)}, u32[]{:S(2)}, u32[]{:S(2)}) async-start(f32[128,1,896]{2,1,0:T(1,128)} %get-tuple-element.10), calls=%async_computation | async-start | bytes 917504 | tf_op jit(solution)/shard_map/all_to_all | solution.py:445
  19.4 0.0 copy-start.2
  19.4 0.0 copy-start
  19.4 0.0 copy-start.1
  19.4 0.0 copy-start.9
  19.4 10.6 %gradient_pass.1.a_ref = f32[4,24,512]{2,1,0:T(8,128)} custom-call(f32[1,128]{1,0:T(1,128)} %bitcast.21, bf16[343,512]{1,0:T(8,128)(2,1)} %bitcast.17, bf16[3,343,512]{2,1,0:T(8,128)(2,1)} %bitcast.13, bf16[3072,384]{1,0:T(8,128)(2,1)} %get-tuple-element.11.node_hbm), custom_call_target="tpu_custom_call" | custom-call | flops 6442450944 | bytes 8388608 | tf_op jit(solution)/shard_map/gradient_pass/pallas_call | solution.py:227
  30.0 2.8 %collective-permute-start.5 = (f32[4,24,512]{2,1,0:T(8,128)}, f32[4,24,512]{2,1,0:T(8,128)}, u32[]{:S(2)}, u32[]{:S(2)}) collective-permute-start(f32[4,24,512]{2,1,0:T(8,128)} %gradient_pass.1.a_ref), channel_id=1, source_target_pairs={{0,192},{64,0},{128,64},{192,128},{1,193},{65,1},{129,65},{193,129... | collective-permute-start | bytes 589832 | tf_op jit(solution)/shard_map/ppermute | solution.py:430
  32.9 0.8 %collective-permute-start.4 = (f32[4,24,512]{2,1,0:T(8,128)}, f32[4,24,512]{2,1,0:T(8,128)}, u32[]{:S(2)}, u32[]{:S(2)}) collective-permute-start(f32[4,24,512]{2,1,0:T(8,128)} %gradient_pass.1.a_ref), channel_id=1, source_target_pairs={{0,128},{64,192},{128,0},{192,64},{1,129},{65,193},{129,1},{193,65... | collective-permute-start | bytes 589832 | tf_op jit(solution)/shard_map/ppermute | solution.py:430
  33.7 0.9 %collective-permute-start.3 = (f32[4,24,512]{2,1,0:T(8,128)}, f32[4,24,512]{2,1,0:T(8,128)}, u32[]{:S(2)}, u32[]{:S(2)}) collective-permute-start(f32[4,24,512]{2,1,0:T(8,128)} %gradient_pass.1.a_ref), channel_id=1, source_target_pairs={{0,64},{64,128},{128,192},{192,0},{1,65},{65,129},{129,193},{193,1... | collective-permute-start | bytes 589832 | tf_op jit(solution)/shard_map/ppermute | solution.py:430
  34.6 1.0 %all-to-all-done.came_ref = f32[128,1,896]{2,1,0:T(1,128)S(1)} async-done(((f32[128,1,896]{2,1,0:T(1,128)}), f32[128,1,896]{2,1,0:T(1,128)S(1)}, u32[]{:S(2)}, u32[]{:S(2)}) %all-to-all-start) | async-done | bytes 458784 | tf_op jit(solution)/shard_map/all_to_all | solution.py:445
  35.5 0.7 %gather.1.m0_ref = f32[264,128]{1,0:T(8,128)S(1)} custom-call(s32[24]{0:T(128)S(1)} %copy-done.2, s32[48]{0:T(128)S(1)} %copy-done.3, f32[128,1,896]{2,1,0:T(1,128)S(1)} %all-to-all-done.came_ref), custom_call_target="tpu_custom_call" | custom-call | flops 1000000 | bytes 1048576 | tf_op jit(solution)/shard_map/gather/pallas_call | solution.py:262
  36.3 2.8 %collective-permute-start.2 = (f32[264,128]{1,0:T(8,128)S(1)}, f32[264,128]{1,0:T(8,128)S(1)}, u32[]{:S(2)}, u32[]{:S(2)}) collective-permute-start(f32[264,128]{1,0:T(8,128)S(1)} %gather.1.m0_ref), channel_id=1, source_target_pairs={{0,192},{64,0},{128,64},{192,128},{1,193},{65,1},{129,65},{193,129... | collective-permute-start | bytes 405512 | tf_op jit(solution)/shard_map/ppermute | solution.py:430
  39.1 0.8 %collective-permute-start.1 = (f32[264,128]{1,0:T(8,128)S(1)}, f32[264,128]{1,0:T(8,128)S(1)}, u32[]{:S(2)}, u32[]{:S(2)}) collective-permute-start(f32[264,128]{1,0:T(8,128)S(1)} %gather.1.m0_ref), channel_id=1, source_target_pairs={{0,128},{64,192},{128,0},{192,64},{1,129},{65,193},{129,1},{193,65... | collective-permute-start | bytes 405512 | tf_op jit(solution)/shard_map/ppermute | solution.py:430
  39.9 2.6 %collective-permute-done.5.d_ref = f32[4,24,512]{2,1,0:T(8,128)} collective-permute-done((f32[4,24,512]{2,1,0:T(8,128)}, f32[4,24,512]{2,1,0:T(8,128)}, u32[]{:S(2)}, u32[]{:S(2)}) %collective-permute-start.5) | collective-permute-done | bytes 196640 | tf_op jit(solution)/shard_map/ppermute | solution.py:430
  42.5 1.1 %stiff_part.1.stiff_ref = f32[48,729]{1,0:T(8,128)S(1)} custom-call(f32[48,729]{1,0:T(8,128)S(1)} %bitcast.9, f32[729,729]{1,0:T(8,128)S(1)} %copy-done, f32[1,48]{1,0:T(1,128)S(1)} %bitcast.10), custom_call_target="tpu_custom_call" | custom-call | flops 306110016 | bytes 3145728 | tf_op jit(solution)/shard_map/stiff_part/pallas_call | solution.py:418
  43.6 3.1 %collective-permute-done.3.b_ref = f32[4,24,512]{2,1,0:T(8,128)} collective-permute-done((f32[4,24,512]{2,1,0:T(8,128)}, f32[4,24,512]{2,1,0:T(8,128)}, u32[]{:S(2)}, u32[]{:S(2)}) %collective-permute-start.3) | collective-permute-done | bytes 196640 | tf_op jit(solution)/shard_map/ppermute | solution.py:430
  46.8 0.8 %collective-permute-done.2.m3_ref = f32[264,128]{1,0:T(8,128)S(1)} collective-permute-done((f32[264,128]{1,0:T(8,128)S(1)}, f32[264,128]{1,0:T(8,128)S(1)}, u32[]{:S(2)}, u32[]{:S(2)}) %collective-permute-start.2) | collective-permute-done | bytes 135200 | tf_op jit(solution)/shard_map/ppermute | solution.py:430
  47.6 1.9 %collective-permute-done.1.m2_ref = f32[264,128]{1,0:T(8,128)S(1)} collective-permute-done((f32[264,128]{1,0:T(8,128)S(1)}, f32[264,128]{1,0:T(8,128)S(1)}, u32[]{:S(2)}, u32[]{:S(2)}) %collective-permute-start.1) | collective-permute-done | bytes 135200 | tf_op jit(solution)/shard_map/ppermute | solution.py:430
  49.5 1.8 %collective-permute-done.m1_ref = f32[264,128]{1,0:T(8,128)S(1)} collective-permute-done((f32[264,128]{1,0:T(8,128)S(1)}, f32[264,128]{1,0:T(8,128)S(1)}, u32[]{:S(2)}, u32[]{:S(2)}) %collective-permute-start) | collective-permute-done | bytes 135200 | tf_op jit(solution)/shard_map/ppermute | solution.py:430
  51.3 0.0 copy-start.10
  51.3 0.9 %copy-done.10 = f32[48,512]{1,0:T(8,128)S(1)} copy-done((f32[48,512]{1,0:T(8,128)S(1)}, f32[48,512]{1,0:T(8,128)}, u32[]{:S(2)}) %copy-start.10) | copy-done | bytes 98328
  52.2 1.7 %copy-done.11 = bf16[3072,384]{1,0:T(8,128)(2,1)S(1)} copy-done((bf16[3072,384]{1,0:T(8,128)(2,1)S(1)}, bf16[3072,384]{1,0:T(8,128)(2,1)}, u32[]{:S(2)}) %copy-start.11) | copy-done | bytes 2359320
  53.9 17.2 %second_pass.1 = (bf16[343,24,128]{2,1,0:T(8,128)(2,1)}, f32[48,729]{1,0:T(8,128)}) custom-call(s32[1]{0:T(128)} %bitcast.band_ref, f32[264,128]{1,0:T(8,128)S(1)} %gather.1.m0_ref, f32[264,128]{1,0:T(8,128)S(1)} %collective-permute-done.m1_ref, f32[264,128]{1,0:T(8,128)S(1)} %collective-permute-done.1.m2_ref, f32[264,128]{1,0:T(8,128)S(1)} %collective-permute-done.2.m3_ref, ...), custom_call_target="tpu_custom_call" | custom-call | flops 12884901888 | bytes 8388608 | tf_op jit(solution)/shard_map/second_pass/pallas_call | solution.py:381
  (19 shorter events, 0.0 us)
Async XLA Ops:
  7.2 28.3 %all-to-all-start = ((f32[128,1,896]{2,1,0:T(1,128)}), f32[128,1,896]{2,1,0:T(1,128)S(1)}, u32[]{:S(2)}, u32[]{:S(2)}) async-start(f32[128,1,896]{2,1,0:T(1,128)} %get-tuple-element.10), calls=%async_computation | async-start | bytes 917504 | tf_op jit(solution)/shard_map/all_to_all | solution.py:445
  19.4 16.2 %copy-start.2 = (s32[24]{0:T(128)S(1)}, s32[24]{0:T(128)}, u32[]{:S(2)}) copy-start(s32[24]{0:T(128)} %get-tuple-element.8.wave_row_ref) | copy-start | bytes 292
  19.4 16.2 %copy-start.3 = (s32[48]{0:T(128)S(1)}, s32[48]{0:T(128)}, u32[]{:S(2)}) copy-start(s32[48]{0:T(128)} %get-tuple-element.9.slot_row_ref) | copy-start | bytes 580
  19.4 23.1 %copy-start = (f32[729,729]{1,0:T(8,128)S(1)}, f32[729,729]{1,0:T(8,128)}, u32[]{:S(2)}) copy-start(f32[729,729]{1,0:T(8,128)} %stiff_ref.1) | copy-start | bytes 6377296
  19.4 23.1 %copy-start.1 = (f32[729,48]{0,1:T(8,128)S(1)}, f32[729,48]{0,1:T(8,128)}, u32[]{:S(2)}) copy-start(f32[729,48]{0,1:T(8,128)} %param.18) | copy-start | bytes 419908
  19.4 23.1 %copy-start.4 = (f32[48]{0:T(128)S(1)}, f32[48]{0:T(128)}, u32[]{:S(2)}) copy-start(f32[48]{0:T(128)} %param.20) | copy-start | bytes 580
  19.4 31.9 %copy-start.9 = (f32[48,512]{1,0:T(8,128)S(1)}, f32[48,512]{1,0:T(8,128)}, u32[]{:S(2)}) copy-start(f32[48,512]{1,0:T(8,128)} %core_ref.1) | copy-start | bytes 294916
  30.0 21.3 %copy-start.7 = (bf16[512,343]{0,1:T(8,128)(2,1)S(1)}, bf16[512,343]{0,1:T(8,128)(2,1)}, u32[]{:S(2)}) copy-start(bf16[512,343]{0,1:T(8,128)(2,1)} %param.14) | copy-start | bytes 1053700
  30.0 21.3 %copy-start.8 = (f32[4,24,512]{2,1,0:T(8,128)S(1)}, f32[4,24,512]{2,1,0:T(8,128)}, u32[]{:S(2)}) copy-start(f32[4,24,512]{2,1,0:T(8,128)} %gradient_pass.1.a_ref) | copy-start | bytes 589828
  30.0 12.5 %collective-permute-start.5 = (f32[4,24,512]{2,1,0:T(8,128)}, f32[4,24,512]{2,1,0:T(8,128)}, u32[]{:S(2)}, u32[]{:S(2)}) collective-permute-start(f32[4,24,512]{2,1,0:T(8,128)} %gradient_pass.1.a_ref), channel_id=1, source_target_pairs={{0,192},{64,0},{128,64},{192,128},{1,193},{65,1},{129,65},{193,129... | collective-permute-start | bytes 589832 | tf_op jit(solution)/shard_map/ppermute | solution.py:430
  32.9 10.8 %collective-permute-start.4 = (f32[4,24,512]{2,1,0:T(8,128)}, f32[4,24,512]{2,1,0:T(8,128)}, u32[]{:S(2)}, u32[]{:S(2)}) collective-permute-start(f32[4,24,512]{2,1,0:T(8,128)} %gradient_pass.1.a_ref), channel_id=1, source_target_pairs={{0,128},{64,192},{128,0},{192,64},{1,129},{65,193},{129,1},{193,65... | collective-permute-start | bytes 589832 | tf_op jit(solution)/shard_map/ppermute | solution.py:430
  33.7 13.1 %collective-permute-start.3 = (f32[4,24,512]{2,1,0:T(8,128)}, f32[4,24,512]{2,1,0:T(8,128)}, u32[]{:S(2)}, u32[]{:S(2)}) collective-permute-start(f32[4,24,512]{2,1,0:T(8,128)} %gradient_pass.1.a_ref), channel_id=1, source_target_pairs={{0,64},{64,128},{128,192},{192,0},{1,65},{65,129},{129,193},{193,1... | collective-permute-start | bytes 589832 | tf_op jit(solution)/shard_map/ppermute | solution.py:430
  35.5 15.8 %copy-start.5 = (f32[512,729]{0,1:T(8,128)S(1)}, f32[512,729]{0,1:T(8,128)}, u32[]{:S(2)}) copy-start(f32[512,729]{0,1:T(8,128)} %param.21) | copy-start | bytes 4478980
  35.5 15.8 %copy-start.6 = (bf16[3,512,343]{1,2,0:T(8,128)(2,1)S(1)}, bf16[3,512,343]{1,2,0:T(8,128)(2,1)}, u32[]{:S(2)}) copy-start(bf16[3,512,343]{1,2,0:T(8,128)(2,1)} %param.15) | copy-start | bytes 3161092
  36.3 11.3 %collective-permute-start.2 = (f32[264,128]{1,0:T(8,128)S(1)}, f32[264,128]{1,0:T(8,128)S(1)}, u32[]{:S(2)}, u32[]{:S(2)}) collective-permute-start(f32[264,128]{1,0:T(8,128)S(1)} %gather.1.m0_ref), channel_id=1, source_target_pairs={{0,192},{64,0},{128,64},{192,128},{1,193},{65,1},{129,65},{193,129... | collective-permute-start | bytes 405512 | tf_op jit(solution)/shard_map/ppermute | solution.py:430
  39.1 10.4 %collective-permute-start.1 = (f32[264,128]{1,0:T(8,128)S(1)}, f32[264,128]{1,0:T(8,128)S(1)}, u32[]{:S(2)}, u32[]{:S(2)}) collective-permute-start(f32[264,128]{1,0:T(8,128)S(1)} %gather.1.m0_ref), channel_id=1, source_target_pairs={{0,128},{64,192},{128,0},{192,64},{1,129},{65,193},{129,1},{193,65... | collective-permute-start | bytes 405512 | tf_op jit(solution)/shard_map/ppermute | solution.py:430
  42.5 8.8 %collective-permute-start = (f32[264,128]{1,0:T(8,128)S(1)}, f32[264,128]{1,0:T(8,128)S(1)}, u32[]{:S(2)}, u32[]{:S(2)}) collective-permute-start(f32[264,128]{1,0:T(8,128)S(1)} %gather.1.m0_ref), channel_id=1, source_target_pairs={{0,64},{64,128},{128,192},{192,0},{1,65},{65,129},{129,193},{193,1... | collective-permute-start | bytes 405512 | tf_op jit(solution)/shard_map/ppermute | solution.py:430
  51.3 0.9 %copy-start.10 = (f32[48,512]{1,0:T(8,128)S(1)}, f32[48,512]{1,0:T(8,128)}, u32[]{:S(2)}) copy-start(f32[48,512]{1,0:T(8,128)} %weight_ref.1) | copy-start | bytes 294916
  52.2 1.7 %copy-start.11 = (bf16[3072,384]{1,0:T(8,128)(2,1)S(1)}, bf16[3072,384]{1,0:T(8,128)(2,1)}, u32[]{:S(2)}) copy-start(bf16[3072,384]{1,0:T(8,128)(2,1)} %get-tuple-element.11.node_hbm) | copy-start | bytes 7077892

commit v5 on v3

--- a/solution.py
+++ b/solution.py
@@ -197,26 +197,31 @@
     spread_ref[...] = jnp.broadcast_to(occ_ref[...], (BANDS, BANDS)).T
     take(0).wait()
 
+    def evaluate(g, k):
+        rows = slice(g * GROUP * BANDS, (g + 1) * GROUP * BANDS)
+        slab_ref[g % 2, k] = jnp.dot(node_ref[rows, :NODES], table_ref[k], preferred_element_type=F32)
+
+    def reduce(g, i):
+        c = g * GROUP + i
+        bands = slice(i * BANDS, (i + 1) * BANDS)
+        for q in range(RANKS):
+            lead = slab_ref[g % 2, 0, bands, lanes(q)]
+            scaled = spread_ref[...] * lead
+            sum_ref[q, 0, c : c + 1, :] = jnp.sum(scaled * lead, axis=0, keepdims=True)
+            for k in range(1, 4):
+                term = slab_ref[g % 2, k, bands, lanes(q)]
+                sum_ref[q, k, c : c + 1, :] = 2.0 * jnp.sum(scaled * term, axis=0, keepdims=True)
+
+    for k in range(4):
+        tables[k].wait()
+        evaluate(0, k)
+    for g in range(1, groups):
+        take(g).wait()
     for g in range(groups):
-        slab = slab_ref.at[g % 2]
-        rows = slice(g * GROUP * BANDS, (g + 1) * GROUP * BANDS)
-        if g == 1:
-            for later in range(1, groups):
-                take(later).wait()
-        for k in range(4):
-            if g == 0:
-                tables[k].wait()
-            slab[k] = jnp.dot(node_ref[rows, :NODES], table_ref[k], preferred_element_type=F32)
         for i in range(GROUP):
-            c = g * GROUP + i
-            bands = slice(i * BANDS, (i + 1) * BANDS)
-            for q in range(RANKS):
-                lead = slab[0, bands, lanes(q)]
-                scaled = spread_ref[...] * lead
-                sum_ref[q, 0, c : c + 1, :] = jnp.sum(scaled * lead, axis=0, keepdims=True)
-                for k in range(1, 4):
-                    term = slab[k, bands, lanes(q)]
-                    sum_ref[q, k, c : c + 1, :] = 2.0 * jnp.sum(scaled * term, axis=0, keepdims=True)
+            if g + 1 < groups:
+                evaluate(g + 1, i)
+            reduce(g, i)
     for d, part_ref in enumerate((part0_ref, part1_ref, part2_ref, part3_ref)):
         part_ref[...] = sum_ref[(band_ref[0] + d) & (RANKS - 1)]
 
@@ -255,7 +260,8 @@
     return d_density, d_square
 
 
-def gather_kernel(wave_row_ref, slot_row_ref, came_ref, field_ref, dens_ref):
+def gather_kernel(wave_row_ref, slot_row_ref, came_ref, part_ref, field_ref, dens_ref, own_ref):
+    own_ref[...] = part_ref[...]
     for c in range(CELLS):
         row = wave_row_ref[c]
         for f in range(3):
@@ -270,19 +276,20 @@
             dens_ref[place : place + 1, :] = jnp.where(row < ROWS, value, 0.0)
 
 
-def gather(wave_rows, slot_rows, came):
+def gather(wave_rows, slot_rows, came, part):
     return pl.pallas_call(
         gather_kernel,
         out_shape=(
             jax.ShapeDtypeStruct((3 * CELLS, PART), F32),
             jax.ShapeDtypeStruct((RANKS * SLOTS, PART), F32),
+            jax.ShapeDtypeStruct((4, CELLS, PART), F32),
         ),
-        in_specs=[SM, SM, VM],
-        out_specs=(VM, VM),
+        in_specs=[SM, SM, VM, VM],
+        out_specs=(VM, VM, VM),
         compiler_params=params(8),
         cost_estimate=cost(1e6, MIB),
         name="gather",
-    )(wave_rows, slot_rows, came)
+    )(wave_rows, slot_rows, came, part)
 
 
 def exchange_kernel(field_ref, dens_ref, a_ref, b_ref, c_ref, d_ref, mix_ref):
@@ -309,10 +316,10 @@
 
 
 def second_kernel(
-    band_ref, m0_ref, m1_ref, m2_ref, m3_ref, val_ref, grad_ref, node_ref,
-    core_ref, weight_ref, shape_ref, stiff_ref, val_hbm, grad_hbm,
+    band_ref, m0_ref, m1_ref, m2_ref, m3_ref, val_ref, grad_ref,
+    core_ref, weight_ref, shape_ref, stiff_ref, node_hbm, val_hbm, grad_hbm,
     out_hbm, rest_ref,
-    wt_ref, table_ref, slab_ref, prod_ref, wide_ref, out_ref, source_ref, table_sem, out_sem,
+    wt_ref, node_ref, table_ref, slab_ref, prod_ref, wide_ref, out_ref, source_ref, node_sem, table_sem, out_sem,
 ):
     groups = CELLS // GROUP
     tables = [pltpu.make_async_copy(val_hbm, table_ref.at[:, :POINTS], table_sem.at[0])]
@@ -322,6 +329,13 @@
                 grad_hbm.at[k], table_ref.at[:, (k + 1) * POINTS : (k + 2) * POINTS], table_sem.at[k + 1]
             )
         )
+
+    def take(g):
+        rows = pl.ds(g * GROUP * BANDS, GROUP * BANDS)
+        return pltpu.make_async_copy(node_hbm.at[rows], node_ref.at[rows], node_sem.at[g])
+
+    for g in range(groups):
+        take(g).start()
     for table in tables:
         table.start()
     for d, source in enumerate((m0_ref, m1_ref, m2_ref, m3_ref)):
@@ -353,8 +367,11 @@
             c = g * GROUP + 2 * pair + i
             wide_ref[pl.ds(c, NODES, stride=CELLS), :] = result[:, i * BANDS : (i + 1) * BANDS]
 
+    take(0).wait()
     for k in range(4):
         evaluate(0, k)
+    for g in range(1, groups):
+        take(g).wait()
     for table in tables:
         table.wait()
     for g in range(groups):
@@ -385,29 +402,32 @@
 
 
 def second_pass(band, mixes, values, grads, cell_nodes, core, weight, shape, stiff):
+    cell_nodes = pltpu.with_memory_space_constraint(cell_nodes, pltpu.HBM)
     return pl.pallas_call(
         second_kernel,
         out_shape=(
             jax.ShapeDtypeStruct((NODES, CELLS, BANDS), BF16),
             jax.ShapeDtypeStruct((SLOTS, ENODES), F32),
         ),
-        in_specs=[SM] + [VM] * 11 + [HB] * 2,
+        in_specs=[SM] + [VM] * 10 + [HB] * 3,
         out_specs=(HB, VM),
         scratch_shapes=[
             pltpu.VMEM((RANKS, TERMS, PART), F32),
+            pltpu.VMEM((CELLS * BANDS, KPAD), BF16),
             pltpu.VMEM((NODES, 4 * POINTS), BF16),
             pltpu.VMEM((2, 4, GROUP * BANDS, POINTS), F32),
             pltpu.VMEM((2, GROUP * BANDS, 4 * POINTS), BF16),
             pltpu.VMEM((NODES * CELLS, BANDS), F32),
             pltpu.VMEM((NODES, CELLS, BANDS), BF16),
             pltpu.VMEM((SLOTS, POINTS), F32),
+            pltpu.SemaphoreType.DMA((CELLS // GROUP,)),
             pltpu.SemaphoreType.DMA((4,)),
             pltpu.SemaphoreType.DMA((NODES // STEP,)),
         ],
         compiler_params=params(36),
         cost_estimate=cost(4 * 2048 * 512 * 3072, 8 * MIB),
         name="second_pass",
-    )(band, *mixes, values, grads, cell_nodes, core, weight, shape, stiff, values, grads)
+    )(band, *mixes, values, grads, core, weight, shape, stiff, cell_nodes, values, grads)
 
 
 def stiff_kernel(nodes_ref, stiff_ref, scale_ref, out_ref):
@@ -448,10 +468,10 @@
     )
     came = lax.all_to_all(send, "dom", split_axis=0, concat_axis=0, tiled=True)
     parts = gradient_pass(band, occupancy, values, grads, cell_nodes)
-    parts = [parts[0]] + [shift(parts[d], d) for d in (1, 2, 3)]
+    others = [shift(parts[d], d) for d in (1, 2, 3)]
     stiff = stiff_part(nodes, stiffness, stiff_scale.reshape(1, SLOTS))
-    field, dens = gather(wave_rows, slot_rows, came)
-    mix = exchange(field, dens, parts)
+    field, dens, own = gather(wave_rows, slot_rows, came, parts[0])
+    mix = exchange(field, dens, [own] + others)
     mixes = [mix] + [shift(mix, d) for d in (1, 2, 3)]
     action, rest = second_pass(
         band, mixes, values, grads, cell_nodes, core_density, quad_weight, shape, stiff

time: 67.8 us -> 67.2 us (level); the launches traced: 67.5 us -> 66.2 us
  local copies, waits for them, and re-layouts: 2.51 us -> 0.84 us
  Pallas kernels: 33.9 us -> 34.8 us
    unnamed x24 -> x22, local copies, waits for them, and re-layouts: 2.51 us -> 0.84 us
  transfers between devices with their start and end apart: 7 -> 7, of which waited for: 5 -> 5; matrix products, arithmetic and copies ran while one was open for 0% -> 0% of each run, Pallas kernels for 18% -> 19%
where the time goes in v5:
time: 67.2 us; the launch traced here: 66.2 us
  Pallas kernels  34.8 us (52%)
  starting transfers between devices  21.5 us (32%)
  waiting for transfers between devices  8.06 us (12%)
  between operations  0.95 us (1%)
  local copies, waits for them, and re-layouts  0.84 us (1%)
    pallas_call x1, Pallas kernels, second_pass(): pl.pallas_call(second_kernel, out_shape=(jax.ShapeDtypeStruct((NODES, CEL...  15.8 us
    all_to_all x1, starting transfers between devices, body(): came = lax.all_to_all(send, 'dom', split_axis=0, concat_axis=0, tiled=True)  12.1 us
    pallas_call x1, Pallas kernels, gradient_pass(): pl.pallas_call(gradient_kernel, out_shape=(part, part, part, part), in_sp...  10.6 us
    ppermute x6, starting transfers between devices, shift(): lax.ppermute(array, 'band', [(i, (i + distance) % RANKS) for i in range(R...  9.39 us
    ppermute x6, waiting for transfers between devices, shift(): lax.ppermute(array, 'band', [(i, (i + distance) % RANKS) for i in range(R...  8.06 us
    pallas_call x1, Pallas kernels, first_pass(): pl.pallas_call(first_kernel, out_shape=(jax.ShapeDtypeStruct((ROWS, 1, WI...  6.6 us
  transfers between devices with their start and end apart: 7, of which 5 were waited for; matrix products, arithmetic and copies ran while one was open for 0% of the time, Pallas kernels for 19%

profile of v5, /device:TPU:8, one launch (start us, length us, event | category | flops | bytes accessed | tf_op | source)
XLA Modules:
  0.0 66.2 jit_solution(17817292956130293505)
XLA Ops:
  0.6 6.6 %first_pass.1 = (f32[128,1,896]{2,1,0:T(1,128)}, bf16[3072,384]{1,0:T(8,128)(2,1)}, s32[24]{0:T(128)}, s32[48]{0:T(128)}) custom-call(s32[1]{0:T(128)} %bitcast.band_ref, s32[48]{0:T(128)} %slot_cell_ref.1, s32[24]{0:T(128)} %cell_slot_ref.1, bf16[343,24,128]{2,1,0:T(8,128)(2,1)} %orb_hbm.1, f32[1,128]{1,0:T(1,128)} %bitcast.20, bf16[343,512]{1,0:T(8,128)(2,1)} %bitcast.16, ...), custom_call_target="tpu_custom_call" | custom-call | flops 1610612736 | bytes 8388608 | tf_op jit(solution)/shard_map/first_pass/pallas_call | solution.py:143
  7.2 12.1 %all-to-all-start = ((f32[128,1,896]{2,1,0:T(1,128)}), f32[128,1,896]{2,1,0:T(1,128)S(1)}, u32[]{:S(2)}, u32[]{:S(2)}) async-start(f32[128,1,896]{2,1,0:T(1,128)} %get-tuple-element.17), calls=%async_computation | async-start | bytes 917504 | tf_op jit(solution)/shard_map/all_to_all | solution.py:469
  19.4 0.0 copy-start
  19.4 0.0 copy-start.1
  19.4 0.0 copy-start.5
  19.4 0.0 copy-start.8
  19.4 0.0 copy-start.9
  19.4 10.6 %gradient_pass.1 = (f32[4,24,128]{2,1,0:T(8,128)}, f32[4,24,128]{2,1,0:T(8,128)}, f32[4,24,128]{2,1,0:T(8,128)}, f32[4,24,128]{2,1,0:T(8,128)}) custom-call(s32[1]{0:T(128)} %bitcast.band_ref, f32[1,128]{1,0:T(1,128)} %bitcast.21, bf16[343,512]{1,0:T(8,128)(2,1)} %bitcast.17, bf16[3,343,512]{2,1,0:T(8,128)(2,1)} %bitcast.13, ...), custom_call_target="tpu_custom_call" | custom-call | flops 6442450944 | bytes 8388608 | tf_op jit(solution)/shard_map/gradient_pass/pallas_call | solution.py:231
  30.1 1.6 %collective-permute-start = (f32[4,24,128]{2,1,0:T(8,128)}, f32[4,24,128]{2,1,0:T(8,128)S(1)}, u32[]{:S(2)}, u32[]{:S(2)}) collective-permute-start(f32[4,24,128]{2,1,0:T(8,128)} %get-tuple-element.23), channel_id=1, source_target_pairs={{0,64},{64,128},{128,192},{192,0},{1,65},{65,129},{129,193},{193,1... | collective-permute-start | bytes 147464 | tf_op jit(solution)/shard_map/ppermute | solution.py:454
  31.6 2.7 %collective-permute-start.1 = (f32[4,24,128]{2,1,0:T(8,128)}, f32[4,24,128]{2,1,0:T(8,128)S(1)}, u32[]{:S(2)}, u32[]{:S(2)}) collective-permute-start(f32[4,24,128]{2,1,0:T(8,128)} %get-tuple-element.24), channel_id=1, source_target_pairs={{0,128},{64,192},{128,0},{192,64},{1,129},{65,193},{129,1},{193,65... | collective-permute-start | bytes 147464 | tf_op jit(solution)/shard_map/ppermute | solution.py:454
  34.4 1.4 %collective-permute-start.2 = (f32[4,24,128]{2,1,0:T(8,128)}, f32[4,24,128]{2,1,0:T(8,128)S(1)}, u32[]{:S(2)}, u32[]{:S(2)}) collective-permute-start(f32[4,24,128]{2,1,0:T(8,128)} %get-tuple-element.25), channel_id=1, source_target_pairs={{0,192},{64,0},{128,64},{192,128},{1,193},{65,1},{129,65},{193,129... | collective-permute-start | bytes 147464 | tf_op jit(solution)/shard_map/ppermute | solution.py:454
  35.8 0.0 all-to-all-done.came_ref
  35.8 0.0 copy-start.2
  35.8 0.8 %copy-done.2 = f32[4,24,128]{2,1,0:T(8,128)S(1)} copy-done((f32[4,24,128]{2,1,0:T(8,128)S(1)}, f32[4,24,128]{2,1,0:T(8,128)}, u32[]{:S(2)}) %copy-start.2) | copy-done | bytes 49176
  36.6 0.7 %gather.1 = (f32[72,128]{1,0:T(8,128)S(1)}, f32[192,128]{1,0:T(8,128)S(1)}, f32[4,24,128]{2,1,0:T(8,128)S(1)}) custom-call(s32[24]{0:T(128)S(1)} %copy-done.3, s32[48]{0:T(128)S(1)} %copy-done.4, f32[128,1,896]{2,1,0:T(1,128)S(1)} %all-to-all-done.came_ref, f32[4,24,128]{2,1,0:T(8,128)S(1)} %copy-done.2), custom_call_target="tpu_custom_call" | custom-call | flops 1000000 | bytes 1048576 | tf_op jit(solution)/shard_map/gather/pallas_call | solution.py:280
  37.3 0.1 collective-permute-done.1.c_ref
  37.4 1.2 %collective-permute-done.2.d_ref = f32[4,24,128]{2,1,0:T(8,128)S(1)} collective-permute-done((f32[4,24,128]{2,1,0:T(8,128)}, f32[4,24,128]{2,1,0:T(8,128)S(1)}, u32[]{:S(2)}, u32[]{:S(2)}) %collective-permute-start.2) | collective-permute-done | bytes 49184 | tf_op jit(solution)/shard_map/ppermute | solution.py:454
  38.7 2.7 %collective-permute-start.5 = (f32[288,128]{1,0:T(8,128)S(1)}, f32[288,128]{1,0:T(8,128)S(1)}, u32[]{:S(2)}, u32[]{:S(2)}) collective-permute-start(f32[288,128]{1,0:T(8,128)S(1)} %exchange.1.m0_ref), channel_id=1, source_target_pairs={{0,192},{64,0},{128,64},{192,128},{1,193},{65,1},{129,65},{193,129... | collective-permute-start | bytes 442376 | tf_op jit(solution)/shard_map/ppermute | solution.py:454
  41.4 1.0 %collective-permute-start.3 = (f32[288,128]{1,0:T(8,128)S(1)}, f32[288,128]{1,0:T(8,128)S(1)}, u32[]{:S(2)}, u32[]{:S(2)}) collective-permute-start(f32[288,128]{1,0:T(8,128)S(1)} %exchange.1.m0_ref), channel_id=1, source_target_pairs={{0,64},{64,128},{128,192},{192,0},{1,65},{65,129},{129,193},{193,1... | collective-permute-start | bytes 442376 | tf_op jit(solution)/shard_map/ppermute | solution.py:454
  42.4 1.1 %stiff_part.1.stiff_ref = f32[48,729]{1,0:T(8,128)S(1)} custom-call(f32[48,729]{1,0:T(8,128)S(1)} %bitcast.9, f32[729,729]{1,0:T(8,128)S(1)} %copy-done, f32[1,48]{1,0:T(1,128)S(1)} %bitcast.10), custom_call_target="tpu_custom_call" | custom-call | flops 306110016 | bytes 3145728 | tf_op jit(solution)/shard_map/stiff_part/pallas_call | solution.py:442
  43.5 3.1 %collective-permute-done.5.m3_ref = f32[288,128]{1,0:T(8,128)S(1)} collective-permute-done((f32[288,128]{1,0:T(8,128)S(1)}, f32[288,128]{1,0:T(8,128)S(1)}, u32[]{:S(2)}, u32[]{:S(2)}) %collective-permute-start.5) | collective-permute-done | bytes 147488 | tf_op jit(solution)/shard_map/ppermute | solution.py:454
  46.6 2.2 %collective-permute-done.4.m2_ref = f32[288,128]{1,0:T(8,128)S(1)} collective-permute-done((f32[288,128]{1,0:T(8,128)S(1)}, f32[288,128]{1,0:T(8,128)S(1)}, u32[]{:S(2)}, u32[]{:S(2)}) %collective-permute-start.4) | collective-permute-done | bytes 147488 | tf_op jit(solution)/shard_map/ppermute | solution.py:454
  48.7 1.5 %collective-permute-done.3.m1_ref = f32[288,128]{1,0:T(8,128)S(1)} collective-permute-done((f32[288,128]{1,0:T(8,128)S(1)}, f32[288,128]{1,0:T(8,128)S(1)}, u32[]{:S(2)}, u32[]{:S(2)}) %collective-permute-start.3) | collective-permute-done | bytes 147488 | tf_op jit(solution)/shard_map/ppermute | solution.py:454
  50.3 15.8 %second_pass.1 = (bf16[343,24,128]{2,1,0:T(8,128)(2,1)}, f32[48,729]{1,0:T(8,128)}) custom-call(s32[1]{0:T(128)} %bitcast.band_ref, f32[288,128]{1,0:T(8,128)S(1)} %exchange.1.m0_ref, f32[288,128]{1,0:T(8,128)S(1)} %collective-permute-done.3.m1_ref, f32[288,128]{1,0:T(8,128)S(1)} %collective-permute-done.4.m2_ref, ...), custom_call_target="tpu_custom_call" | custom-call | flops 12884901888 | bytes 8388608 | tf_op jit(solution)/shard_map/second_pass/pallas_call | solution.py:406
  (18 shorter events, 0.1 us)
Async XLA Ops:
  7.2 28.5 %all-to-all-start = ((f32[128,1,896]{2,1,0:T(1,128)}), f32[128,1,896]{2,1,0:T(1,128)S(1)}, u32[]{:S(2)}, u32[]{:S(2)}) async-start(f32[128,1,896]{2,1,0:T(1,128)} %get-tuple-element.17), calls=%async_computation | async-start | bytes 917504 | tf_op jit(solution)/shard_map/all_to_all | solution.py:469
  19.4 16.4 %copy-start.3 = (s32[24]{0:T(128)S(1)}, s32[24]{0:T(128)}, u32[]{:S(2)}) copy-start(s32[24]{0:T(128)} %get-tuple-element.15.wave_row_ref) | copy-start | bytes 292
  19.4 16.4 %copy-start.4 = (s32[48]{0:T(128)S(1)}, s32[48]{0:T(128)}, u32[]{:S(2)}) copy-start(s32[48]{0:T(128)} %get-tuple-element.16.slot_row_ref) | copy-start | bytes 580
  19.4 23.0 %copy-start = (f32[729,729]{1,0:T(8,128)S(1)}, f32[729,729]{1,0:T(8,128)}, u32[]{:S(2)}) copy-start(f32[729,729]{1,0:T(8,128)} %stiff_ref.1) | copy-start | bytes 6377296
  19.4 23.0 %copy-start.1 = (f32[729,48]{0,1:T(8,128)S(1)}, f32[729,48]{0,1:T(8,128)}, u32[]{:S(2)}) copy-start(f32[729,48]{0,1:T(8,128)} %param.18) | copy-start | bytes 419908
  19.4 23.0 %copy-start.5 = (f32[48]{0:T(128)S(1)}, f32[48]{0:T(128)}, u32[]{:S(2)}) copy-start(f32[48]{0:T(128)} %param.20) | copy-start | bytes 580
  19.4 30.8 %copy-start.8 = (bf16[512,343]{0,1:T(8,128)(2,1)S(1)}, bf16[512,343]{0,1:T(8,128)(2,1)}, u32[]{:S(2)}) copy-start(bf16[512,343]{0,1:T(8,128)(2,1)} %param.14) | copy-start | bytes 1053700
  19.4 30.8 %copy-start.9 = (f32[48,512]{1,0:T(8,128)S(1)}, f32[48,512]{1,0:T(8,128)}, u32[]{:S(2)}) copy-start(f32[48,512]{1,0:T(8,128)} %core_ref.1) | copy-start | bytes 294916
  30.1 7.3 %collective-permute-start = (f32[4,24,128]{2,1,0:T(8,128)}, f32[4,24,128]{2,1,0:T(8,128)S(1)}, u32[]{:S(2)}, u32[]{:S(2)}) collective-permute-start(f32[4,24,128]{2,1,0:T(8,128)} %get-tuple-element.23), channel_id=1, source_target_pairs={{0,64},{64,128},{128,192},{192,0},{1,65},{65,129},{129,193},{193,1... | collective-permute-start | bytes 147464 | tf_op jit(solution)/shard_map/ppermute | solution.py:454
  31.6 5.8 %collective-permute-start.1 = (f32[4,24,128]{2,1,0:T(8,128)}, f32[4,24,128]{2,1,0:T(8,128)S(1)}, u32[]{:S(2)}, u32[]{:S(2)}) collective-permute-start(f32[4,24,128]{2,1,0:T(8,128)} %get-tuple-element.24), channel_id=1, source_target_pairs={{0,128},{64,192},{128,0},{192,64},{1,129},{65,193},{129,1},{193,65... | collective-permute-start | bytes 147464 | tf_op jit(solution)/shard_map/ppermute | solution.py:454
  34.4 4.3 %collective-permute-start.2 = (f32[4,24,128]{2,1,0:T(8,128)}, f32[4,24,128]{2,1,0:T(8,128)S(1)}, u32[]{:S(2)}, u32[]{:S(2)}) collective-permute-start(f32[4,24,128]{2,1,0:T(8,128)} %get-tuple-element.25), channel_id=1, source_target_pairs={{0,192},{64,0},{128,64},{192,128},{1,193},{65,1},{129,65},{193,129... | collective-permute-start | bytes 147464 | tf_op jit(solution)/shard_map/ppermute | solution.py:454
  35.8 0.8 %copy-start.2 = (f32[4,24,128]{2,1,0:T(8,128)S(1)}, f32[4,24,128]{2,1,0:T(8,128)}, u32[]{:S(2)}) copy-start(f32[4,24,128]{2,1,0:T(8,128)} %get-tuple-element.19.part_ref) | copy-start | bytes 147460
  36.6 13.6 %copy-start.6 = (f32[512,729]{0,1:T(8,128)S(1)}, f32[512,729]{0,1:T(8,128)}, u32[]{:S(2)}) copy-start(f32[512,729]{0,1:T(8,128)} %param.21) | copy-start | bytes 4478980
  36.6 13.6 %copy-start.7 = (bf16[3,512,343]{1,2,0:T(8,128)(2,1)S(1)}, bf16[3,512,343]{1,2,0:T(8,128)(2,1)}, u32[]{:S(2)}) copy-start(bf16[3,512,343]{1,2,0:T(8,128)(2,1)} %param.15) | copy-start | bytes 3161092
  36.6 13.7 %copy-start.10 = (f32[48,512]{1,0:T(8,128)S(1)}, f32[48,512]{1,0:T(8,128)}, u32[]{:S(2)}) copy-start(f32[48,512]{1,0:T(8,128)} %weight_ref.1) | copy-start | bytes 294916
  38.7 7.8 %collective-permute-start.5 = (f32[288,128]{1,0:T(8,128)S(1)}, f32[288,128]{1,0:T(8,128)S(1)}, u32[]{:S(2)}, u32[]{:S(2)}) collective-permute-start(f32[288,128]{1,0:T(8,128)S(1)} %exchange.1.m0_ref), channel_id=1, source_target_pairs={{0,192},{64,0},{128,64},{192,128},{1,193},{65,1},{129,65},{193,129... | collective-permute-start | bytes 442376 | tf_op jit(solution)/shard_map/ppermute | solution.py:454
  41.4 7.3 %collective-permute-start.4 = (f32[288,128]{1,0:T(8,128)S(1)}, f32[288,128]{1,0:T(8,128)S(1)}, u32[]{:S(2)}, u32[]{:S(2)}) collective-permute-start(f32[288,128]{1,0:T(8,128)S(1)} %exchange.1.m0_ref), channel_id=1, source_target_pairs={{0,128},{64,192},{128,0},{192,64},{1,129},{65,193},{129,1},{193,65... | collective-permute-start | bytes 442376 | tf_op jit(solution)/shard_map/ppermute | solution.py:454
  41.4 8.8 %collective-permute-start.3 = (f32[288,128]{1,0:T(8,128)S(1)}, f32[288,128]{1,0:T(8,128)S(1)}, u32[]{:S(2)}, u32[]{:S(2)}) collective-permute-start(f32[288,128]{1,0:T(8,128)S(1)} %exchange.1.m0_ref), channel_id=1, source_target_pairs={{0,64},{64,128},{128,192},{192,0},{1,65},{65,129},{129,193},{193,1... | collective-permute-start | bytes 442376 | tf_op jit(solution)/shard_map/ppermute | solution.py:454

commit v6 on v3

--- a/solution.py
+++ b/solution.py
@@ -48,9 +48,9 @@
 def first_kernel(
     band_ref, slot_cell_ref, cell_slot_ref,
     orb_hbm, occ_ref, val_hbm, nodes_hbm, shape_hbm, core_hbm, weight_hbm,
-    send_hbm, node_hbm, wave_row_ref, slot_row_ref,
+    send_hbm, node_hbm, head_hbm, wave_row_ref, slot_row_ref,
     orb_ref, val_ref, nodes_ref, shape_ref, field_ref, send_ref,
-    wide_ref, node_ref, table_ref, spread_ref, sum_ref, count_ref, in_sem, orb_sem, out_sem, send_sem,
+    wide_ref, node_ref, table_ref, spread_ref, sum_ref, count_ref, in_sem, orb_sem, out_sem, send_sem, head_sem,
 ):
     mine = pl.ds(pl.multiple_of(band_ref[0] * PART, PART), PART)
     chunks = NODES // STEP
@@ -124,6 +124,9 @@
             block = wide_ref[pl.ds(c, KPAD, stride=CELLS), :]
             node_ref[c * BANDS : (c + 1) * BANDS, :] = block.T.astype(BF16)
         store(g).start()
+        if g == 0:
+            head = pltpu.make_async_copy(node_ref.at[pl.ds(0, GROUP * BANDS)], head_hbm, head_sem)
+            head.start()
         values = jnp.dot(node_ref[rows, :], table_ref[...], preferred_element_type=F32)
         for i in range(GROUP):
             c = g * GROUP + i
@@ -136,6 +139,7 @@
     leave.start()
     for g in range(groups):
         store(g).wait()
+    head.wait()
     leave.wait()
 
 
@@ -145,11 +149,12 @@
         out_shape=(
             jax.ShapeDtypeStruct((ROWS, 1, WIDTH), F32),
             jax.ShapeDtypeStruct((CELLS * BANDS, KPAD), BF16),
+            jax.ShapeDtypeStruct((GROUP * BANDS, KPAD), BF16),
             jax.ShapeDtypeStruct((CELLS,), I32),
             jax.ShapeDtypeStruct((SLOTS,), I32),
         ),
         in_specs=[SM, SM, SM, HB, VM] + [HB] * 5,
-        out_specs=(HB, HB, SM, SM),
+        out_specs=(HB, HB, HB, SM, SM),
         scratch_shapes=[
             pltpu.VMEM((NODES, CELLS, BANDS), BF16),
             pltpu.VMEM((NODES, POINTS), BF16),
@@ -166,6 +171,7 @@
             pltpu.SemaphoreType.DMA((5,)),
             pltpu.SemaphoreType.DMA((NODES // STEP,)),
             pltpu.SemaphoreType.DMA((CELLS // GROUP,)),
+            pltpu.SemaphoreType.DMA,
             pltpu.SemaphoreType.DMA,
         ],
         compiler_params=params(60),
@@ -255,7 +261,8 @@
     return d_density, d_square
 
 
-def gather_kernel(wave_row_ref, slot_row_ref, came_ref, field_ref, dens_ref):
+def gather_kernel(wave_row_ref, slot_row_ref, came_ref, part_ref, field_ref, dens_ref, own_ref):
+    own_ref[...] = part_ref[...]
     for c in range(CELLS):
         row = wave_row_ref[c]
         for f in range(3):
@@ -270,19 +277,20 @@
             dens_ref[place : place + 1, :] = jnp.where(row < ROWS, value, 0.0)
 
 
-def gather(wave_rows, slot_rows, came):
+def gather(wave_rows, slot_rows, came, part):
     return pl.pallas_call(
         gather_kernel,
         out_shape=(
             jax.ShapeDtypeStruct((3 * CELLS, PART), F32),
             jax.ShapeDtypeStruct((RANKS * SLOTS, PART), F32),
+            jax.ShapeDtypeStruct((4, CELLS, PART), F32),
         ),
-        in_specs=[SM, SM, VM],
-        out_specs=(VM, VM),
+        in_specs=[SM, SM, VM, VM],
+        out_specs=(VM, VM, VM),
         compiler_params=params(8),
         cost_estimate=cost(1e6, MIB),
         name="gather",
-    )(wave_rows, slot_rows, came)
+    )(wave_rows, slot_rows, came, part)
 
 
 def exchange_kernel(field_ref, dens_ref, a_ref, b_ref, c_ref, d_ref, mix_ref):
@@ -309,10 +317,10 @@
 
 
 def second_kernel(
-    band_ref, m0_ref, m1_ref, m2_ref, m3_ref, val_ref, grad_ref, node_ref,
-    core_ref, weight_ref, shape_ref, stiff_ref, val_hbm, grad_hbm,
+    band_ref, m0_ref, m1_ref, m2_ref, m3_ref, val_ref, grad_ref, head_ref,
+    core_ref, weight_ref, shape_ref, stiff_ref, node_hbm, val_hbm, grad_hbm,
     out_hbm, rest_ref,
-    wt_ref, table_ref, slab_ref, prod_ref, wide_ref, out_ref, source_ref, table_sem, out_sem,
+    wt_ref, node_ref, table_ref, slab_ref, prod_ref, wide_ref, out_ref, source_ref, node_sem, table_sem, out_sem,
 ):
     groups = CELLS // GROUP
     tables = [pltpu.make_async_copy(val_hbm, table_ref.at[:, :POINTS], table_sem.at[0])]
@@ -322,6 +330,13 @@
                 grad_hbm.at[k], table_ref.at[:, (k + 1) * POINTS : (k + 2) * POINTS], table_sem.at[k + 1]
             )
         )
+
+    def take(g):
+        rows = pl.ds(g * GROUP * BANDS, GROUP * BANDS)
+        return pltpu.make_async_copy(node_hbm.at[rows], node_ref.at[rows], node_sem.at[g])
+
+    for g in range(1, groups):
+        take(g).start()
     for table in tables:
         table.start()
     for d, source in enumerate((m0_ref, m1_ref, m2_ref, m3_ref)):
@@ -330,7 +345,9 @@
     def evaluate(g, k):
         rows = slice(g * GROUP * BANDS, (g + 1) * GROUP * BANDS)
         slab_ref[g % 2, k] = jnp.dot(
-            node_ref[rows, :NODES], grad_ref[k - 1] if k else val_ref[...], preferred_element_type=F32
+            node_ref[rows, :NODES] if g else head_ref[:, :NODES],
+            grad_ref[k - 1] if k else val_ref[...],
+            preferred_element_type=F32,
         )
 
     def products(g, i):
@@ -355,6 +372,8 @@
 
     for k in range(4):
         evaluate(0, k)
+    for g in range(1, groups):
+        take(g).wait()
     for table in tables:
         table.wait()
     for g in range(groups):
@@ -384,30 +403,33 @@
         leave(i).wait()
 
 
-def second_pass(band, mixes, values, grads, cell_nodes, core, weight, shape, stiff):
+def second_pass(band, mixes, values, grads, head, cell_nodes, core, weight, shape, stiff):
+    cell_nodes = pltpu.with_memory_space_constraint(cell_nodes, pltpu.HBM)
     return pl.pallas_call(
         second_kernel,
         out_shape=(
             jax.ShapeDtypeStruct((NODES, CELLS, BANDS), BF16),
             jax.ShapeDtypeStruct((SLOTS, ENODES), F32),
         ),
-        in_specs=[SM] + [VM] * 11 + [HB] * 2,
+        in_specs=[SM] + [VM] * 11 + [HB] * 3,
         out_specs=(HB, VM),
         scratch_shapes=[
             pltpu.VMEM((RANKS, TERMS, PART), F32),
+            pltpu.VMEM((CELLS * BANDS, KPAD), BF16),
             pltpu.VMEM((NODES, 4 * POINTS), BF16),
             pltpu.VMEM((2, 4, GROUP * BANDS, POINTS), F32),
             pltpu.VMEM((2, GROUP * BANDS, 4 * POINTS), BF16),
             pltpu.VMEM((NODES * CELLS, BANDS), F32),
             pltpu.VMEM((NODES, CELLS, BANDS), BF16),
             pltpu.VMEM((SLOTS, POINTS), F32),
+            pltpu.SemaphoreType.DMA((CELLS // GROUP,)),
             pltpu.SemaphoreType.DMA((4,)),
             pltpu.SemaphoreType.DMA((NODES // STEP,)),
         ],
         compiler_params=params(36),
         cost_estimate=cost(4 * 2048 * 512 * 3072, 8 * MIB),
         name="second_pass",
-    )(band, *mixes, values, grads, cell_nodes, core, weight, shape, stiff, values, grads)
+    )(band, *mixes, values, grads, head, core, weight, shape, stiff, cell_nodes, values, grads)
 
 
 def stiff_kernel(nodes_ref, stiff_ref, scale_ref, out_ref):
@@ -443,18 +465,18 @@
     occupancy = occupancy.reshape(1, BANDS)
     band = lax.axis_index("band").astype(I32).reshape(1)
 
-    send, cell_nodes, wave_rows, slot_rows = first_pass(
+    send, cell_nodes, head, wave_rows, slot_rows = first_pass(
         band, slot_cell, cell_slot, orbitals, occupancy, values, nodes, shape, core_density, quad_weight
     )
     came = lax.all_to_all(send, "dom", split_axis=0, concat_axis=0, tiled=True)
     parts = gradient_pass(band, occupancy, values, grads, cell_nodes)
-    parts = [parts[0]] + [shift(parts[d], d) for d in (1, 2, 3)]
+    others = [shift(parts[d], d) for d in (1, 2, 3)]
     stiff = stiff_part(nodes, stiffness, stiff_scale.reshape(1, SLOTS))
-    field, dens = gather(wave_rows, slot_rows, came)
-    mix = exchange(field, dens, parts)
+    field, dens, own = gather(wave_rows, slot_rows, came, parts[0])
+    mix = exchange(field, dens, [own] + others)
     mixes = [mix] + [shift(mix, d) for d in (1, 2, 3)]
     action, rest = second_pass(
-        band, mixes, values, grads, cell_nodes, core_density, quad_weight, shape, stiff
+        band, mixes, values, grads, head, cell_nodes, core_density, quad_weight, shape, stiff
     )
     return action, rest.T
 

time: 67.8 us -> 66.7 us (0.984); the launches traced: 67.5 us -> 65.6 us
  local copies, waits for them, and re-layouts: 2.51 us -> 0.85 us
    unnamed x24, local copies, waits for them, and re-layouts: 2.51 us -> 0.85 us
  transfers between devices with their start and end apart: 7 -> 7, of which waited for: 5 -> 5; matrix products, arithmetic and copies ran while one was open for 0% -> 0% of each run, Pallas kernels for 18% -> 19%
where the time goes in v6:
time: 66.7 us; the launch traced here: 65.6 us
  Pallas kernels  34.1 us (51%)
  starting transfers between devices  21.5 us (32%)
  waiting for transfers between devices  8.15 us (12%)
  between operations  0.98 us (1%)
  local copies, waits for them, and re-layouts  0.85 us (1%)
    pallas_call x1, Pallas kernels, second_pass(): pl.pallas_call(second_kernel, out_shape=(jax.ShapeDtypeStruct((NODES, CEL...  15.1 us
    all_to_all x1, starting transfers between devices, body(): came = lax.all_to_all(send, 'dom', split_axis=0, concat_axis=0, tiled=True)  12.1 us
    pallas_call x1, Pallas kernels, gradient_pass(): pl.pallas_call(gradient_kernel, out_shape=(part, part, part, part), in_sp...  10.5 us
    ppermute x6, starting transfers between devices, shift(): lax.ppermute(array, 'band', [(i, (i + distance) % RANKS) for i in range(R...  9.42 us
    ppermute x6, waiting for transfers between devices, shift(): lax.ppermute(array, 'band', [(i, (i + distance) % RANKS) for i in range(R...  8.15 us
    pallas_call x1, Pallas kernels, first_pass(): pl.pallas_call(first_kernel, out_shape=(jax.ShapeDtypeStruct((ROWS, 1, WI...  6.61 us
  transfers between devices with their start and end apart: 7, of which 5 were waited for; matrix products, arithmetic and copies ran while one was open for 0% of the time, Pallas kernels for 19%

profile of v6, /device:TPU:8, one launch (start us, length us, event | category | flops | bytes accessed | tf_op | source)
XLA Modules:
  0.0 65.6 jit_solution(7102317134901830783)
XLA Ops:
  0.6 6.6 %first_pass.1 = (f32[128,1,896]{2,1,0:T(1,128)}, bf16[3072,384]{1,0:T(8,128)(2,1)}, bf16[512,384]{1,0:T(8,128)(2,1)}, s32[24]{0:T(128)}, s32[48]{0:T(128)}) custom-call(s32[1]{0:T(128)} %bitcast.band_ref, s32[48]{0:T(128)} %slot_cell_ref.1, s32[24]{0:T(128)} %cell_slot_ref.1, bf16[343,24,128]{2,1,0:T(8,128)(2,1)} %orb_hbm.1, f32[1,128]{1,0:T(1,128)} %bitcast.20, ...), custom_call_target="tpu_custom_call" | custom-call | flops 1610612736 | bytes 8388608 | tf_op jit(solution)/shard_map/first_pass/pallas_call | solution.py:147
  7.3 12.1 %all-to-all-start = ((f32[128,1,896]{2,1,0:T(1,128)}), f32[128,1,896]{2,1,0:T(1,128)S(1)}, u32[]{:S(2)}, u32[]{:S(2)}) async-start(f32[128,1,896]{2,1,0:T(1,128)} %get-tuple-element.18), calls=%async_computation | async-start | bytes 917504 | tf_op jit(solution)/shard_map/all_to_all | solution.py:471
  19.4 0.0 copy-start
  19.4 0.0 copy-start.1
  19.4 0.0 copy-start.5
  19.4 0.0 copy-start.8
  19.4 0.0 copy-start.9
  19.5 10.5 %gradient_pass.1 = (f32[4,24,128]{2,1,0:T(8,128)}, f32[4,24,128]{2,1,0:T(8,128)}, f32[4,24,128]{2,1,0:T(8,128)}, f32[4,24,128]{2,1,0:T(8,128)}) custom-call(s32[1]{0:T(128)} %bitcast.band_ref, f32[1,128]{1,0:T(1,128)} %bitcast.21, bf16[343,512]{1,0:T(8,128)(2,1)} %bitcast.17, bf16[3,343,512]{2,1,0:T(8,128)(2,1)} %bitcast.13, ...), custom_call_target="tpu_custom_call" | custom-call | flops 6442450944 | bytes 8388608 | tf_op jit(solution)/shard_map/gradient_pass/pallas_call | solution.py:232
  29.9 1.6 %collective-permute-start = (f32[4,24,128]{2,1,0:T(8,128)}, f32[4,24,128]{2,1,0:T(8,128)S(1)}, u32[]{:S(2)}, u32[]{:S(2)}) collective-permute-start(f32[4,24,128]{2,1,0:T(8,128)} %get-tuple-element.24), channel_id=1, source_target_pairs={{0,64},{64,128},{128,192},{192,0},{1,65},{65,129},{129,193},{193,1... | collective-permute-start | bytes 147464 | tf_op jit(solution)/shard_map/ppermute | solution.py:456
  31.5 2.8 %collective-permute-start.1 = (f32[4,24,128]{2,1,0:T(8,128)}, f32[4,24,128]{2,1,0:T(8,128)S(1)}, u32[]{:S(2)}, u32[]{:S(2)}) collective-permute-start(f32[4,24,128]{2,1,0:T(8,128)} %get-tuple-element.25), channel_id=1, source_target_pairs={{0,128},{64,192},{128,0},{192,64},{1,129},{65,193},{129,1},{193,65... | collective-permute-start | bytes 147464 | tf_op jit(solution)/shard_map/ppermute | solution.py:456
  34.3 1.4 %collective-permute-start.2 = (f32[4,24,128]{2,1,0:T(8,128)}, f32[4,24,128]{2,1,0:T(8,128)S(1)}, u32[]{:S(2)}, u32[]{:S(2)}) collective-permute-start(f32[4,24,128]{2,1,0:T(8,128)} %get-tuple-element.26), channel_id=1, source_target_pairs={{0,192},{64,0},{128,64},{192,128},{1,193},{65,1},{129,65},{193,129... | collective-permute-start | bytes 147464 | tf_op jit(solution)/shard_map/ppermute | solution.py:456
  35.7 0.0 all-to-all-done.came_ref
  35.7 0.0 copy-start.2
  35.7 0.8 %copy-done.2 = f32[4,24,128]{2,1,0:T(8,128)S(1)} copy-done((f32[4,24,128]{2,1,0:T(8,128)S(1)}, f32[4,24,128]{2,1,0:T(8,128)}, u32[]{:S(2)}) %copy-start.2) | copy-done | bytes 49176
  36.5 0.7 %gather.1 = (f32[72,128]{1,0:T(8,128)S(1)}, f32[192,128]{1,0:T(8,128)S(1)}, f32[4,24,128]{2,1,0:T(8,128)S(1)}) custom-call(s32[24]{0:T(128)S(1)} %copy-done.3, s32[48]{0:T(128)S(1)} %copy-done.4, f32[128,1,896]{2,1,0:T(1,128)S(1)} %all-to-all-done.came_ref, f32[4,24,128]{2,1,0:T(8,128)S(1)} %copy-done.2), custom_call_target="tpu_custom_call" | custom-call | flops 1000000 | bytes 1048576 | tf_op jit(solution)/shard_map/gather/pallas_call | solution.py:281
  37.3 0.1 collective-permute-done.1.c_ref
  37.3 1.2 %collective-permute-done.2.d_ref = f32[4,24,128]{2,1,0:T(8,128)S(1)} collective-permute-done((f32[4,24,128]{2,1,0:T(8,128)}, f32[4,24,128]{2,1,0:T(8,128)S(1)}, u32[]{:S(2)}, u32[]{:S(2)}) %collective-permute-start.2) | collective-permute-done | bytes 49184 | tf_op jit(solution)/shard_map/ppermute | solution.py:456
  38.6 2.7 %collective-permute-start.5 = (f32[288,128]{1,0:T(8,128)S(1)}, f32[288,128]{1,0:T(8,128)S(1)}, u32[]{:S(2)}, u32[]{:S(2)}) collective-permute-start(f32[288,128]{1,0:T(8,128)S(1)} %exchange.1.m0_ref), channel_id=1, source_target_pairs={{0,192},{64,0},{128,64},{192,128},{1,193},{65,1},{129,65},{193,129... | collective-permute-start | bytes 442376 | tf_op jit(solution)/shard_map/ppermute | solution.py:456
  41.3 1.0 %collective-permute-start.3 = (f32[288,128]{1,0:T(8,128)S(1)}, f32[288,128]{1,0:T(8,128)S(1)}, u32[]{:S(2)}, u32[]{:S(2)}) collective-permute-start(f32[288,128]{1,0:T(8,128)S(1)} %exchange.1.m0_ref), channel_id=1, source_target_pairs={{0,64},{64,128},{128,192},{192,0},{1,65},{65,129},{129,193},{193,1... | collective-permute-start | bytes 442376 | tf_op jit(solution)/shard_map/ppermute | solution.py:456
  42.3 1.1 %stiff_part.1.stiff_ref = f32[48,729]{1,0:T(8,128)S(1)} custom-call(f32[48,729]{1,0:T(8,128)S(1)} %bitcast.9, f32[729,729]{1,0:T(8,128)S(1)} %copy-done, f32[1,48]{1,0:T(1,128)S(1)} %bitcast.10), custom_call_target="tpu_custom_call" | custom-call | flops 306110016 | bytes 3145728 | tf_op jit(solution)/shard_map/stiff_part/pallas_call | solution.py:444
  43.4 3.2 %collective-permute-done.5.m3_ref = f32[288,128]{1,0:T(8,128)S(1)} collective-permute-done((f32[288,128]{1,0:T(8,128)S(1)}, f32[288,128]{1,0:T(8,128)S(1)}, u32[]{:S(2)}, u32[]{:S(2)}) %collective-permute-start.5) | collective-permute-done | bytes 147488 | tf_op jit(solution)/shard_map/ppermute | solution.py:456
  46.6 2.2 %collective-permute-done.4.m2_ref = f32[288,128]{1,0:T(8,128)S(1)} collective-permute-done((f32[288,128]{1,0:T(8,128)S(1)}, f32[288,128]{1,0:T(8,128)S(1)}, u32[]{:S(2)}, u32[]{:S(2)}) %collective-permute-start.4) | collective-permute-done | bytes 147488 | tf_op jit(solution)/shard_map/ppermute | solution.py:456
  48.7 1.5 %collective-permute-done.3.m1_ref = f32[288,128]{1,0:T(8,128)S(1)} collective-permute-done((f32[288,128]{1,0:T(8,128)S(1)}, f32[288,128]{1,0:T(8,128)S(1)}, u32[]{:S(2)}, u32[]{:S(2)}) %collective-permute-start.3) | collective-permute-done | bytes 147488 | tf_op jit(solution)/shard_map/ppermute | solution.py:456
  50.3 15.1 %second_pass.1 = (bf16[343,24,128]{2,1,0:T(8,128)(2,1)}, f32[48,729]{1,0:T(8,128)}) custom-call(s32[1]{0:T(128)} %bitcast.band_ref, f32[288,128]{1,0:T(8,128)S(1)} %exchange.1.m0_ref, f32[288,128]{1,0:T(8,128)S(1)} %collective-permute-done.3.m1_ref, f32[288,128]{1,0:T(8,128)S(1)} %collective-permute-done.4.m2_ref, ...), custom_call_target="tpu_custom_call" | custom-call | flops 12884901888 | bytes 8388608 | tf_op jit(solution)/shard_map/second_pass/pallas_call | solution.py:408
  (20 shorter events, 0.1 us)
Async XLA Ops:
  7.3 28.5 %all-to-all-start = ((f32[128,1,896]{2,1,0:T(1,128)}), f32[128,1,896]{2,1,0:T(1,128)S(1)}, u32[]{:S(2)}, u32[]{:S(2)}) async-start(f32[128,1,896]{2,1,0:T(1,128)} %get-tuple-element.18), calls=%async_computation | async-start | bytes 917504 | tf_op jit(solution)/shard_map/all_to_all | solution.py:471
  19.4 16.3 %copy-start.3 = (s32[24]{0:T(128)S(1)}, s32[24]{0:T(128)}, u32[]{:S(2)}) copy-start(s32[24]{0:T(128)} %get-tuple-element.16.wave_row_ref) | copy-start | bytes 292
  19.4 16.3 %copy-start.4 = (s32[48]{0:T(128)S(1)}, s32[48]{0:T(128)}, u32[]{:S(2)}) copy-start(s32[48]{0:T(128)} %get-tuple-element.17.slot_row_ref) | copy-start | bytes 580
  19.4 22.9 %copy-start = (f32[729,729]{1,0:T(8,128)S(1)}, f32[729,729]{1,0:T(8,128)}, u32[]{:S(2)}) copy-start(f32[729,729]{1,0:T(8,128)} %stiff_ref.1) | copy-start | bytes 6377296
  19.4 22.9 %copy-start.1 = (f32[729,48]{0,1:T(8,128)S(1)}, f32[729,48]{0,1:T(8,128)}, u32[]{:S(2)}) copy-start(f32[729,48]{0,1:T(8,128)} %param.18) | copy-start | bytes 419908
  19.4 22.9 %copy-start.5 = (f32[48]{0:T(128)S(1)}, f32[48]{0:T(128)}, u32[]{:S(2)}) copy-start(f32[48]{0:T(128)} %param.20) | copy-start | bytes 580
  19.4 30.8 %copy-start.8 = (bf16[512,343]{0,1:T(8,128)(2,1)S(1)}, bf16[512,343]{0,1:T(8,128)(2,1)}, u32[]{:S(2)}) copy-start(bf16[512,343]{0,1:T(8,128)(2,1)} %param.14) | copy-start | bytes 1053700
  19.4 30.8 %copy-start.9 = (f32[48,512]{1,0:T(8,128)S(1)}, f32[48,512]{1,0:T(8,128)}, u32[]{:S(2)}) copy-start(f32[48,512]{1,0:T(8,128)} %core_ref.1) | copy-start | bytes 294916
  29.9 7.3 %collective-permute-start = (f32[4,24,128]{2,1,0:T(8,128)}, f32[4,24,128]{2,1,0:T(8,128)S(1)}, u32[]{:S(2)}, u32[]{:S(2)}) collective-permute-start(f32[4,24,128]{2,1,0:T(8,128)} %get-tuple-element.24), channel_id=1, source_target_pairs={{0,64},{64,128},{128,192},{192,0},{1,65},{65,129},{129,193},{193,1... | collective-permute-start | bytes 147464 | tf_op jit(solution)/shard_map/ppermute | solution.py:456
  31.5 5.8 %collective-permute-start.1 = (f32[4,24,128]{2,1,0:T(8,128)}, f32[4,24,128]{2,1,0:T(8,128)S(1)}, u32[]{:S(2)}, u32[]{:S(2)}) collective-permute-start(f32[4,24,128]{2,1,0:T(8,128)} %get-tuple-element.25), channel_id=1, source_target_pairs={{0,128},{64,192},{128,0},{192,64},{1,129},{65,193},{129,1},{193,65... | collective-permute-start | bytes 147464 | tf_op jit(solution)/shard_map/ppermute | solution.py:456
  34.3 4.3 %collective-permute-start.2 = (f32[4,24,128]{2,1,0:T(8,128)}, f32[4,24,128]{2,1,0:T(8,128)S(1)}, u32[]{:S(2)}, u32[]{:S(2)}) collective-permute-start(f32[4,24,128]{2,1,0:T(8,128)} %get-tuple-element.26), channel_id=1, source_target_pairs={{0,192},{64,0},{128,64},{192,128},{1,193},{65,1},{129,65},{193,129... | collective-permute-start | bytes 147464 | tf_op jit(solution)/shard_map/ppermute | solution.py:456
  35.7 0.8 %copy-start.2 = (f32[4,24,128]{2,1,0:T(8,128)S(1)}, f32[4,24,128]{2,1,0:T(8,128)}, u32[]{:S(2)}) copy-start(f32[4,24,128]{2,1,0:T(8,128)} %get-tuple-element.20.part_ref) | copy-start | bytes 147460
  36.5 13.7 %copy-start.6 = (f32[512,729]{0,1:T(8,128)S(1)}, f32[512,729]{0,1:T(8,128)}, u32[]{:S(2)}) copy-start(f32[512,729]{0,1:T(8,128)} %param.21) | copy-start | bytes 4478980
  36.5 13.7 %copy-start.7 = (bf16[3,512,343]{1,2,0:T(8,128)(2,1)S(1)}, bf16[3,512,343]{1,2,0:T(8,128)(2,1)}, u32[]{:S(2)}) copy-start(bf16[3,512,343]{1,2,0:T(8,128)(2,1)} %param.15) | copy-start | bytes 3161092
  36.5 13.8 %copy-start.10 = (f32[48,512]{1,0:T(8,128)S(1)}, f32[48,512]{1,0:T(8,128)}, u32[]{:S(2)}) copy-start(f32[48,512]{1,0:T(8,128)} %weight_ref.1) | copy-start | bytes 294916
  36.5 13.8 %copy-start.11 = (bf16[512,384]{1,0:T(8,128)(2,1)S(1)}, bf16[512,384]{1,0:T(8,128)(2,1)}, u32[]{:S(2)}) copy-start(bf16[512,384]{1,0:T(8,128)(2,1)} %get-tuple-element.27.head_ref) | copy-start | bytes 1179652
  38.6 7.9 %collective-permute-start.5 = (f32[288,128]{1,0:T(8,128)S(1)}, f32[288,128]{1,0:T(8,128)S(1)}, u32[]{:S(2)}, u32[]{:S(2)}) collective-permute-start(f32[288,128]{1,0:T(8,128)S(1)} %exchange.1.m0_ref), channel_id=1, source_target_pairs={{0,192},{64,0},{128,64},{192,128},{1,193},{65,1},{129,65},{193,129... | collective-permute-start | bytes 442376 | tf_op jit(solution)/shard_map/ppermute | solution.py:456
  41.3 7.4 %collective-permute-start.4 = (f32[288,128]{1,0:T(8,128)S(1)}, f32[288,128]{1,0:T(8,128)S(1)}, u32[]{:S(2)}, u32[]{:S(2)}) collective-permute-start(f32[288,128]{1,0:T(8,128)S(1)} %exchange.1.m0_ref), channel_id=1, source_target_pairs={{0,128},{64,192},{128,0},{192,64},{1,129},{65,193},{129,1},{193,65... | collective-permute-start | bytes 442376 | tf_op jit(solution)/shard_map/ppermute | solution.py:456
  41.3 8.9 %collective-permute-start.3 = (f32[288,128]{1,0:T(8,128)S(1)}, f32[288,128]{1,0:T(8,128)S(1)}, u32[]{:S(2)}, u32[]{:S(2)}) collective-permute-start(f32[288,128]{1,0:T(8,128)S(1)} %exchange.1.m0_ref), channel_id=1, source_target_pairs={{0,64},{64,128},{128,192},{192,0},{1,65},{65,129},{129,193},{193,1... | collective-permute-start | bytes 442376 | tf_op jit(solution)/shard_map/ppermute | solution.py:456

commit v7 on v6

--- a/solution.py
+++ b/solution.py
@@ -419,7 +419,7 @@
             pltpu.VMEM((NODES, 4 * POINTS), BF16),
             pltpu.VMEM((2, 4, GROUP * BANDS, POINTS), F32),
             pltpu.VMEM((2, GROUP * BANDS, 4 * POINTS), BF16),
-            pltpu.VMEM((NODES * CELLS, BANDS), F32),
+            pltpu.VMEM(((NODES + 1) * CELLS, BANDS), F32),
             pltpu.VMEM((NODES, CELLS, BANDS), BF16),
             pltpu.VMEM((SLOTS, POINTS), F32),
             pltpu.SemaphoreType.DMA((CELLS // GROUP,)),

time: 66.7 us -> 66.7 us (level)
  no operation moved by 1% of the time
where the time goes in v7:
time: 66.7 us; the launch traced here: 65.6 us
  Pallas kernels  34.1 us (51%)
  starting transfers between devices  21.5 us (32%)
  waiting for transfers between devices  8.15 us (12%)
  between operations  0.98 us (1%)
  local copies, waits for them, and re-layouts  0.85 us (1%)
    pallas_call x1, Pallas kernels, second_pass(): pl.pallas_call(second_kernel, out_shape=(jax.ShapeDtypeStruct((NODES, CEL...  15.1 us
    all_to_all x1, starting transfers between devices, body(): came = lax.all_to_all(send, 'dom', split_axis=0, concat_axis=0, tiled=True)  12.1 us
    pallas_call x1, Pallas kernels, gradient_pass(): pl.pallas_call(gradient_kernel, out_shape=(part, part, part, part), in_sp...  10.5 us
    ppermute x6, starting transfers between devices, shift(): lax.ppermute(array, 'band', [(i, (i + distance) % RANKS) for i in range(R...  9.42 us
    ppermute x6, waiting for transfers between devices, shift(): lax.ppermute(array, 'band', [(i, (i + distance) % RANKS) for i in range(R...  8.15 us
    pallas_call x1, Pallas kernels, first_pass(): pl.pallas_call(first_kernel, out_shape=(jax.ShapeDtypeStruct((ROWS, 1, WI...  6.61 us
  transfers between devices with their start and end apart: 7, of which 5 were waited for; matrix products, arithmetic and copies ran while one was open for 0% of the time, Pallas kernels for 19%

profile of v7, /device:TPU:8, one launch (start us, length us, event | category | flops | bytes accessed | tf_op | source)
XLA Modules:
  0.0 65.6 jit_solution(8707974060398924595)
XLA Ops:
  0.6 6.6 %first_pass.1 = (f32[128,1,896]{2,1,0:T(1,128)}, bf16[3072,384]{1,0:T(8,128)(2,1)}, bf16[512,384]{1,0:T(8,128)(2,1)}, s32[24]{0:T(128)}, s32[48]{0:T(128)}) custom-call(s32[1]{0:T(128)} %bitcast.band_ref, s32[48]{0:T(128)} %slot_cell_ref.1, s32[24]{0:T(128)} %cell_slot_ref.1, bf16[343,24,128]{2,1,0:T(8,128)(2,1)} %orb_hbm.1, f32[1,128]{1,0:T(1,128)} %bitcast.20, ...), custom_call_target="tpu_custom_call" | custom-call | flops 1610612736 | bytes 8388608 | tf_op jit(solution)/shard_map/first_pass/pallas_call | solution.py:147
  7.3 12.1 %all-to-all-start = ((f32[128,1,896]{2,1,0:T(1,128)}), f32[128,1,896]{2,1,0:T(1,128)S(1)}, u32[]{:S(2)}, u32[]{:S(2)}) async-start(f32[128,1,896]{2,1,0:T(1,128)} %get-tuple-element.18), calls=%async_computation | async-start | bytes 917504 | tf_op jit(solution)/shard_map/all_to_all | solution.py:471
  19.4 0.0 copy-start
  19.4 0.0 copy-start.1
  19.4 0.0 copy-start.5
  19.4 0.0 copy-start.8
  19.4 0.0 copy-start.9
  19.5 10.5 %gradient_pass.1 = (f32[4,24,128]{2,1,0:T(8,128)}, f32[4,24,128]{2,1,0:T(8,128)}, f32[4,24,128]{2,1,0:T(8,128)}, f32[4,24,128]{2,1,0:T(8,128)}) custom-call(s32[1]{0:T(128)} %bitcast.band_ref, f32[1,128]{1,0:T(1,128)} %bitcast.21, bf16[343,512]{1,0:T(8,128)(2,1)} %bitcast.17, bf16[3,343,512]{2,1,0:T(8,128)(2,1)} %bitcast.13, ...), custom_call_target="tpu_custom_call" | custom-call | flops 6442450944 | bytes 8388608 | tf_op jit(solution)/shard_map/gradient_pass/pallas_call | solution.py:232
  29.9 1.6 %collective-permute-start = (f32[4,24,128]{2,1,0:T(8,128)}, f32[4,24,128]{2,1,0:T(8,128)S(1)}, u32[]{:S(2)}, u32[]{:S(2)}) collective-permute-start(f32[4,24,128]{2,1,0:T(8,128)} %get-tuple-element.24), channel_id=1, source_target_pairs={{0,64},{64,128},{128,192},{192,0},{1,65},{65,129},{129,193},{193,1... | collective-permute-start | bytes 147464 | tf_op jit(solution)/shard_map/ppermute | solution.py:456
  31.5 2.8 %collective-permute-start.1 = (f32[4,24,128]{2,1,0:T(8,128)}, f32[4,24,128]{2,1,0:T(8,128)S(1)}, u32[]{:S(2)}, u32[]{:S(2)}) collective-permute-start(f32[4,24,128]{2,1,0:T(8,128)} %get-tuple-element.25), channel_id=1, source_target_pairs={{0,128},{64,192},{128,0},{192,64},{1,129},{65,193},{129,1},{193,65... | collective-permute-start | bytes 147464 | tf_op jit(solution)/shard_map/ppermute | solution.py:456
  34.3 1.4 %collective-permute-start.2 = (f32[4,24,128]{2,1,0:T(8,128)}, f32[4,24,128]{2,1,0:T(8,128)S(1)}, u32[]{:S(2)}, u32[]{:S(2)}) collective-permute-start(f32[4,24,128]{2,1,0:T(8,128)} %get-tuple-element.26), channel_id=1, source_target_pairs={{0,192},{64,0},{128,64},{192,128},{1,193},{65,1},{129,65},{193,129... | collective-permute-start | bytes 147464 | tf_op jit(solution)/shard_map/ppermute | solution.py:456
  35.7 0.0 all-to-all-done.came_ref
  35.7 0.0 copy-start.2
  35.7 0.8 %copy-done.2 = f32[4,24,128]{2,1,0:T(8,128)S(1)} copy-done((f32[4,24,128]{2,1,0:T(8,128)S(1)}, f32[4,24,128]{2,1,0:T(8,128)}, u32[]{:S(2)}) %copy-start.2) | copy-done | bytes 49176
  36.5 0.7 %gather.1 = (f32[72,128]{1,0:T(8,128)S(1)}, f32[192,128]{1,0:T(8,128)S(1)}, f32[4,24,128]{2,1,0:T(8,128)S(1)}) custom-call(s32[24]{0:T(128)S(1)} %copy-done.3, s32[48]{0:T(128)S(1)} %copy-done.4, f32[128,1,896]{2,1,0:T(1,128)S(1)} %all-to-all-done.came_ref, f32[4,24,128]{2,1,0:T(8,128)S(1)} %copy-done.2), custom_call_target="tpu_custom_call" | custom-call | flops 1000000 | bytes 1048576 | tf_op jit(solution)/shard_map/gather/pallas_call | solution.py:281
  37.3 0.1 collective-permute-done.1.c_ref
  37.3 1.2 %collective-permute-done.2.d_ref = f32[4,24,128]{2,1,0:T(8,128)S(1)} collective-permute-done((f32[4,24,128]{2,1,0:T(8,128)}, f32[4,24,128]{2,1,0:T(8,128)S(1)}, u32[]{:S(2)}, u32[]{:S(2)}) %collective-permute-start.2) | collective-permute-done | bytes 49184 | tf_op jit(solution)/shard_map/ppermute | solution.py:456
  38.6 2.7 %collective-permute-start.5 = (f32[288,128]{1,0:T(8,128)S(1)}, f32[288,128]{1,0:T(8,128)S(1)}, u32[]{:S(2)}, u32[]{:S(2)}) collective-permute-start(f32[288,128]{1,0:T(8,128)S(1)} %exchange.1.m0_ref), channel_id=1, source_target_pairs={{0,192},{64,0},{128,64},{192,128},{1,193},{65,1},{129,65},{193,129... | collective-permute-start | bytes 442376 | tf_op jit(solution)/shard_map/ppermute | solution.py:456
  41.3 1.0 %collective-permute-start.3 = (f32[288,128]{1,0:T(8,128)S(1)}, f32[288,128]{1,0:T(8,128)S(1)}, u32[]{:S(2)}, u32[]{:S(2)}) collective-permute-start(f32[288,128]{1,0:T(8,128)S(1)} %exchange.1.m0_ref), channel_id=1, source_target_pairs={{0,64},{64,128},{128,192},{192,0},{1,65},{65,129},{129,193},{193,1... | collective-permute-start | bytes 442376 | tf_op jit(solution)/shard_map/ppermute | solution.py:456
  42.3 1.1 %stiff_part.1.stiff_ref = f32[48,729]{1,0:T(8,128)S(1)} custom-call(f32[48,729]{1,0:T(8,128)S(1)} %bitcast.9, f32[729,729]{1,0:T(8,128)S(1)} %copy-done, f32[1,48]{1,0:T(1,128)S(1)} %bitcast.10), custom_call_target="tpu_custom_call" | custom-call | flops 306110016 | bytes 3145728 | tf_op jit(solution)/shard_map/stiff_part/pallas_call | solution.py:444
  43.4 3.2 %collective-permute-done.5.m3_ref = f32[288,128]{1,0:T(8,128)S(1)} collective-permute-done((f32[288,128]{1,0:T(8,128)S(1)}, f32[288,128]{1,0:T(8,128)S(1)}, u32[]{:S(2)}, u32[]{:S(2)}) %collective-permute-start.5) | collective-permute-done | bytes 147488 | tf_op jit(solution)/shard_map/ppermute | solution.py:456
  46.6 2.2 %collective-permute-done.4.m2_ref = f32[288,128]{1,0:T(8,128)S(1)} collective-permute-done((f32[288,128]{1,0:T(8,128)S(1)}, f32[288,128]{1,0:T(8,128)S(1)}, u32[]{:S(2)}, u32[]{:S(2)}) %collective-permute-start.4) | collective-permute-done | bytes 147488 | tf_op jit(solution)/shard_map/ppermute | solution.py:456
  48.7 1.5 %collective-permute-done.3.m1_ref = f32[288,128]{1,0:T(8,128)S(1)} collective-permute-done((f32[288,128]{1,0:T(8,128)S(1)}, f32[288,128]{1,0:T(8,128)S(1)}, u32[]{:S(2)}, u32[]{:S(2)}) %collective-permute-start.3) | collective-permute-done | bytes 147488 | tf_op jit(solution)/shard_map/ppermute | solution.py:456
  50.3 15.1 %second_pass.1 = (bf16[343,24,128]{2,1,0:T(8,128)(2,1)}, f32[48,729]{1,0:T(8,128)}) custom-call(s32[1]{0:T(128)} %bitcast.band_ref, f32[288,128]{1,0:T(8,128)S(1)} %exchange.1.m0_ref, f32[288,128]{1,0:T(8,128)S(1)} %collective-permute-done.3.m1_ref, f32[288,128]{1,0:T(8,128)S(1)} %collective-permute-done.4.m2_ref, ...), custom_call_target="tpu_custom_call" | custom-call | flops 12884901888 | bytes 8388608 | tf_op jit(solution)/shard_map/second_pass/pallas_call | solution.py:408
  (20 shorter events, 0.1 us)
Async XLA Ops:
  7.3 28.5 %all-to-all-start = ((f32[128,1,896]{2,1,0:T(1,128)}), f32[128,1,896]{2,1,0:T(1,128)S(1)}, u32[]{:S(2)}, u32[]{:S(2)}) async-start(f32[128,1,896]{2,1,0:T(1,128)} %get-tuple-element.18), calls=%async_computation | async-start | bytes 917504 | tf_op jit(solution)/shard_map/all_to_all | solution.py:471
  19.4 16.3 %copy-start.3 = (s32[24]{0:T(128)S(1)}, s32[24]{0:T(128)}, u32[]{:S(2)}) copy-start(s32[24]{0:T(128)} %get-tuple-element.16.wave_row_ref) | copy-start | bytes 292
  19.4 16.3 %copy-start.4 = (s32[48]{0:T(128)S(1)}, s32[48]{0:T(128)}, u32[]{:S(2)}) copy-start(s32[48]{0:T(128)} %get-tuple-element.17.slot_row_ref) | copy-start | bytes 580
  19.4 22.9 %copy-start = (f32[729,729]{1,0:T(8,128)S(1)}, f32[729,729]{1,0:T(8,128)}, u32[]{:S(2)}) copy-start(f32[729,729]{1,0:T(8,128)} %stiff_ref.1) | copy-start | bytes 6377296
  19.4 22.9 %copy-start.1 = (f32[729,48]{0,1:T(8,128)S(1)}, f32[729,48]{0,1:T(8,128)}, u32[]{:S(2)}) copy-start(f32[729,48]{0,1:T(8,128)} %param.18) | copy-start | bytes 419908
  19.4 22.9 %copy-start.5 = (f32[48]{0:T(128)S(1)}, f32[48]{0:T(128)}, u32[]{:S(2)}) copy-start(f32[48]{0:T(128)} %param.20) | copy-start | bytes 580
  19.4 30.8 %copy-start.8 = (bf16[512,343]{0,1:T(8,128)(2,1)S(1)}, bf16[512,343]{0,1:T(8,128)(2,1)}, u32[]{:S(2)}) copy-start(bf16[512,343]{0,1:T(8,128)(2,1)} %param.14) | copy-start | bytes 1053700
  19.4 30.8 %copy-start.9 = (f32[48,512]{1,0:T(8,128)S(1)}, f32[48,512]{1,0:T(8,128)}, u32[]{:S(2)}) copy-start(f32[48,512]{1,0:T(8,128)} %core_ref.1) | copy-start | bytes 294916
  29.9 7.3 %collective-permute-start = (f32[4,24,128]{2,1,0:T(8,128)}, f32[4,24,128]{2,1,0:T(8,128)S(1)}, u32[]{:S(2)}, u32[]{:S(2)}) collective-permute-start(f32[4,24,128]{2,1,0:T(8,128)} %get-tuple-element.24), channel_id=1, source_target_pairs={{0,64},{64,128},{128,192},{192,0},{1,65},{65,129},{129,193},{193,1... | collective-permute-start | bytes 147464 | tf_op jit(solution)/shard_map/ppermute | solution.py:456
  31.5 5.8 %collective-permute-start.1 = (f32[4,24,128]{2,1,0:T(8,128)}, f32[4,24,128]{2,1,0:T(8,128)S(1)}, u32[]{:S(2)}, u32[]{:S(2)}) collective-permute-start(f32[4,24,128]{2,1,0:T(8,128)} %get-tuple-element.25), channel_id=1, source_target_pairs={{0,128},{64,192},{128,0},{192,64},{1,129},{65,193},{129,1},{193,65... | collective-permute-start | bytes 147464 | tf_op jit(solution)/shard_map/ppermute | solution.py:456
  34.3 4.3 %collective-permute-start.2 = (f32[4,24,128]{2,1,0:T(8,128)}, f32[4,24,128]{2,1,0:T(8,128)S(1)}, u32[]{:S(2)}, u32[]{:S(2)}) collective-permute-start(f32[4,24,128]{2,1,0:T(8,128)} %get-tuple-element.26), channel_id=1, source_target_pairs={{0,192},{64,0},{128,64},{192,128},{1,193},{65,1},{129,65},{193,129... | collective-permute-start | bytes 147464 | tf_op jit(solution)/shard_map/ppermute | solution.py:456
  35.7 0.8 %copy-start.2 = (f32[4,24,128]{2,1,0:T(8,128)S(1)}, f32[4,24,128]{2,1,0:T(8,128)}, u32[]{:S(2)}) copy-start(f32[4,24,128]{2,1,0:T(8,128)} %get-tuple-element.20.part_ref) | copy-start | bytes 147460
  36.5 13.7 %copy-start.6 = (f32[512,729]{0,1:T(8,128)S(1)}, f32[512,729]{0,1:T(8,128)}, u32[]{:S(2)}) copy-start(f32[512,729]{0,1:T(8,128)} %param.21) | copy-start | bytes 4478980
  36.5 13.7 %copy-start.7 = (bf16[3,512,343]{1,2,0:T(8,128)(2,1)S(1)}, bf16[3,512,343]{1,2,0:T(8,128)(2,1)}, u32[]{:S(2)}) copy-start(bf16[3,512,343]{1,2,0:T(8,128)(2,1)} %param.15) | copy-start | bytes 3161092
  36.5 13.8 %copy-start.10 = (f32[48,512]{1,0:T(8,128)S(1)}, f32[48,512]{1,0:T(8,128)}, u32[]{:S(2)}) copy-start(f32[48,512]{1,0:T(8,128)} %weight_ref.1) | copy-start | bytes 294916
  36.5 13.8 %copy-start.11 = (bf16[512,384]{1,0:T(8,128)(2,1)S(1)}, bf16[512,384]{1,0:T(8,128)(2,1)}, u32[]{:S(2)}) copy-start(bf16[512,384]{1,0:T(8,128)(2,1)} %get-tuple-element.27.head_ref) | copy-start | bytes 1179652
  38.6 7.9 %collective-permute-start.5 = (f32[288,128]{1,0:T(8,128)S(1)}, f32[288,128]{1,0:T(8,128)S(1)}, u32[]{:S(2)}, u32[]{:S(2)}) collective-permute-start(f32[288,128]{1,0:T(8,128)S(1)} %exchange.1.m0_ref), channel_id=1, source_target_pairs={{0,192},{64,0},{128,64},{192,128},{1,193},{65,1},{129,65},{193,129... | collective-permute-start | bytes 442376 | tf_op jit(solution)/shard_map/ppermute | solution.py:456
  41.3 7.4 %collective-permute-start.4 = (f32[288,128]{1,0:T(8,128)S(1)}, f32[288,128]{1,0:T(8,128)S(1)}, u32[]{:S(2)}, u32[]{:S(2)}) collective-permute-start(f32[288,128]{1,0:T(8,128)S(1)} %exchange.1.m0_ref), channel_id=1, source_target_pairs={{0,128},{64,192},{128,0},{192,64},{1,129},{65,193},{129,1},{193,65... | collective-permute-start | bytes 442376 | tf_op jit(solution)/shard_map/ppermute | solution.py:456
  41.3 8.9 %collective-permute-start.3 = (f32[288,128]{1,0:T(8,128)S(1)}, f32[288,128]{1,0:T(8,128)S(1)}, u32[]{:S(2)}, u32[]{:S(2)}) collective-permute-start(f32[288,128]{1,0:T(8,128)S(1)} %exchange.1.m0_ref), channel_id=1, source_target_pairs={{0,64},{64,128},{128,192},{192,0},{1,65},{65,129},{129,193},{193,1... | collective-permute-start | bytes 442376 | tf_op jit(solution)/shard_map/ppermute | solution.py:456
